TPU v7x, 32 devices: a whole 2x2x4 slice. The times are simulated.
32 devices in a mesh: gx: 16 (over z, y, x), gy: 2 (over core).
Axes of the slice: x: 2, y: 2, z: 4, core: 2. Of those that a mesh axis runs over, the one named last changes fastest.
Arguments:
- tokens_in: bfloat16 [4096, 2048], P('gx'), may hold values from -6 to 6
- doc_ids: int32 [16, 256], P('gx'), may hold values from 0 to 3, never falling along the last dimension, each value on 1 to 128 neighbouring positions
- routes: int32 [4096, 8], P('gx'), may hold values from 0 to 15, all different within a row; in each aligned block of 256 rows (0 to 255, 256 to 511, ...) at most 160 rows name the same one
- q_weight: bfloat16 [2048, 4096], P('gx', 'gy'), may hold values from -0.125 to 0.125
- key_matrix: bfloat16 [2048, 512], P('gx', 'gy'), may hold values from -0.125 to 0.125
- value_matrix: bfloat16 [2048, 512], P('gx', 'gy'), may hold values from -0.125 to 0.125
- out_weight: bfloat16 [2048, 4096], P('gx', 'gy'), may hold values from -0.75 to 0.75
- router_weight: bfloat16 [2048, 16], P('gx'), may hold values from -0.0625 to 0.0625
- attn_gain: float32 [2048], replicated, may hold values from 0.1 to 1.9
- ffn_gain: float32 [2048], replicated, may hold values from 0.1 to 1.9
- query_norm_gain: float32 [128], replicated, may hold values from 0.5 to 2
- k_gain: float32 [128], replicated, may hold values from 0.5 to 2
- gate_weight: bfloat16 [16, 2048, 768], P('gx', None, 'gy'), may hold values from -0.125 to 0.125
- up_weight: bfloat16 [16, 2048, 768], P('gx', None, 'gy'), may hold values from -0.125 to 0.125
- down_weight: bfloat16 [16, 768, 2048], P('gx', 'gy'), may hold values from -0.625 to 0.625
- cotangent: bfloat16 [4096, 2048], P('gx'), may hold values from -6 to 6
Outputs:
- output: bfloat16 [4096, 2048], P('gx')
- grad_input: bfloat16 [4096, 2048], P('gx')
- grad_q: float32 [2048, 4096], P('gx', 'gy')
- grad_k: float32 [2048, 512], P('gx', 'gy')
- grad_v: float32 [2048, 512], P('gx', 'gy')
- grad_out: float32 [2048, 4096], P('gx', 'gy')
- grad_router: float32 [2048, 16], P('gx')
- grad_attn_gain: float32 [2048], replicated
- grad_ffn_gain: float32 [2048], replicated
- grad_q_gain: float32 [128], replicated
- grad_k_gain: float32 [128], replicated
- grad_gate: float32 [16, 2048, 768], P('gx', None, 'gy')
- grad_up: float32 [16, 2048, 768], P('gx', None, 'gy')
- grad_down: float32 [16, 768, 2048], P('gx', 'gy')
Inputs may be any that keep to these rules, and one draw needn't show every extreme that they name: `routes`: each row names 8 different experts. Among the 256 rows of one index of gx no expert is named by more than 160 rows, and in every draw some expert is named by exactly 160 rows of some index. `doc_ids`: along a sequence the document numbers never fall; each document takes 1 to half of 256 positions, and one takes exactly half.
All inputs are finite; a program needn't handle non-finite values.
Results may differ from a plain program's by a relative error of at most 0.018.
Values may be sent and summed in bfloat16 or wider, within the bound.
A program may use at most 256 MiB of HBM per device.

v0:
```python
import math

import jax
import jax.numpy as jnp
from jax import lax
from jax.sharding import PartitionSpec as P

QUERY_HEADS = 32
KEY_VALUE_HEADS = 4
HEAD_DIM = 128
TOP = 8


EPSILON = 1e-06
THETA = 1000000.0


def root_mean_scale(values):
    return lax.rsqrt(jnp.mean(values * values, axis=-1, keepdims=True) + EPSILON)


def rotary_tables(sequence_length, head_width):
    half_width = head_width // 2
    frequencies = THETA ** (-(2.0 * jnp.arange(half_width, dtype=jnp.float32)) / head_width)
    angles = jnp.arange(sequence_length, dtype=jnp.float32)[:, None] * frequencies[None, :]
    return (jnp.cos(angles)[:, None, :], jnp.sin(angles)[:, None, :])


def rotate(values, cosine, sine_table):
    half_width = values.shape[-1] // 2
    lead_half = values[..., :half_width]
    tail_half = values[..., half_width:]
    return jnp.concatenate(
        [lead_half * cosine - tail_half * sine_table, tail_half * cosine + lead_half * sine_table],
        axis=-1,
    )


def norm_back(grad_normed, normed_unit, scale_rows):
    return scale_rows * (
        grad_normed - normed_unit * jnp.mean(grad_normed * normed_unit, axis=-1, keepdims=True)
    )


def contract(first_op, second_op, first_dim, second_dim):
    return lax.dot_general(
        first_op,
        second_op,
        (((first_dim,), (second_dim,)), ((), ())),
        preferred_element_type=jnp.float32,
    )


def on_device(
    tokens_in,
    doc_ids,
    routes,
    q_weight,
    key_matrix,
    value_matrix,
    out_weight,
    router_weight,
    attn_gain,
    ffn_gain,
    query_norm_gain,
    k_gain,
    gate_weight,
    up_weight,
    down_weight,
    cotangent,
):
    sequence_length = tokens_in.shape[0]
    model_width = tokens_in.shape[1]
    devices_gx = lax.axis_size("gx")
    devices_gy = lax.axis_size("gy")
    part_width = model_width // devices_gy
    experts_all = router_weight.shape[1]
    capacity = 5 * sequence_length * TOP // (4 * experts_all)
    pairs_count = sequence_length * TOP
    query_group_count = QUERY_HEADS // KEY_VALUE_HEADS
    inv_root = 1.0 / math.sqrt(HEAD_DIM)
    q_full, k_full, v_full, o_full, router_full = (
        lax.all_gather(q_weight, "gx", axis=0, tiled=True),
        lax.all_gather(key_matrix, "gx", axis=0, tiled=True),
        lax.all_gather(value_matrix, "gx", axis=0, tiled=True),
        lax.all_gather(out_weight, "gx", axis=0, tiled=True),
        lax.all_gather(router_weight, "gx", axis=0, tiled=True),
    )
    heads_local = q_full.shape[1] // HEAD_DIM
    kv_local = k_full.shape[1] // HEAD_DIM
    inputs_f = tokens_in.astype(jnp.float32)
    scale_one = root_mean_scale(inputs_f)
    unit_one = inputs_f * scale_one
    normalized_input = (unit_one * attn_gain).astype(jnp.bfloat16)
    query_unrotated = jnp.dot(normalized_input, q_full, preferred_element_type=jnp.float32).reshape(
        sequence_length, heads_local, HEAD_DIM
    )
    key_unrotated = jnp.dot(normalized_input, k_full, preferred_element_type=jnp.float32).reshape(
        sequence_length, kv_local, HEAD_DIM
    )
    value_rows = (
        jnp.dot(normalized_input, v_full, preferred_element_type=jnp.float32)
        .astype(jnp.bfloat16)
        .reshape(sequence_length, kv_local, HEAD_DIM)
    )
    cosine, sine_table = rotary_tables(sequence_length, HEAD_DIM)
    q_scale = root_mean_scale(query_unrotated)
    q_unit = query_unrotated * q_scale
    query_rows = (
        rotate(q_unit * query_norm_gain, cosine, sine_table)
        .astype(jnp.bfloat16)
        .reshape(sequence_length, kv_local, query_group_count, HEAD_DIM)
    )
    k_scale = root_mean_scale(key_unrotated)
    k_unit = key_unrotated * k_scale
    keys_rows = rotate(k_unit * k_gain, cosine, sine_table).astype(jnp.bfloat16)
    positions = jnp.arange(sequence_length)
    documents = doc_ids[0]
    allowed = (positions[None, :] <= positions[:, None]) & (
        documents[None, :] == documents[:, None]
    )

    def score_block():
        raw_scores = (
            jnp.einsum("qngd,knd->ngqk", query_rows, keys_rows, preferred_element_type=jnp.float32)
            * inv_root
        )
        return jnp.where(allowed, raw_scores, -1e30)

    scores = score_block()
    row_peak = jnp.max(scores, axis=-1, keepdims=True)
    attn_exps = jnp.exp(scores - row_peak)
    row_total = jnp.sum(attn_exps, axis=-1, keepdims=True)
    log_total = row_peak + jnp.log(row_total)
    probs_low = (attn_exps / row_total).astype(jnp.bfloat16)
    attended = jnp.einsum(
        "ngqk,knd->qngd", probs_low, value_rows, preferred_element_type=jnp.float32
    )
    attended = attended.reshape(sequence_length, heads_local * HEAD_DIM).astype(jnp.bfloat16)
    attn_part = contract(attended, o_full, 1, 1)
    attn_total = lax.psum(attn_part, "gy")
    residual = inputs_f + attn_total
    scale_two = root_mean_scale(residual)
    unit_two = residual * scale_two
    normed_ffn = (unit_two * ffn_gain).astype(jnp.bfloat16)
    logits = jnp.dot(normed_ffn, router_full, preferred_element_type=jnp.float32)
    expert_iota = jnp.arange(experts_all, dtype=jnp.int32)
    route_hits = routes[:, :, None] == expert_iota
    hits_float = route_hits.astype(jnp.float32)
    chosen = jnp.sum(logits[:, None, :] * hits_float, axis=-1)
    gate_exps = jnp.exp(chosen)
    gate_values = gate_exps / jnp.sum(gate_exps, axis=1, keepdims=True)
    flat_hits = route_hits.reshape(pairs_count, experts_all).astype(jnp.int32)
    slot_rank = jnp.sum((jnp.cumsum(flat_hits, axis=0) - flat_hits) * flat_hits, axis=1)
    slot_dest = routes.reshape(-1) * capacity + slot_rank
    slot_pair = (
        jnp.full((experts_all * capacity,), pairs_count, jnp.int32)
        .at[slot_dest]
        .set(jnp.arange(pairs_count, dtype=jnp.int32))
    )
    slot_token = jnp.where(slot_pair < pairs_count, slot_pair // TOP, sequence_length)

    def to_experts(buffer):
        arrived = lax.all_to_all(buffer, "gx", split_axis=0, concat_axis=0, tiled=True)
        return arrived.reshape(devices_gx * capacity, model_width)

    def from_experts(partial_rows):
        share_rows = lax.psum_scatter(
            partial_rows.astype(jnp.bfloat16), "gy", scatter_dimension=1, tiled=True
        )
        returned = lax.all_to_all(
            share_rows.reshape(devices_gx, capacity, part_width),
            "gx",
            split_axis=0,
            concat_axis=0,
            tiled=True,
        )
        whole_rows = lax.all_gather(returned, "gy", axis=2, tiled=True)
        return whole_rows.reshape(devices_gx * capacity, model_width)

    w_gate = gate_weight[0]
    w_up = up_weight[0]
    w_down = down_weight[0]
    send_rows = jnp.take(normed_ffn, slot_token, axis=0, mode="fill", fill_value=0)
    expert_in = to_experts(send_rows.reshape(devices_gx, capacity, model_width))
    gate_in = jnp.dot(expert_in, w_gate, preferred_element_type=jnp.float32)
    up_in = jnp.dot(expert_in, w_up, preferred_element_type=jnp.float32)
    gate_sigmoid = jax.nn.sigmoid(gate_in)
    gate_swish = gate_in * gate_sigmoid
    activated = (gate_swish * up_in).astype(jnp.bfloat16)
    expert_part = jnp.dot(activated, w_down, preferred_element_type=jnp.float32)
    expert_out = from_experts(expert_part)
    pair_rows = jnp.take(expert_out, slot_dest, axis=0).reshape(sequence_length, TOP, model_width)
    mixed_rows = jnp.einsum(
        "tk,tkd->td", gate_values, pair_rows, preferred_element_type=jnp.float32
    )
    output = (residual + mixed_rows).astype(jnp.bfloat16)
    grad_out_f = cotangent.astype(jnp.float32)
    grad_gates = jnp.einsum("td,tkd->tk", grad_out_f, pair_rows, preferred_element_type=jnp.float32)
    grad_chosen = gate_values * (
        grad_gates - jnp.sum(gate_values * grad_gates, axis=1, keepdims=True)
    )
    grad_logits = jnp.sum(grad_chosen[:, :, None] * hits_float, axis=1).astype(jnp.bfloat16)
    router_term = contract(normed_ffn, grad_logits, 0, 0)
    grad_ffn_in = contract(grad_logits, router_full, 1, 1)
    slot_gate = jnp.take(gate_values.reshape(-1), slot_pair, mode="fill", fill_value=0.0)
    grad_send = (
        jnp.take(grad_out_f, slot_token, axis=0, mode="fill", fill_value=0) * slot_gate[:, None]
    )
    grad_expert_out = to_experts(
        grad_send.astype(jnp.bfloat16).reshape(devices_gx, capacity, model_width)
    )
    grad_act = contract(grad_expert_out, w_down, 1, 1)
    down_term = contract(activated, grad_expert_out, 0, 0)
    grad_gate_in = (
        grad_act * up_in * gate_sigmoid * (1.0 + gate_in * (1.0 - gate_sigmoid))
    ).astype(jnp.bfloat16)
    grad_up_in = (grad_act * gate_swish).astype(jnp.bfloat16)
    gate_term = contract(expert_in, grad_gate_in, 0, 0)
    up_term = contract(expert_in, grad_up_in, 0, 0)
    grad_in_part = contract(grad_gate_in, w_gate, 1, 1) + contract(grad_up_in, w_up, 1, 1)
    grad_rows = from_experts(grad_in_part)
    grad_pairs = jnp.take(grad_rows, slot_dest, axis=0).reshape(sequence_length, TOP, model_width)
    grad_ffn_in = grad_ffn_in + jnp.sum(grad_pairs.astype(jnp.float32), axis=1)
    ffn_gain_term = jnp.sum(grad_ffn_in * unit_two, axis=0)
    grad_residual = grad_out_f + norm_back(grad_ffn_in * ffn_gain, unit_two, scale_two)
    grad_attn = grad_residual.astype(jnp.bfloat16)
    out_term = contract(grad_attn, attended, 0, 0)
    grad_attended = jnp.dot(grad_attn, o_full, preferred_element_type=jnp.float32).astype(
        jnp.bfloat16
    )
    grad_attended = grad_attended.reshape(sequence_length, kv_local, query_group_count, HEAD_DIM)
    probs_again = jnp.exp(score_block() - log_total)
    probs_again_low = probs_again.astype(jnp.bfloat16)
    grad_values = jnp.einsum(
        "ngqk,qngd->knd", probs_again_low, grad_attended, preferred_element_type=jnp.float32
    )
    grad_probs = jnp.einsum(
        "qngd,knd->ngqk", grad_attended, value_rows, preferred_element_type=jnp.float32
    )
    prob_inner = jnp.sum(probs_again * grad_probs, axis=-1, keepdims=True)
    grad_scores = (probs_again * (grad_probs - prob_inner)).astype(jnp.bfloat16)
    grad_queries = (
        jnp.einsum("ngqk,knd->qngd", grad_scores, keys_rows, preferred_element_type=jnp.float32)
        * inv_root
    )
    grad_keys = (
        jnp.einsum("ngqk,qngd->knd", grad_scores, query_rows, preferred_element_type=jnp.float32)
        * inv_root
    )
    grad_q_rot = rotate(
        grad_queries.reshape(sequence_length, heads_local, HEAD_DIM), cosine, -sine_table
    )
    grad_k_rot = rotate(grad_keys, cosine, -sine_table)
    q_gain_term = jnp.sum(grad_q_rot * q_unit, axis=(0, 1))
    k_gain_term = jnp.sum(grad_k_rot * k_unit, axis=(0, 1))
    grad_q_raw = (
        norm_back(grad_q_rot * query_norm_gain, q_unit, q_scale)
        .astype(jnp.bfloat16)
        .reshape(sequence_length, heads_local * HEAD_DIM)
    )
    grad_k_raw = (
        norm_back(grad_k_rot * k_gain, k_unit, k_scale)
        .astype(jnp.bfloat16)
        .reshape(sequence_length, kv_local * HEAD_DIM)
    )
    grad_v_raw = grad_values.astype(jnp.bfloat16).reshape(sequence_length, kv_local * HEAD_DIM)
    q_term = contract(normalized_input, grad_q_raw, 0, 0)
    k_term = contract(normalized_input, grad_k_raw, 0, 0)
    v_term = contract(normalized_input, grad_v_raw, 0, 0)
    grad_normed_part = (
        contract(grad_q_raw, q_full, 1, 1)
        + contract(grad_k_raw, k_full, 1, 1)
        + contract(grad_v_raw, v_full, 1, 1)
    )
    grad_normed = lax.psum(grad_normed_part, "gy")
    attn_gain_term = jnp.sum(grad_normed * unit_one, axis=0)
    grad_input = (grad_residual + norm_back(grad_normed * attn_gain, unit_one, scale_one)).astype(
        jnp.bfloat16
    )
    grad_q, grad_k, grad_v, grad_out, grad_router = (
        lax.psum_scatter(q_term, "gx", scatter_dimension=0, tiled=True),
        lax.psum_scatter(k_term, "gx", scatter_dimension=0, tiled=True),
        lax.psum_scatter(v_term, "gx", scatter_dimension=0, tiled=True),
        lax.psum_scatter(out_term, "gx", scatter_dimension=0, tiled=True),
        lax.psum_scatter(router_term, "gx", scatter_dimension=0, tiled=True),
    )
    own_mask = (jnp.arange(model_width) // part_width == lax.axis_index("gy")).astype(jnp.float32)
    gain_attn, gain_ffn, gain_query, gain_key = lax.psum(
        (attn_gain_term * own_mask, ffn_gain_term * own_mask, q_gain_term, k_gain_term),
        ("gx", "gy"),
    )
    expert_grads = (gate_term[None], up_term[None], down_term[None])
    return (
        output,
        grad_input,
        grad_q,
        grad_k,
        grad_v,
        grad_out,
        grad_router,
        gain_attn,
        gain_ffn,
        gain_query,
        gain_key,
        expert_grads[0],
        expert_grads[1],
        expert_grads[2],
    )


def solution(mesh):
    return jax.shard_map(
        on_device,
        mesh=mesh,
        in_specs=(
            P("gx", None),
            P("gx", None),
            P("gx", None),
            P("gx", "gy"),
            P("gx", "gy"),
            P("gx", "gy"),
            P("gx", "gy"),
            P("gx", None),
            P(),
            P(),
            P(),
            P(),
            P("gx", None, "gy"),
            P("gx", None, "gy"),
            P("gx", "gy", None),
            P("gx", None),
        ),
        out_specs=(
            P("gx", None),
            P("gx", None),
            P("gx", "gy"),
            P("gx", "gy"),
            P("gx", "gy"),
            P("gx", "gy"),
            P("gx", None),
            P(),
            P(),
            P(),
            P(),
            P("gx", None, "gy"),
            P("gx", None, "gy"),
            P("gx", "gy", None),
        ),
        check_vma=False,
    )
```

profile of v0, /device:TPU:0, one launch (start us, length us, event | category | flops | bytes accessed | tf_op | source)
XLA Modules:
  0.0 2393.8 jit_solution(7394783359592529284)
XLA Ops:
  12.9 55.9 %all-gather.9.cloned.1.call-done = bf16[2048,256]{1,0:T(8,128)(2,1)} async-done(((bf16[128,256]{1,0:T(8,128)(2,1)}), bf16[2048,256]{1,0:T(8,128)(2,1)}) %all-gather.9.cloned.1.call-update) | async-done | bytes 1048592 | tf_op jit(solution)/shard_map/all_gather | solution.py:84
  71.7 54.0 %all-gather.7.cloned.1.call-done = bf16[2048,256]{1,0:T(8,128)(2,1)} async-done(((bf16[128,256]{1,0:T(8,128)(2,1)}), bf16[2048,256]{1,0:T(8,128)(2,1)}) %all-gather.7.cloned.1.call-update) | async-done | bytes 1048592 | tf_op jit(solution)/shard_map/all_gather | solution.py:85
  128.2 111.9 %all-gather.11.cloned.1.call-done = bf16[2048,2048]{1,0:T(8,128)(2,1)} async-done(((bf16[128,2048]{1,0:T(8,128)(2,1)}), bf16[2048,2048]{1,0:T(8,128)(2,1)}) %all-gather.11.cloned.1.call-update) | async-done | bytes 8388624 | tf_op jit(solution)/shard_map/all_gather | solution.py:83
  257.4 96.4 %all-gather.13.cloned.1.call-done = bf16[2048,2048]{1,0:T(8,128)(2,1)} async-done(((bf16[128,2048]{1,0:T(8,128)(2,1)}), bf16[2048,2048]{1,0:T(8,128)(2,1)}) %all-gather.13.cloned.1.call-update) | async-done | bytes 8388624 | tf_op jit(solution)/shard_map/all_gather | solution.py:86
  400.9 235.8 %all_to_all.20 = bf16[16,160,2048]{2,1,0:T(8,128)(2,1)S(1)} all-to-all(bf16[16,160,2048]{2,1,0:T(8,128)(2,1)S(1)} %broadcast_select_fusion), channel_id=1, replica_groups=mesh['gx'=16,'gy'=2] {'gx'}, dimensions={0} | all-to-all | bytes 20971520 | tf_op jit(solution)/shard_map/all_to_all | solution.py:164
  660.5 17.5 reduce-scatter.8.cloned.1.call-done
  678.0 123.5 %all_to_all.21 = bf16[16,160,1024]{2,1,0:T(8,128)(2,1)} all-to-all(bf16[16,160,1024]{2,1,0:T(8,128)(2,1)} %bitcast.259), channel_id=1, replica_groups=mesh['gx'=16,'gy'=2] {'gx'}, dimensions={0} | all-to-all | bytes 10485760 | tf_op jit(solution)/shard_map/all_to_all | solution.py:171
  804.4 21.4 gather_fusion.1
  825.8 38.2 %all_gather.25 = bf16[2048,16]{0,1:T(8,128)(2,1)S(1)} all-gather(bf16[128,16]{0,1:T(8,128)(2,1)S(1)} %copy-done.68), channel_id=1, replica_groups=mesh['gx'=16,'gy'=2] {'gx'}, dimensions={0}, use_global_device_ids=true | all-gather | bytes 69632 | tf_op jit(solution)/shard_map/all_gather | solution.py:87
  864.6 21.7 gather_fusion.3
  895.6 13.6 gather_fusion.2
  917.7 224.4 %all_to_all.22 = bf16[16,160,2048]{2,1,0:T(8,128)(2,1)S(1)} all-to-all(bf16[16,160,2048]{2,1,0:T(8,128)(2,1)S(1)} %multiply_convert_fusion), channel_id=1, replica_groups=mesh['gx'=16,'gy'=2] {'gx'}, dimensions={0} | all-to-all | bytes 20971520 | tf_op jit(solution)/shard_map/all_to_all | solution.py:164
  1162.4 12.4 add_convert_fusion
  1174.8 17.4 reduce-scatter.10.cloned.1.call-done
  1192.2 123.6 %all_to_all.23 = bf16[16,160,1024]{2,1,0:T(8,128)(2,1)} all-to-all(bf16[16,160,1024]{2,1,0:T(8,128)(2,1)} %bitcast.260), channel_id=1, replica_groups=mesh['gx'=16,'gy'=2] {'gx'}, dimensions={0} | all-to-all | bytes 10485760 | tf_op jit(solution)/shard_map/all_to_all | solution.py:171
  1323.9 13.2 all-gather.17.cloned.1.call-done
  1337.1 21.8 gather_fusion.4
  1359.0 13.4 convert_reduce_fusion
  1459.6 11.2 convolution_bitcast_fusion.1
  1480.5 40.9 %all-reduce = (f32[2048]{0:T(1024)}, f32[2048]{0:T(1024)}, f32[128]{0:T(128)}, f32[128]{0:T(128)}) all-reduce(f32[2048]{0:T(1024)S(1)} %get-tuple-element.66, f32[2048]{0:T(1024)S(1)} %get-tuple-element.65, f32[128]{0:T(128)S(1)} %bitcast_reduce_fusion, f32[128]{0:T(128)S(1)} %bitcast_reduce_fusion.1), channel_id=1, replica_groups=mesh['gx'=16,'gy'=2] {'gx','gy'}, use_global_device_ids=true, to_apply=%region_30.32 | all-reduce | flops 4352 | bytes 34816 | tf_op jit(solution)/shard_map/psum | solution.py:289
  1525.4 79.5 %reduce-scatter.16.cloned.1.call-done = f32[128,256]{1,0:T(8,128)} async-done(((f32[2048,256]{1,0:T(8,128)}), f32[128,256]{1,0:T(8,128)}) %reduce-scatter.16.cloned.1.call-update) | async-done | bytes 131088 | tf_op jit(solution)/shard_map/reduce_scatter | solution.py:284
  1604.9 80.9 %reduce-scatter.14.cloned.1.call-done = f32[128,256]{1,0:T(8,128)} async-done(((f32[2048,256]{1,0:T(8,128)}), f32[128,256]{1,0:T(8,128)}) %reduce-scatter.14.cloned.1.call-update) | async-done | bytes 131088 | tf_op jit(solution)/shard_map/reduce_scatter | solution.py:283
  1685.8 346.4 %reduce-scatter.18.cloned.1.call-done = f32[128,2048]{1,0:T(8,128)} async-done(((f32[2048,2048]{1,0:T(8,128)}), f32[128,2048]{1,0:T(8,128)}) %reduce-scatter.18.cloned.1.call-update) | async-done | bytes 1048592 | tf_op jit(solution)/shard_map/reduce_scatter | solution.py:285
  2032.2 354.8 %reduce-scatter.12.cloned.1.call-done = f32[128,2048]{1,0:T(8,128)} async-done(((f32[2048,2048]{1,0:T(8,128)}), f32[128,2048]{1,0:T(8,128)}) %reduce-scatter.12.cloned.1.call-update) | async-done | bytes 1048592 | tf_op jit(solution)/shard_map/reduce_scatter | solution.py:282
  (311 shorter events, 248.4 us)
Async XLA Ops:
  7.2 644.9 %copy-start = (bf16[1,384,2048]{2,1,0:T(8,128)(2,1)S(1)}, bf16[1,384,2048]{2,1,0:T(8,128)(2,1)}, u32[]{:S(2)}) copy-start(bf16[1,384,2048]{2,1,0:T(8,128)(2,1)} %param.32) | copy-start | bytes 4718596
  7.2 61.6 %all-gather.9.cloned.1.call-start = ((), (), s32[]{:S(2)}) async-start(), calls=%async_computation.12 | async-start | bytes 1114112 | tf_op jit(solution)/shard_map/all_gather | solution.py:84
  8.0 117.7 %all-gather.7.cloned.1.call-start = ((), (), s32[]{:S(2)}) async-start(), calls=%async_computation.11 | async-start | bytes 1114112 | tf_op jit(solution)/shard_map/all_gather | solution.py:85
  8.7 231.4 %all-gather.11.cloned.1.call-start = ((), (), s32[]{:S(2)}) async-start(), calls=%async_computation.13 | async-start | bytes 8912896 | tf_op jit(solution)/shard_map/all_gather | solution.py:83
  9.4 344.4 %all-gather.13.cloned.1.call-start = ((), (), s32[]{:S(2)}) async-start(), calls=%async_computation.14 | async-start | bytes 8912896 | tf_op jit(solution)/shard_map/all_gather | solution.py:86
  10.0 370.9 %all-reduce.4.cloned.1.call-start = ((), (), s32[]{:S(2)}) async-start(), calls=%async_computation.15 | async-start | bytes 4194304 | tf_op jit(solution)/shard_map/psum | solution.py:141
  11.6 228.5 %copy-start.60 = (f32[256]{0:T(256)}, f32[256]{0:T(256)S(1)}, u32[]{:S(2)}) copy-start(f32[256]{0:T(256)S(1)} %add_rsqrt_fusion.3) | copy-start | bytes 3076
  12.9 237.7 %copy-start.28 = (f32[256,64]{1,0:T(8,128)}, f32[256,64]{1,0:T(8,128)S(1)}, u32[]{:S(2)}) copy-start(f32[256,64]{1,0:T(8,128)S(1)} %get-tuple-element.55) | copy-start | bytes 196612
  71.7 180.3 %copy-start.40 = (bf16[256,2,64]{2,0,1:T(8,128)(2,1)}, bf16[256,2,64]{2,0,1:T(8,128)(2,1)S(1)}, u32[]{:S(2)}) copy-start(bf16[256,2,64]{2,0,1:T(8,128)(2,1)S(1)} %get-tuple-element.51) | copy-start | bytes 196612
  71.7 180.3 %copy-start.42 = (bf16[256,2,64]{2,0,1:T(8,128)(2,1)}, bf16[256,2,64]{2,0,1:T(8,128)(2,1)S(1)}, u32[]{:S(2)}) copy-start(bf16[256,2,64]{2,0,1:T(8,128)(2,1)S(1)} %get-tuple-element.52) | copy-start | bytes 196612
  361.3 316.7 %reduce-scatter.8.cloned.1.call-start = ((), (), s32[]{:S(2)}) async-start(), calls=%async_computation.16 | async-start | bytes 15728640 | tf_op jit(solution)/shard_map/reduce_scatter | solution.py:168
  384.5 479.6 %copy-start.2 = (bf16[256,2048]{1,0:T(8,128)(2,1)}, bf16[256,2048]{1,0:T(8,128)(2,1)S(1)}, u32[]{:S(2)}) copy-start(bf16[256,2048]{1,0:T(8,128)(2,1)S(1)} %multiply_convert_fusion.4) | copy-start | bytes 3145732
  400.9 235.9 %copy-start.35 = (bf16[1,2048,384]{2,1,0:T(8,128)(2,1)S(1)}, bf16[1,2048,384]{2,1,0:T(8,128)(2,1)}, u32[]{:S(2)}) copy-start(bf16[1,2048,384]{2,1,0:T(8,128)(2,1)} %param.30) | copy-start | bytes 4718596
  660.4 204.2 %all-gather.15.cloned.1.call-start = ((), (), s32[]{:S(2)}) async-start(), calls=%async_computation.17 | async-start | bytes 15728640 | tf_op jit(solution)/shard_map/all_gather | solution.py:178
  801.6 390.6 %reduce-scatter.10.cloned.1.call-start = ((), (), s32[]{:S(2)}) async-start(), calls=%async_computation.18 | async-start | bytes 15728640 | tf_op jit(solution)/shard_map/reduce_scatter | solution.py:168
  917.7 224.4 %copy-start.74 = (f32[2560,384]{1,0:T(8,128)S(1)}, f32[2560,384]{1,0:T(8,128)}, u32[]{:S(2)}) copy-start(f32[2560,384]{1,0:T(8,128)} %copy-done.73) | copy-start | bytes 11796484
  1174.8 162.4 %all-gather.17.cloned.1.call-start = ((), (), s32[]{:S(2)}) async-start(), calls=%async_computation.19 | async-start | bytes 15728640 | tf_op jit(solution)/shard_map/all_gather | solution.py:178
  1315.8 162.5 %all-reduce.6.cloned.1.call-start = ((), (), s32[]{:S(2)}) async-start(), calls=%async_computation.20 | async-start | bytes 4194304 | tf_op jit(solution)/shard_map/psum | solution.py:276
  1422.9 102.5 %reduce-scatter.20.cloned.1.call-start = ((), (), s32[]{:S(2)}) async-start(), calls=%async_computation.25 | async-start | bytes 139264 | tf_op jit(solution)/shard_map/reduce_scatter | solution.py:286
  1425.0 179.9 %reduce-scatter.16.cloned.1.call-start = ((), (), s32[]{:S(2)}) async-start(), calls=%async_computation.23 | async-start | bytes 2228224 | tf_op jit(solution)/shard_map/reduce_scatter | solution.py:284
  1427.1 258.7 %reduce-scatter.14.cloned.1.call-start = ((), (), s32[]{:S(2)}) async-start(), calls=%async_computation.22 | async-start | bytes 2228224 | tf_op jit(solution)/shard_map/reduce_scatter | solution.py:283
  1429.1 603.2 %reduce-scatter.18.cloned.1.call-start = ((), (), s32[]{:S(2)}) async-start(), calls=%async_computation.24 | async-start | bytes 17825792 | tf_op jit(solution)/shard_map/reduce_scatter | solution.py:285
  1439.4 947.6 %reduce-scatter.12.cloned.1.call-start = ((), (), s32[]{:S(2)}) async-start(), calls=%async_computation.21 | async-start | bytes 17825792 | tf_op jit(solution)/shard_map/reduce_scatter | solution.py:282
  1521.5 865.6 %copy-start.1 = (bf16[1,384,2048]{2,1,0:T(8,128)(2,1)S(1)}, bf16[1,384,2048]{2,1,0:T(8,128)(2,1)}, u32[]{:S(2)}) copy-start(bf16[1,384,2048]{2,1,0:T(8,128)(2,1)} %param.32) | copy-start | bytes 4718596
  (71 other events, 584.1 us)
Sparse Core Ops, SparseCore 0:
  10.8 57.9 all-gather.8
  71.6 54.0 all-gather.6
  128.5 111.6 all-gather.10
  242.8 111.0 all-gather.12
  361.4 19.5 all-reduce.3
  660.5 17.4 reduce-scatter.7
  801.7 21.1 all-gather.14
  1174.9 17.2 reduce-scatter.9
  1315.9 21.1 all-gather.16
  1423.0 22.3 all-reduce.5
  1448.2 77.0 reduce-scatter.19
  1528.1 76.7 reduce-scatter.15
  1607.9 77.8 reduce-scatter.13
  1688.6 343.5 reduce-scatter.17
  2035.0 351.9 reduce-scatter.11
where the time goes:
time: 2400 us; the launch traced here: 2390 us
  waiting for transfers between devices  1240 us (52%)
  blocking collectives  787 us (33%)
  matrix products  166 us (7%)
  local copies, waits for them, and re-layouts  126 us (5%)
  other arithmetic  64.4 us (3%)
    all_to_all x2, blocking collectives, to_experts(): lax.all_to_all(buffer, 'gx', split_axis=0, concat_axis=0, tiled=True)  460 us
    reduce_scatter x1, waiting for transfers between devices, on_device(): lax.psum_scatter(q_term, 'gx', scatter_dimension=0, tiled=True)  355 us
    reduce_scatter x1, waiting for transfers between devices, on_device(): lax.psum_scatter(out_term, 'gx', scatter_dimension=0, tiled=True)  346 us
    all_to_all x2, blocking collectives, from_experts(): lax.all_to_all(share_rows.reshape(devices_gx, capacity, part_width), 'gx'...  247 us
    all_gather x1, waiting for transfers between devices, on_device(): lax.all_gather(q_weight, 'gx', axis=0, tiled=True)  112 us
    dot_general x16, matrix products, contract(): lax.dot_general(first_op, second_op, (((first_dim,), (second_dim,)), ((),...  100 us
    all_gather x1, waiting for transfers between devices, on_device(): lax.all_gather(out_weight, 'gx', axis=0, tiled=True)  96.4 us
    reduce_scatter x1, waiting for transfers between devices, on_device(): lax.psum_scatter(k_term, 'gx', scatter_dimension=0, tiled=True)  80.9 us
  transfers between devices with their start and end apart: 15, of which 12 were waited for; matrix products, arithmetic and copies ran while one was open for 5% of the time, Pallas kernels for 0%

commit v1 on v0

--- a/solution.py
+++ b/solution.py
@@ -49,6 +49,164 @@
         (((first_dim,), (second_dim,)), ((), ())),
         preferred_element_type=jnp.float32,
     )
+
+
+def scatter_sum(term):
+    low = lax.psum_scatter(term.astype(jnp.bfloat16), "gx", scatter_dimension=0, tiled=True)
+    return low.astype(jnp.float32)
+
+
+def sparse_experts(normed_ffn, logits, route_hits, routes, cotangent, w_gate, w_up, w_down):
+    sequence_length, model_width = normed_ffn.shape
+    experts_all = logits.shape[1]
+    devices_gx = lax.axis_size("gx")
+    part_width = model_width // lax.axis_size("gy")
+    capacity = 5 * sequence_length * TOP // (4 * experts_all)
+    pairs_count = sequence_length * TOP
+    hits_float = route_hits.astype(jnp.float32)
+    chosen = jnp.sum(logits[:, None, :] * hits_float, axis=-1)
+    gate_exps = jnp.exp(chosen)
+    gate_values = gate_exps / jnp.sum(gate_exps, axis=1, keepdims=True)
+    flat_hits = route_hits.reshape(pairs_count, experts_all).astype(jnp.int32)
+    slot_rank = jnp.sum((jnp.cumsum(flat_hits, axis=0) - flat_hits) * flat_hits, axis=1)
+    slot_dest = routes.reshape(-1) * capacity + slot_rank
+    slot_pair = (
+        jnp.full((experts_all * capacity,), pairs_count, jnp.int32)
+        .at[slot_dest]
+        .set(jnp.arange(pairs_count, dtype=jnp.int32))
+    )
+    slot_token = jnp.where(slot_pair < pairs_count, slot_pair // TOP, sequence_length)
+
+    def to_experts(buffer):
+        arrived = lax.all_to_all(buffer, "gx", split_axis=0, concat_axis=0, tiled=True)
+        return arrived.reshape(devices_gx * capacity, model_width)
+
+    def from_experts(partial_rows):
+        share_rows = lax.psum_scatter(
+            partial_rows.astype(jnp.bfloat16), "gy", scatter_dimension=1, tiled=True
+        )
+        returned = lax.all_to_all(
+            share_rows.reshape(devices_gx, capacity, part_width),
+            "gx",
+            split_axis=0,
+            concat_axis=0,
+            tiled=True,
+        )
+        whole_rows = lax.all_gather(returned, "gy", axis=2, tiled=True)
+        return whole_rows.reshape(devices_gx * capacity, model_width)
+
+    send_rows = jnp.take(normed_ffn, slot_token, axis=0, mode="fill", fill_value=0)
+    expert_in = to_experts(send_rows.reshape(devices_gx, capacity, model_width))
+    gate_in = jnp.dot(expert_in, w_gate, preferred_element_type=jnp.float32)
+    up_in = jnp.dot(expert_in, w_up, preferred_element_type=jnp.float32)
+    gate_sigmoid = jax.nn.sigmoid(gate_in)
+    gate_swish = gate_in * gate_sigmoid
+    activated = (gate_swish * up_in).astype(jnp.bfloat16)
+    expert_part = jnp.dot(activated, w_down, preferred_element_type=jnp.float32)
+    expert_out = from_experts(expert_part)
+    pair_rows = jnp.take(expert_out, slot_dest, axis=0).reshape(sequence_length, TOP, model_width)
+    mixed_rows = jnp.einsum(
+        "tk,tkd->td", gate_values, pair_rows, preferred_element_type=jnp.float32
+    )
+    grad_out_f = cotangent.astype(jnp.float32)
+    grad_gates = jnp.einsum("td,tkd->tk", grad_out_f, pair_rows, preferred_element_type=jnp.float32)
+    grad_chosen = gate_values * (
+        grad_gates - jnp.sum(gate_values * grad_gates, axis=1, keepdims=True)
+    )
+    grad_logits = jnp.sum(grad_chosen[:, :, None] * hits_float, axis=1).astype(jnp.bfloat16)
+    slot_gate = jnp.take(gate_values.reshape(-1), slot_pair, mode="fill", fill_value=0.0)
+    grad_send = (
+        jnp.take(grad_out_f, slot_token, axis=0, mode="fill", fill_value=0) * slot_gate[:, None]
+    )
+    grad_expert_out = to_experts(
+        grad_send.astype(jnp.bfloat16).reshape(devices_gx, capacity, model_width)
+    )
+    grad_act = contract(grad_expert_out, w_down, 1, 1)
+    down_term = contract(activated, grad_expert_out, 0, 0)
+    grad_gate_in = (
+        grad_act * up_in * gate_sigmoid * (1.0 + gate_in * (1.0 - gate_sigmoid))
+    ).astype(jnp.bfloat16)
+    grad_up_in = (grad_act * gate_swish).astype(jnp.bfloat16)
+    gate_term = contract(expert_in, grad_gate_in, 0, 0)
+    up_term = contract(expert_in, grad_up_in, 0, 0)
+    grad_in_part = contract(grad_gate_in, w_gate, 1, 1) + contract(grad_up_in, w_up, 1, 1)
+    grad_rows = from_experts(grad_in_part)
+    grad_pairs = jnp.take(grad_rows, slot_dest, axis=0).reshape(sequence_length, TOP, model_width)
+    grad_rows_sum = jnp.sum(grad_pairs.astype(jnp.float32), axis=1)
+    return mixed_rows, grad_rows_sum, grad_logits, (gate_term[None], up_term[None], down_term[None])
+
+
+def swap_cores(rows):
+    return lax.ppermute(rows, "gy", [(0, 1), (1, 0)])
+
+
+def dense_experts(normed_ffn, logits, route_hits, cotangent, w_gate, w_up, w_down):
+    sequence_length, model_width = normed_ffn.shape
+    devices_gx = lax.axis_size("gx")
+    half_rows = sequence_length // lax.axis_size("gy")
+    my_core = lax.axis_index("gy")
+    my_expert = lax.axis_index("gx")
+
+    def own_half(rows):
+        return lax.dynamic_slice_in_dim(rows, my_core * half_rows, half_rows, 0)
+
+    def to_experts(rows):
+        own_rows = lax.all_gather(own_half(rows), "gx", axis=0, tiled=True)
+        return (own_rows, swap_cores(own_rows))
+
+    def both_halves(own_rows):
+        other = swap_cores(own_rows)
+        return jnp.where(
+            my_core == 0,
+            jnp.concatenate([own_rows, other], axis=0),
+            jnp.concatenate([other, own_rows], axis=0),
+        )
+
+    def from_experts(partial_rows):
+        there = swap_cores(partial_rows(1).astype(jnp.bfloat16))
+        own_rows = (partial_rows(0) + there).astype(jnp.bfloat16)
+        summed = lax.psum_scatter(own_rows, "gx", scatter_dimension=0, tiled=True)
+        return both_halves(summed).astype(jnp.float32)
+
+    def dot(left, right):
+        return jnp.dot(left, right, preferred_element_type=jnp.float32)
+
+    gate_exps = jnp.exp(jnp.where(jnp.any(route_hits, axis=1), logits, -1e30))
+    gate_all = gate_exps / jnp.sum(gate_exps, axis=1, keepdims=True)
+    grad_sets = to_experts(cotangent)
+    row_sets = to_experts(normed_ffn)
+    gate_sets = to_experts(gate_all)
+    weighted, gate_terms, grad_gate_in, grad_up_in = [], [], [], []
+    for part in range(2):
+        gate_rows = lax.dynamic_slice_in_dim(gate_sets[part], my_expert, 1, 1)
+        gate_in = dot(row_sets[part], w_gate)
+        up_in = dot(row_sets[part], w_up)
+        grad_hidden = contract(grad_sets[part], w_down, 1, 1)
+        gate_sigmoid = jax.nn.sigmoid(gate_in)
+        gate_swish = gate_in * gate_sigmoid
+        activated = gate_swish * up_in
+        gate_terms.append(jnp.sum(activated * grad_hidden, axis=1))
+        weighted.append((gate_rows * activated).astype(jnp.bfloat16))
+        grad_act = gate_rows * grad_hidden
+        grad_gate_in.append(
+            (grad_act * up_in * gate_sigmoid * (1.0 + gate_in * (1.0 - gate_sigmoid))).astype(jnp.bfloat16)
+        )
+        grad_up_in.append((grad_act * gate_swish).astype(jnp.bfloat16))
+    mixed_rows = from_experts(lambda part: dot(weighted[part], w_down))
+    grad_rows_sum = from_experts(
+        lambda part: contract(grad_gate_in[part], w_gate, 1, 1) + contract(grad_up_in[part], w_up, 1, 1)
+    )
+    down_term, gate_term, up_term = (
+        contract(first[0], second[0], 0, 0) + contract(first[1], second[1], 0, 0)
+        for first, second in ((weighted, grad_sets), (row_sets, grad_gate_in), (row_sets, grad_up_in))
+    )
+    own_terms = gate_terms[0] + swap_cores(gate_terms[1])
+    back = lax.all_to_all(own_terms.reshape(devices_gx, half_rows), "gx", split_axis=0, concat_axis=0, tiled=True)
+    grad_gates = both_halves(back.T)
+    grad_logits = (
+        gate_all * (grad_gates - jnp.sum(gate_all * grad_gates, axis=1, keepdims=True))
+    ).astype(jnp.bfloat16)
+    return mixed_rows, grad_rows_sum, grad_logits, (gate_term[None], up_term[None], down_term[None])
 
 
 def on_device(
@@ -75,8 +233,6 @@
     devices_gy = lax.axis_size("gy")
     part_width = model_width // devices_gy
     experts_all = router_weight.shape[1]
-    capacity = 5 * sequence_length * TOP // (4 * experts_all)
-    pairs_count = sequence_length * TOP
     query_group_count = QUERY_HEADS // KEY_VALUE_HEADS
     inv_root = 1.0 / math.sqrt(HEAD_DIM)
     q_full, k_full, v_full, o_full, router_full = (
@@ -138,7 +294,7 @@
     )
     attended = attended.reshape(sequence_length, heads_local * HEAD_DIM).astype(jnp.bfloat16)
     attn_part = contract(attended, o_full, 1, 1)
-    attn_total = lax.psum(attn_part, "gy")
+    attn_total = attn_part + swap_cores(attn_part)
     residual = inputs_f + attn_total
     scale_two = root_mean_scale(residual)
     unit_two = residual * scale_two
@@ -146,82 +302,18 @@
     logits = jnp.dot(normed_ffn, router_full, preferred_element_type=jnp.float32)
     expert_iota = jnp.arange(experts_all, dtype=jnp.int32)
     route_hits = routes[:, :, None] == expert_iota
-    hits_float = route_hits.astype(jnp.float32)
-    chosen = jnp.sum(logits[:, None, :] * hits_float, axis=-1)
-    gate_exps = jnp.exp(chosen)
-    gate_values = gate_exps / jnp.sum(gate_exps, axis=1, keepdims=True)
-    flat_hits = route_hits.reshape(pairs_count, experts_all).astype(jnp.int32)
-    slot_rank = jnp.sum((jnp.cumsum(flat_hits, axis=0) - flat_hits) * flat_hits, axis=1)
-    slot_dest = routes.reshape(-1) * capacity + slot_rank
-    slot_pair = (
-        jnp.full((experts_all * capacity,), pairs_count, jnp.int32)
-        .at[slot_dest]
-        .set(jnp.arange(pairs_count, dtype=jnp.int32))
-    )
-    slot_token = jnp.where(slot_pair < pairs_count, slot_pair // TOP, sequence_length)
-
-    def to_experts(buffer):
-        arrived = lax.all_to_all(buffer, "gx", split_axis=0, concat_axis=0, tiled=True)
-        return arrived.reshape(devices_gx * capacity, model_width)
-
-    def from_experts(partial_rows):
-        share_rows = lax.psum_scatter(
-            partial_rows.astype(jnp.bfloat16), "gy", scatter_dimension=1, tiled=True
-        )
-        returned = lax.all_to_all(
-            share_rows.reshape(devices_gx, capacity, part_width),
-            "gx",
-            split_axis=0,
-            concat_axis=0,
-            tiled=True,
-        )
-        whole_rows = lax.all_gather(returned, "gy", axis=2, tiled=True)
-        return whole_rows.reshape(devices_gx * capacity, model_width)
-
-    w_gate = gate_weight[0]
-    w_up = up_weight[0]
-    w_down = down_weight[0]
-    send_rows = jnp.take(normed_ffn, slot_token, axis=0, mode="fill", fill_value=0)
-    expert_in = to_experts(send_rows.reshape(devices_gx, capacity, model_width))
-    gate_in = jnp.dot(expert_in, w_gate, preferred_element_type=jnp.float32)
-    up_in = jnp.dot(expert_in, w_up, preferred_element_type=jnp.float32)
-    gate_sigmoid = jax.nn.sigmoid(gate_in)
-    gate_swish = gate_in * gate_sigmoid
-    activated = (gate_swish * up_in).astype(jnp.bfloat16)
-    expert_part = jnp.dot(activated, w_down, preferred_element_type=jnp.float32)
-    expert_out = from_experts(expert_part)
-    pair_rows = jnp.take(expert_out, slot_dest, axis=0).reshape(sequence_length, TOP, model_width)
-    mixed_rows = jnp.einsum(
-        "tk,tkd->td", gate_values, pair_rows, preferred_element_type=jnp.float32
-    )
+    if experts_all <= 2 * TOP:
+        mixed_rows, grad_rows_sum, grad_logits, expert_grads = dense_experts(
+            normed_ffn, logits, route_hits, cotangent, gate_weight[0], up_weight[0], down_weight[0]
+        )
+    else:
+        mixed_rows, grad_rows_sum, grad_logits, expert_grads = sparse_experts(
+            normed_ffn, logits, route_hits, routes, cotangent, gate_weight[0], up_weight[0], down_weight[0]
+        )
     output = (residual + mixed_rows).astype(jnp.bfloat16)
     grad_out_f = cotangent.astype(jnp.float32)
-    grad_gates = jnp.einsum("td,tkd->tk", grad_out_f, pair_rows, preferred_element_type=jnp.float32)
-    grad_chosen = gate_values * (
-        grad_gates - jnp.sum(gate_values * grad_gates, axis=1, keepdims=True)
-    )
-    grad_logits = jnp.sum(grad_chosen[:, :, None] * hits_float, axis=1).astype(jnp.bfloat16)
     router_term = contract(normed_ffn, grad_logits, 0, 0)
-    grad_ffn_in = contract(grad_logits, router_full, 1, 1)
-    slot_gate = jnp.take(gate_values.reshape(-1), slot_pair, mode="fill", fill_value=0.0)
-    grad_send = (
-        jnp.take(grad_out_f, slot_token, axis=0, mode="fill", fill_value=0) * slot_gate[:, None]
-    )
-    grad_expert_out = to_experts(
-        grad_send.astype(jnp.bfloat16).reshape(devices_gx, capacity, model_width)
-    )
-    grad_act = contract(grad_expert_out, w_down, 1, 1)
-    down_term = contract(activated, grad_expert_out, 0, 0)
-    grad_gate_in = (
-        grad_act * up_in * gate_sigmoid * (1.0 + gate_in * (1.0 - gate_sigmoid))
-    ).astype(jnp.bfloat16)
-    grad_up_in = (grad_act * gate_swish).astype(jnp.bfloat16)
-    gate_term = contract(expert_in, grad_gate_in, 0, 0)
-    up_term = contract(expert_in, grad_up_in, 0, 0)
-    grad_in_part = contract(grad_gate_in, w_gate, 1, 1) + contract(grad_up_in, w_up, 1, 1)
-    grad_rows = from_experts(grad_in_part)
-    grad_pairs = jnp.take(grad_rows, slot_dest, axis=0).reshape(sequence_length, TOP, model_width)
-    grad_ffn_in = grad_ffn_in + jnp.sum(grad_pairs.astype(jnp.float32), axis=1)
+    grad_ffn_in = contract(grad_logits, router_full, 1, 1) + grad_rows_sum
     ffn_gain_term = jnp.sum(grad_ffn_in * unit_two, axis=0)
     grad_residual = grad_out_f + norm_back(grad_ffn_in * ffn_gain, unit_two, scale_two)
     grad_attn = grad_residual.astype(jnp.bfloat16)
@@ -273,16 +365,16 @@
         + contract(grad_k_raw, k_full, 1, 1)
         + contract(grad_v_raw, v_full, 1, 1)
     )
-    grad_normed = lax.psum(grad_normed_part, "gy")
+    grad_normed = grad_normed_part + swap_cores(grad_normed_part)
     attn_gain_term = jnp.sum(grad_normed * unit_one, axis=0)
     grad_input = (grad_residual + norm_back(grad_normed * attn_gain, unit_one, scale_one)).astype(
         jnp.bfloat16
     )
     grad_q, grad_k, grad_v, grad_out, grad_router = (
-        lax.psum_scatter(q_term, "gx", scatter_dimension=0, tiled=True),
-        lax.psum_scatter(k_term, "gx", scatter_dimension=0, tiled=True),
-        lax.psum_scatter(v_term, "gx", scatter_dimension=0, tiled=True),
-        lax.psum_scatter(out_term, "gx", scatter_dimension=0, tiled=True),
+        scatter_sum(q_term),
+        scatter_sum(k_term),
+        scatter_sum(v_term),
+        scatter_sum(out_term),
         lax.psum_scatter(router_term, "gx", scatter_dimension=0, tiled=True),
     )
     own_mask = (jnp.arange(model_width) // part_width == lax.axis_index("gy")).astype(jnp.float32)
@@ -290,7 +382,6 @@
         (attn_gain_term * own_mask, ffn_gain_term * own_mask, q_gain_term, k_gain_term),
         ("gx", "gy"),
     )
-    expert_grads = (gate_term[None], up_term[None], down_term[None])
     return (
         output,
         grad_input,

time: 2400 us -> 1780 us (0.74)
  blocking collectives: 787 us -> 127 us
  waiting for transfers between devices: 1240 us -> 1340 us
  local copies, waits for them, and re-layouts: 126 us -> 32 us
  matrix products: 166 us -> 208 us
    all_to_all x4 -> x0, blocking collectives: 707 us -> none  [the longest x2 460 us: to_experts(): lax.all_to_all(buffer, 'gx', split_axis=0, concat_axis=0, tiled=True)]
    all_gather x2, waiting for transfers between devices: 13.2 us -> 223 us  [to_experts(): own_rows = lax.all_gather(own_half(rows), 'gx', axis=0, tiled=True)]
    reduce_scatter x6, waiting for transfers between devices: 897 us -> 692 us  [the longest x4 363 us: scatter_sum(): lax.psum_scatter(term.astype(jnp.bfloat16), 'gx', scatter_dimension=0, ti...]
    gather x5 -> x0, local copies, waits for them, and re-layouts: 89.3 us -> none  [the longest x1 21.8 us: on_device(): jnp.take(grad_rows, slot_dest, axis=0)]
    reduce_scatter x1, waiting for transfers between devices: 0.01 us -> 79 us  [on_device(): lax.psum_scatter(router_term, 'gx', scatter_dimension=0, tiled=True)]
    dot_general x16 -> x22, matrix products: 100 us -> 140 us  [contract(): lax.dot_general(first_op, second_op, (((first_dim,), (second_dim,)), ((),...]
    all_gather x0 -> x1, blocking collectives: none -> 36.2 us  [to_experts(): own_rows = lax.all_gather(own_half(rows), 'gx', axis=0, tiled=True)]
  transfers between devices with their start and end apart: 15 -> 25, of which waited for: 12 -> 15; matrix products, arithmetic and copies ran while one was open for 5% -> 11% of each run, Pallas kernels for 0% -> 0%
where the time goes in v1:
time: 1780 us; the launch traced here: 1770 us
  waiting for transfers between devices  1340 us (75%)
  matrix products  208 us (12%)
  blocking collectives  127 us (7%)
  other arithmetic  46.9 us (3%)
  local copies, waits for them, and re-layouts  32 us (2%)
    reduce_scatter x4, waiting for transfers between devices, scatter_sum(): lax.psum_scatter(term.astype(jnp.bfloat16), 'gx', scatter_dimension=0, ti...  363 us
    reduce_scatter x2, waiting for transfers between devices, from_experts(): summed = lax.psum_scatter(own_rows, 'gx', scatter_dimension=0, tiled=True)  329 us
    all_gather x2, waiting for transfers between devices, to_experts(): own_rows = lax.all_gather(own_half(rows), 'gx', axis=0, tiled=True)  223 us
    dot_general x22, matrix products, contract(): lax.dot_general(first_op, second_op, (((first_dim,), (second_dim,)), ((),...  140 us
    all_gather x1, waiting for transfers between devices, on_device(): lax.all_gather(q_weight, 'gx', axis=0, tiled=True)  112 us
    all_gather x1, waiting for transfers between devices, on_device(): lax.all_gather(out_weight, 'gx', axis=0, tiled=True)  96.8 us
    reduce_scatter x1, waiting for transfers between devices, on_device(): lax.psum_scatter(router_term, 'gx', scatter_dimension=0, tiled=True)  79 us
    all_gather x1, waiting for transfers between devices, on_device(): lax.all_gather(key_matrix, 'gx', axis=0, tiled=True)  55.9 us
  transfers between devices with their start and end apart: 25, of which 15 were waited for; matrix products, arithmetic and copies ran while one was open for 11% of the time, Pallas kernels for 0%

profile of v1, /device:TPU:0, one launch (start us, length us, event | category | flops | bytes accessed | tf_op | source)
XLA Modules:
  0.0 1770.9 jit_solution(278714677014283421)
XLA Ops:
  12.9 55.9 %all-gather.9.cloned.1.call-done = bf16[2048,256]{1,0:T(8,128)(2,1)} async-done(((bf16[128,256]{1,0:T(8,128)(2,1)}), bf16[2048,256]{1,0:T(8,128)(2,1)}) %all-gather.9.cloned.1.call-update) | async-done | bytes 1048592 | tf_op jit(solution)/shard_map/all_gather | solution.py:240
  71.7 54.0 %all-gather.7.cloned.1.call-done = bf16[2048,256]{1,0:T(8,128)(2,1)} async-done(((bf16[128,256]{1,0:T(8,128)(2,1)}), bf16[2048,256]{1,0:T(8,128)(2,1)}) %all-gather.7.cloned.1.call-update) | async-done | bytes 1048592 | tf_op jit(solution)/shard_map/all_gather | solution.py:241
  128.2 111.9 %all-gather.11.cloned.1.call-done = bf16[2048,2048]{1,0:T(8,128)(2,1)} async-done(((bf16[128,2048]{1,0:T(8,128)(2,1)}), bf16[2048,2048]{1,0:T(8,128)(2,1)}) %all-gather.11.cloned.1.call-update) | async-done | bytes 8388624 | tf_op jit(solution)/shard_map/all_gather | solution.py:239
  257.0 96.8 %all-gather.13.cloned.1.call-done = bf16[2048,2048]{1,0:T(8,128)(2,1)} async-done(((bf16[128,2048]{1,0:T(8,128)(2,1)}), bf16[2048,2048]{1,0:T(8,128)(2,1)}) %all-gather.13.cloned.1.call-update) | async-done | bytes 8388624 | tf_op jit(solution)/shard_map/all_gather | solution.py:242
  373.7 109.2 %all-gather.15.cloned.1.call-done = bf16[2048,2048]{1,0:T(8,128)(2,1)} async-done(((bf16[128,2048]{1,0:T(8,128)(2,1)}), bf16[2048,2048]{1,0:T(8,128)(2,1)}) %all-gather.15.cloned.1.call-update) | async-done | bytes 8388624 | tf_op jit(solution)/shard_map/all_gather | solution.py:154
  482.9 114.2 %all-gather.17.cloned.1.call-done = bf16[2048,2048]{1,0:T(8,128)(2,1)} async-done(((bf16[128,2048]{1,0:T(8,128)(2,1)}), bf16[2048,2048]{1,0:T(8,128)(2,1)}) %all-gather.17.cloned.1.call-update) | async-done | bytes 8388624 | tf_op jit(solution)/shard_map/all_gather | solution.py:154
  622.1 10.0 multiply_reduce_fusion
  632.6 8.9 multiply_reduce_fusion.1
  645.9 41.3 %all_gather.28 = bf16[2048,16]{0,1:T(8,128)(2,1)S(1)} all-gather(bf16[128,16]{0,1:T(8,128)(2,1)S(1)} %copy-done.72), channel_id=1, replica_groups=mesh['gx'=16,'gy'=2] {'gx'}, dimensions={0}, use_global_device_ids=true | all-gather | bytes 69632 | tf_op jit(solution)/shard_map/all_gather | solution.py:243
  688.9 36.2 %all_gather.29 = f32[2048,16]{0,1:T(8,128)S(1)} all-gather(f32[128,16]{0,1:T(8,128)S(1)} %constant_dynamic-slice_fusion.4), channel_id=1, replica_groups=mesh['gx'=16,'gy'=2] {'gx'}, dimensions={0}, use_global_device_ids=true | all-gather | bytes 139264 | tf_op jit(solution)/shard_map/all_gather | solution.py:154
  740.9 10.3 add_convert_fusion.1
  769.0 17.1 add_convert_fusion
  786.3 8.4 convolution_convert_fusion.2
  795.0 13.0 collective-permute-done.3
  815.2 146.9 %reduce-scatter.10.cloned.1.call-done = bf16[128,2048]{1,0:T(8,128)(2,1)} async-done(((bf16[2048,2048]{1,0:T(8,128)(2,1)}), bf16[128,2048]{1,0:T(8,128)(2,1)}) %reduce-scatter.10.cloned.1.call-update) | async-done | bytes 524304 | tf_op jit(solution)/shard_map/reduce_scatter | solution.py:168
  962.1 182.5 %reduce-scatter.8.cloned.1.call-done = bf16[128,2048]{1,0:T(8,128)(2,1)} async-done(((bf16[2048,2048]{1,0:T(8,128)(2,1)}), bf16[128,2048]{1,0:T(8,128)(2,1)}) %reduce-scatter.8.cloned.1.call-update) | async-done | bytes 524304 | tf_op jit(solution)/shard_map/reduce_scatter | solution.py:168
  1228.7 8.6 add_bitcast_fusion
  1242.4 9.9 add_bitcast_fusion.2
  1252.3 9.6 add_bitcast_fusion.1
  1266.8 56.4 %reduce-scatter.16.cloned.1.call-done = bf16[128,256]{1,0:T(8,128)(2,1)} async-done(((bf16[2048,256]{1,0:T(8,128)(2,1)}), bf16[128,256]{1,0:T(8,128)(2,1)}) %reduce-scatter.16.cloned.1.call-update) | async-done | bytes 65552 | tf_op jit(solution)/shard_map/reduce_scatter | solution.py:55
  1324.7 49.6 %all-reduce = (f32[2048]{0:T(1024)}, f32[2048]{0:T(1024)}, f32[128]{0:T(128)}, f32[128]{0:T(128)}) all-reduce(f32[2048]{0:T(1024)S(1)} %get-tuple-element.71, f32[2048]{0:T(1024)S(1)} %get-tuple-element.70, f32[128]{0:T(128)S(1)} %bitcast_reduce_fusion, f32[128]{0:T(128)S(1)} %bitcast_reduce_fusion.1), channel_id=1, replica_groups=mesh['gx'=16,'gy'=2] {'gx','gy'}, use_global_device_ids=true, to_apply=%region_24.25 | all-reduce | flops 4352 | bytes 34816 | tf_op jit(solution)/shard_map/psum | solution.py:381
  1374.3 126.3 %reduce-scatter.18.cloned.1.call-done = bf16[128,2048]{1,0:T(8,128)(2,1)} async-done(((bf16[2048,2048]{1,0:T(8,128)(2,1)}), bf16[128,2048]{1,0:T(8,128)(2,1)}) %reduce-scatter.18.cloned.1.call-update) | async-done | bytes 524304 | tf_op jit(solution)/shard_map/reduce_scatter | solution.py:55
  1502.7 180.3 %reduce-scatter.12.cloned.1.call-done = bf16[128,2048]{1,0:T(8,128)(2,1)} async-done(((bf16[2048,2048]{1,0:T(8,128)(2,1)}), bf16[128,2048]{1,0:T(8,128)(2,1)}) %reduce-scatter.12.cloned.1.call-update) | async-done | bytes 524304 | tf_op jit(solution)/shard_map/reduce_scatter | solution.py:55
  1685.1 79.0 %reduce-scatter.20.cloned.1.call-done = f32[128,16]{0,1:T(8,128)} async-done(((f32[2048,16]{0,1:T(8,128)}), f32[128,16]{0,1:T(8,128)}) %reduce-scatter.20.cloned.1.call-update) | async-done | bytes 8208 | tf_op jit(solution)/shard_map/reduce_scatter | solution.py:378
  (308 shorter events, 219.2 us)
Async XLA Ops:
  7.2 61.6 %all-gather.9.cloned.1.call-start = ((), (), s32[]{:S(2)}) async-start(), calls=%async_computation.9 | async-start | bytes 1114112 | tf_op jit(solution)/shard_map/all_gather | solution.py:240
  8.0 117.7 %all-gather.7.cloned.1.call-start = ((), (), s32[]{:S(2)}) async-start(), calls=%async_computation.8 | async-start | bytes 1114112 | tf_op jit(solution)/shard_map/all_gather | solution.py:241
  8.7 231.4 %all-gather.11.cloned.1.call-start = ((), (), s32[]{:S(2)}) async-start(), calls=%async_computation.10 | async-start | bytes 8912896 | tf_op jit(solution)/shard_map/all_gather | solution.py:239
  9.4 344.4 %all-gather.13.cloned.1.call-start = ((), (), s32[]{:S(2)}) async-start(), calls=%async_computation.11 | async-start | bytes 8912896 | tf_op jit(solution)/shard_map/all_gather | solution.py:242
  10.0 472.9 %all-gather.15.cloned.1.call-start = ((), (), s32[]{:S(2)}) async-start(), calls=%async_computation.12 | async-start | bytes 8912896 | tf_op jit(solution)/shard_map/all_gather | solution.py:154
  361.2 4.5 collective-permute-start
  371.8 225.4 %all-gather.17.cloned.1.call-start = ((), (), s32[]{:S(2)}) async-start(), calls=%async_computation.14 | async-start | bytes 8912896 | tf_op jit(solution)/shard_map/all_gather | solution.py:154
  482.9 124.7 %collective-permute-start.2 = (bf16[2048,2048]{1,0:T(8,128)(2,1)}, bf16[2048,2048]{1,0:T(8,128)(2,1)}, u32[]{:S(2)}, u32[]{:S(2)}) collective-permute-start(bf16[2048,2048]{1,0:T(8,128)(2,1)} %all-gather.15.cloned.1.call-done), channel_id=1, source_target_pairs={{0,1},{1,0},{2,3},{3,2},{4,5},{5,4},{6,7},{7,6},{8,9},{9,8},{10,11... | collective-permute-start | bytes 25165832 | tf_op jit(solution)/shard_map/ppermute | solution.py:140
  597.2 24.9 %collective-permute-start.5 = (bf16[2048,2048]{1,0:T(8,128)(2,1)}, bf16[2048,2048]{1,0:T(8,128)(2,1)}, u32[]{:S(2)}, u32[]{:S(2)}) collective-permute-start(bf16[2048,2048]{1,0:T(8,128)(2,1)} %all-gather.17.cloned.1.call-done), channel_id=1, source_target_pairs={{0,1},{1,0},{2,3},{3,2},{4,5},{5,4},{6,7},{7,6},{8,9},{9,8},{10,11... | collective-permute-start | bytes 25165832 | tf_op jit(solution)/shard_map/ppermute | solution.py:140
  632.1 9.4 collective-permute-start.6
  642.1 45.2 %all-to-all-start = ((f32[16,1,128]{2,1,0:T(1,128)}), f32[16,1,128]{2,1,0:T(1,128)S(1)}, u32[]{:S(2)}, u32[]{:S(2)}) async-start(f32[16,1,128]{2,1,0:T(1,128)} %bitcast.17), calls=%async_computation.1 | async-start | bytes 16384 | tf_op jit(solution)/shard_map/all_to_all | solution.py:204
  645.9 316.2 %reduce-scatter.10.cloned.1.call-start = ((), (), s32[]{:S(2)}) async-start(), calls=%async_computation.15 | async-start | bytes 8912896 | tf_op jit(solution)/shard_map/reduce_scatter | solution.py:168
  687.2 1.6 collective-permute-start.7
  751.2 14.5 collective-permute-start.8
  786.2 358.4 %reduce-scatter.8.cloned.1.call-start = ((), (), s32[]{:S(2)}) async-start(), calls=%async_computation.13 | async-start | bytes 8912896 | tf_op jit(solution)/shard_map/reduce_scatter | solution.py:168
  794.7 13.4 collective-permute-start.3
  815.1 450.2 %reduce-scatter.14.cloned.1.call-start = ((), (), s32[]{:S(2)}) async-start(), calls=%async_computation.17 | async-start | bytes 1114112 | tf_op jit(solution)/shard_map/reduce_scatter | solution.py:55
  962.1 182.6 %collective-permute-start.9 = (bf16[128,2048]{1,0:T(8,128)(2,1)}, bf16[128,2048]{1,0:T(8,128)(2,1)S(1)}, u32[]{:S(2)}, u32[]{:S(2)}) collective-permute-start(bf16[128,2048]{1,0:T(8,128)(2,1)} %reduce-scatter.10.cloned.1.call-done), channel_id=1, source_target_pairs={{0,1},{1,0},{2,3},{3,2},{4,5},{5,4},{6,7},{7,6},{8,9},{9,8},{10,11... | collective-permute-start | bytes 1572872 | tf_op jit(solution)/shard_map/ppermute | solution.py:140
  1144.6 2.9 collective-permute-start.4
  1166.4 156.8 %reduce-scatter.16.cloned.1.call-start = ((), (), s32[]{:S(2)}) async-start(), calls=%async_computation.18 | async-start | bytes 1114112 | tf_op jit(solution)/shard_map/reduce_scatter | solution.py:55
  1174.8 325.8 %reduce-scatter.18.cloned.1.call-start = ((), (), s32[]{:S(2)}) async-start(), calls=%async_computation.19 | async-start | bytes 8912896 | tf_op jit(solution)/shard_map/reduce_scatter | solution.py:55
  1182.2 500.8 %reduce-scatter.12.cloned.1.call-start = ((), (), s32[]{:S(2)}) async-start(), calls=%async_computation.16 | async-start | bytes 8912896 | tf_op jit(solution)/shard_map/reduce_scatter | solution.py:55
  1208.1 556.0 %reduce-scatter.20.cloned.1.call-start = ((), (), s32[]{:S(2)}) async-start(), calls=%async_computation.20 | async-start | bytes 139264 | tf_op jit(solution)/shard_map/reduce_scatter | solution.py:378
  1241.5 20.5 %collective-permute-start.10 = (f32[256,2048]{1,0:T(8,128)S(1)}, f32[256,2048]{1,0:T(8,128)S(1)}, u32[]{:S(2)}, u32[]{:S(2)}) collective-permute-start(f32[256,2048]{1,0:T(8,128)S(1)} %convolution_add_fusion), channel_id=1, source_target_pairs={{0,1},{1,0},{2,3},{3,2},{4,5},{5,4},{6,7},{7,6},{8,9},{9,8},{10,11... | collective-permute-start | bytes 6291464 | tf_op jit(solution)/shard_map/ppermute | solution.py:140
  (82 other events, 3268.6 us)
Sparse Core Ops, SparseCore 0:
  10.8 57.9 all-gather.8
  71.6 54.0 all-gather.6
  128.5 111.6 all-gather.10
  242.8 111.0 all-gather.12
  371.9 111.0 all-gather.14
  486.1 111.0 all-gather.16
  786.3 175.7 reduce-scatter.9
  964.4 180.2 reduce-scatter.7
  1166.5 80.0 reduce-scatter.13
  1248.8 74.3 reduce-scatter.15
  1325.5 175.0 reduce-scatter.17
  1502.7 180.2 reduce-scatter.11
  1685.8 78.2 reduce-scatter.19

commit v2 on v1

--- a/solution.py
+++ b/solution.py
@@ -1,13 +1,17 @@
+import functools
 import math
 
 import jax
 import jax.numpy as jnp
 from jax import lax
+from jax.experimental import pallas as pl
+from jax.experimental.pallas import tpu as pltpu
 from jax.sharding import PartitionSpec as P
 
 QUERY_HEADS = 32
 KEY_VALUE_HEADS = 4
 HEAD_DIM = 128
+LANES = 128
 TOP = 8
 
 
@@ -51,9 +55,578 @@
     )
 
 
-def scatter_sum(term):
-    low = lax.psum_scatter(term.astype(jnp.bfloat16), "gx", scatter_dimension=0, tiled=True)
-    return low.astype(jnp.float32)
+MESH = pl.DeviceIdType.MESH
+LEVELS = 4
+PLANE = 4
+
+
+def cut_rows(rows):
+    near, far = 3 * rows // 4, rows // 4
+    return (
+        (0, near),
+        ((0, near // 2), (near // 2, near // 2)),
+        (near, far),
+        ((near, far // 2), (near + far // 2, far // 2)),
+    )
+
+
+def neighbours():
+    me, core = lax.axis_index("gx"), lax.axis_index("gy")
+    level = me // PLANE
+    x_side = me + 1 - 2 * (me % 2)
+    y_side = me + 2 - 4 * ((me // 2) % 2)
+    return me, core, level, x_side, y_side
+
+
+def greet(level, targets, with_core, me, core):
+    barrier = pltpu.get_barrier_semaphore()
+
+    def hello(device):
+        pl.semaphore_signal(barrier, inc=1, device_id=device, device_id_type=MESH)
+
+    for target in targets:
+        hello((target, core))
+    if with_core:
+        hello((me, 1 - core))
+
+    @pl.when(level > 0)
+    def _():
+        hello((me - PLANE, core))
+
+    @pl.when(level < LEVELS - 1)
+    def _():
+        hello((me + PLANE, core))
+
+    inner = jnp.where(level > 0, 1, 0) + jnp.where(level < LEVELS - 1, 1, 0)
+    pl.semaphore_wait(barrier, len(targets) + int(with_core) + inner)
+
+
+def when(condition, action):
+    if condition is None:
+        action()
+    else:
+        pl.when(condition)(action)
+
+
+def gather_kernel(count, paired, *refs):
+    ins, outs = refs[:count], refs[count : 2 * count]
+    pairs = refs[2 * count : 3 * count] if paired else ()
+    send_sem, recv_sem, local_sem = refs[-5:-2] if paired else refs[-3:]
+    if paired:
+        pair_send, pair_recv = refs[-2:]
+    me, core, level, x_side, y_side = neighbours()
+    whole_a, half_a, whole_b, half_b = cut_rows(ins[0].shape[0])
+    greet(level, (x_side, y_side), paired, me, core)
+    has_up, has_down = level < LEVELS - 1, level > 0
+    up, down = (me + PLANE, core), (me - PLANE, core)
+    to_x, to_y = (x_side, core), (y_side, core)
+    sent, mirrored = [], []
+
+    def place(array, first, number, span):
+        return array.at[pl.ds(first, number), pl.ds(*span)]
+
+    def send(condition, k, slot, source, first, number, span, target):
+        def copy():
+            here = ins[k].at[pl.ds(*span)] if source == "own" else place(outs[k], first, number, span)
+            there = outs[k].at[first, pl.ds(*span)] if source == "own" else place(outs[k], first, number, span)
+            return pltpu.make_async_remote_copy(
+                here, there, send_sem.at[k, slot], recv_sem.at[k, slot], device_id=target, device_id_type=MESH
+            )
+
+        when(condition, lambda: copy().start())
+        sent.append((condition, copy))
+
+    def mirror(condition, k, first, number, span):
+        if not paired:
+            return
+        slot = len(mirrored)
+
+        def copy():
+            here = place(outs[k], first, number, span)
+            return pltpu.make_async_remote_copy(
+                here,
+                place(pairs[k], first, number, span),
+                pair_send.at[slot],
+                pair_recv.at[slot],
+                device_id=(me, 1 - core),
+                device_id_type=MESH,
+            )
+
+        when(condition, lambda: copy().start())
+        mirrored.append((condition, copy))
+
+    def arrive(condition, k, slot, first, number, span):
+        def wait():
+            pltpu.make_async_remote_copy(
+                place(outs[k], first, number, span),
+                place(outs[k], first, number, span),
+                send_sem.at[k, slot],
+                recv_sem.at[k, slot],
+                device_id=to_x,
+                device_id_type=MESH,
+            ).wait_recv()
+
+        when(condition, wait)
+        mirror(condition, k, first, number, span)
+
+    def slot_of(group, index):
+        return 6 + 7 * group + index
+
+    last = 6 + 28
+    everyone = range(count)
+    for k in everyone:
+        pltpu.make_async_copy(ins[k], outs[k].at[me], local_sem.at[k]).start()
+        send(None, k, last, "own", me, 1, whole_b, to_x)
+        send(None, k, last + 1, "own", me, 1, whole_b, to_y)
+        send(has_up, k, 0, "own", me, 1, whole_a, up)
+        send(has_down, k, 3, "own", me, 1, whole_a, down)
+        send(None, k, slot_of(0, 0), "own", me, 1, whole_a, to_x)
+        send(None, k, slot_of(1, 0), "own", me, 1, whole_a, to_y)
+    diagonal = x_side + y_side - me
+    for k in everyone:
+        arrive(None, k, last, x_side, 1, whole_b)
+        send(None, k, last + 3, "out", x_side, 1, half_b[1], to_y)
+        arrive(None, k, last + 1, y_side, 1, whole_b)
+        send(None, k, last + 2, "out", y_side, 1, half_b[0], to_x)
+    for k in everyone:
+        pltpu.make_async_copy(ins[k], outs[k].at[me], local_sem.at[k]).wait()
+        mirror(None, k, me, 1, (0, ins[k].shape[0]))
+        arrive(None, k, last + 2, diagonal, 1, half_b[0])
+        arrive(None, k, last + 3, diagonal, 1, half_b[1])
+        send(has_up, k, last + 4, "out", PLANE * level, PLANE, whole_b, up)
+        send(has_down, k, last + 7, "out", PLANE * level, PLANE, whole_b, down)
+
+    def round_members(step):
+        if step == 0:
+            return [(None, 0, 0)]
+        return [(level >= step, step, -step), (level + step < LEVELS, 3 + step, step)]
+
+    def cross(k, step):
+        for condition, index, distance in round_members(step):
+            first = x_side + PLANE * distance
+            arrive(condition, k, slot_of(0, index), first, 1, whole_a)
+            send(condition, k, slot_of(3, index), "out", first, 1, half_a[1], to_y)
+            first = y_side + PLANE * distance
+            arrive(condition, k, slot_of(1, index), first, 1, whole_a)
+            send(condition, k, slot_of(2, index), "out", first, 1, half_a[0], to_x)
+
+    for step in range(1, LEVELS):
+        for k in everyone:
+            for condition, index, distance in round_members(step):
+                first = me + PLANE * distance
+                rising = distance < 0
+                arrive(condition, k, step - 1 if rising else 2 + step, first, 1, whole_a)
+                if step < LEVELS - 1:
+                    onward = condition & (has_up if rising else has_down)
+                    send(onward, k, step if rising else 3 + step, "out", first, 1, whole_a, up if rising else down)
+                send(condition, k, slot_of(0, index), "out", first, 1, whole_a, to_x)
+                send(condition, k, slot_of(1, index), "out", first, 1, whole_a, to_y)
+            cross(k, step - 1)
+            for condition, index, distance in round_members(step):
+                first = PLANE * (level + distance)
+                rising = distance < 0
+                arrive(condition, k, last + (3 if rising else 6) + step, first, PLANE, whole_b)
+                if step < LEVELS - 1:
+                    onward = condition & (has_up if rising else has_down)
+                    slot = last + (4 if rising else 7) + step
+                    send(onward, k, slot, "out", first, PLANE, whole_b, up if rising else down)
+    for k in everyone:
+        cross(k, LEVELS - 1)
+    for k in everyone:
+        for step in range(LEVELS):
+            for condition, index, distance in round_members(step):
+                first = diagonal + PLANE * distance
+                arrive(condition, k, slot_of(2, index), first, 1, half_a[0])
+                arrive(condition, k, slot_of(3, index), first, 1, half_a[1])
+    for condition, copy in sent:
+        when(condition, lambda copy=copy: copy().wait_send())
+    for condition, copy in mirrored:
+        when(condition, lambda copy=copy: copy().wait())
+
+
+GATHER_SLOTS = 6 + 28 + 10
+
+
+def gather_blocks(arrays, collective_id, paired=False):
+    count, blocks = len(arrays), lax.axis_size("gx")
+    shapes = [jax.ShapeDtypeStruct((blocks, *a.shape), a.dtype) for a in arrays]
+    scratch = [
+        pltpu.SemaphoreType.DMA((count, GATHER_SLOTS)),
+        pltpu.SemaphoreType.DMA((count, GATHER_SLOTS)),
+        pltpu.SemaphoreType.DMA((count,)),
+    ]
+    if paired:
+        scratch += [pltpu.SemaphoreType.DMA((count * (GATHER_SLOTS + 1),))] * 2
+    return pl.pallas_call(
+        functools.partial(gather_kernel, count, paired),
+        out_shape=shapes * (2 if paired else 1),
+        in_specs=[pl.BlockSpec(memory_space=pl.ANY)] * count,
+        out_specs=[pl.BlockSpec(memory_space=pl.ANY)] * (count * (2 if paired else 1)),
+        scratch_shapes=scratch,
+        compiler_params=pltpu.CompilerParams(collective_id=collective_id, has_side_effects=True),
+    )(*arrays)
+
+
+def scatter_kernel(count, paired, *refs):
+    n_in = 2 * count if paired else count
+    ins, aways, outs = refs[:count], refs[count:n_in], refs[n_in : n_in + count]
+    held = refs[n_in + count :]
+    per = 8 + int(paired)
+    parts = [held[per * k : per * (k + 1)] for k in range(count)]
+    rest = held[per * count :]
+    send_sem, recv_sem, chain_send, chain_recv, local_sem = rest[:5]
+    me, core, level, x_side, y_side = neighbours()
+    rows = ins[0].shape[1]
+    whole_a, half_a, whole_b, half_b = cut_rows(rows)
+    greet(level, (x_side, y_side), paired, me, core)
+    up, down = (me + PLANE, core), (me - PLANE, core)
+    to_x, to_y = (x_side, core), (y_side, core)
+    x_at, y_at, own_at = x_side % PLANE, y_side % PLANE, me % PLANE
+    diagonal_at = (x_side + y_side - me) % PLANE
+    forward = jnp.where(level < 2, 1, 0)
+    order = [
+        3 * forward,
+        2 * forward + (1 - forward),
+        level + 1 - 2 * (level % 2),
+        level,
+    ]
+    sent = []
+
+    def send(condition, source, target_ref, ssem, rsem, target):
+        def copy():
+            return pltpu.make_async_remote_copy(
+                source, target_ref, ssem, rsem, device_id=target, device_id_type=MESH
+            )
+
+        when(condition, lambda: copy().start())
+        sent.append((condition, copy))
+
+    def arrive(condition, target_ref, rsem):
+        def wait():
+            pltpu.make_async_remote_copy(
+                target_ref, target_ref, rsem, rsem, device_id=to_x, device_id_type=MESH
+            ).wait_recv()
+
+        when(condition, wait)
+
+    def add(condition, height, target, *terms, step=16):
+        def run():
+            def body(i, carry):
+                at = pl.multiple_of(i * step, step)
+                total = target(at, step)[...].astype(jnp.float32)
+                for term in terms:
+                    total = total + term(at, step)[...].astype(jnp.float32)
+                target(at, step)[...] = total.astype(jnp.bfloat16)
+                return carry
+
+            lax.fori_loop(0, height // step, body, 0)
+
+        when(condition, run)
+
+    def rows_of(ref, *index, start=0):
+        return lambda at, step: ref.at[(*index, pl.ds(start + at, step))]
+
+    def load(k, to_level):
+        return pltpu.make_async_copy(
+            ins[k].at[pl.ds(PLANE * to_level, PLANE)],
+            parts[k][0].at[pl.ds(PLANE * to_level, PLANE)],
+            local_sem.at[k, to_level],
+        )
+
+    def hand(k, to_level):
+        pair_send, pair_recv = rest[5:7]
+        return pltpu.make_async_remote_copy(
+            aways[k].at[pl.ds(PLANE * to_level, PLANE)],
+            parts[k][8].at[pl.ds(PLANE * to_level, PLANE)],
+            pair_send.at[k, to_level],
+            pair_recv.at[k, to_level],
+            device_id=(me, 1 - core),
+            device_id_type=MESH,
+        )
+
+    everyone = range(count)
+    for to_level in order:
+        for k in everyone:
+            load(k, to_level).start()
+            if paired:
+                hand(k, to_level).start()
+
+    def chain(k, which, to_level, block, slots, spread):
+        rising, falling = to_level > level, to_level < level
+        begins = (rising & (level == 0)) | (falling & (level == LEVELS - 1))
+        middle = (rising | falling) & jnp.logical_not(begins)
+        arrive(middle, slots.at[to_level], chain_recv.at[k, which, to_level])
+        spread(middle, to_level)
+        send(rising, block, slots.at[to_level], chain_send.at[k, which, to_level], chain_recv.at[k, which, to_level], up)
+        at = jnp.where(to_level == level - 1, LEVELS, to_level)
+        send(falling, block, slots.at[at], chain_send.at[k, which, to_level], chain_recv.at[k, which, at], down)
+
+    for turn, to_level in enumerate(order):
+        first = PLANE * to_level
+        for k in everyone:
+            mine, half_y, half_x, full_x, full_y, slots_a, slots_b, side_b = parts[k][:8]
+            load(k, to_level).wait()
+            if paired:
+                hand(k, to_level).wait()
+                for column in range(PLANE):
+                    add(None, rows, rows_of(mine, first + column), rows_of(parts[k][8], first + column))
+            height = half_a[0][1]
+            sems = [(send_sem.at[k, 6 * turn + i], recv_sem.at[k, 6 * turn + i]) for i in range(6)]
+            send(None, mine.at[first + diagonal_at, pl.ds(*half_a[0])], half_y.at[turn], *sems[0], to_y)
+            send(None, mine.at[first + diagonal_at, pl.ds(*half_a[1])], half_x.at[turn], *sems[1], to_x)
+            send(None, mine.at[first + x_at, pl.ds(*half_a[1])], full_x.at[turn, pl.ds(*half_a[1])], *sems[2], to_x)
+            send(None, mine.at[first + y_at, pl.ds(*half_a[0])], full_y.at[turn, pl.ds(*half_a[0])], *sems[3], to_y)
+
+            def spread_b(condition, to_level, mine=mine, slots_b=slots_b, first=first):
+                for column in range(PLANE):
+                    add(
+                        condition,
+                        whole_b[1],
+                        rows_of(mine, first + column, start=whole_b[0]),
+                        rows_of(slots_b, to_level, column),
+                    )
+
+            chain(k, 1, to_level, mine.at[pl.ds(first, PLANE), pl.ds(*whole_b)], slots_b, spread_b)
+            arrive(None, half_y.at[turn], recv_sem.at[k, 6 * turn])
+            add(None, height, rows_of(mine, first + x_at), rows_of(half_y, turn))
+            send(None, mine.at[first + x_at, pl.ds(*half_a[0])], full_x.at[turn, pl.ds(*half_a[0])], *sems[4], to_x)
+            arrive(None, half_x.at[turn], recv_sem.at[k, 6 * turn + 1])
+            add(None, height, rows_of(mine, first + y_at, start=height), rows_of(half_x, turn))
+            send(None, mine.at[first + y_at, pl.ds(*half_a[1])], full_y.at[turn, pl.ds(*half_a[1])], *sems[5], to_y)
+        if turn:
+            finish_plane(turn - 1)
+        else:
+
+            def finish_plane(turn):
+                to_level = order[turn]
+                first = PLANE * to_level
+                for k in everyone:
+                    mine, half_y, half_x, full_x, full_y, slots_a, slots_b, side_b = parts[k][:8]
+                    arrive(None, full_x.at[turn, pl.ds(*half_a[1])], recv_sem.at[k, 6 * turn + 2])
+                    arrive(None, full_y.at[turn, pl.ds(*half_a[0])], recv_sem.at[k, 6 * turn + 3])
+                    arrive(None, full_x.at[turn, pl.ds(*half_a[0])], recv_sem.at[k, 6 * turn + 4])
+                    arrive(None, full_y.at[turn, pl.ds(*half_a[1])], recv_sem.at[k, 6 * turn + 5])
+                    if turn == LEVELS - 1:
+                        continue
+                    add(None, whole_a[1], rows_of(mine, first + own_at), rows_of(full_x, turn), rows_of(full_y, turn))
+
+                    def spread_a(condition, to_level, mine=mine, slots_a=slots_a, first=first):
+                        add(condition, whole_a[1], rows_of(mine, first + own_at), rows_of(slots_a, to_level))
+
+                    chain(k, 0, to_level, mine.at[first + own_at, pl.ds(*whole_a)], slots_a, spread_a)
+
+    first = PLANE * level
+    has_below, has_above = level > 0, level < LEVELS - 1
+    for k in everyone:
+        mine, half_y, half_x, full_x, full_y, slots_a, slots_b, side_b = parts[k][:8]
+        for condition, slot in ((has_below, level), (has_above, LEVELS)):
+            arrive(condition, slots_b.at[slot], chain_recv.at[k, 1, slot])
+            for column in range(PLANE):
+                add(
+                    condition,
+                    whole_b[1],
+                    rows_of(mine, first + column, start=whole_b[0]),
+                    rows_of(slots_b, slot, column),
+                )
+        sems = [(send_sem.at[k, 24 + i], recv_sem.at[k, 24 + i]) for i in range(4)]
+        short = half_b[0][1]
+        send(None, mine.at[first + diagonal_at, pl.ds(*half_b[0])], side_b.at[pl.ds(0, short)], *sems[0], to_y)
+        send(None, mine.at[first + diagonal_at, pl.ds(*half_b[1])], side_b.at[pl.ds(short, short)], *sems[1], to_x)
+    for k in everyone:
+        mine, half_y, half_x, full_x, full_y, slots_a, slots_b, side_b = parts[k][:8]
+        sems = [(send_sem.at[k, 24 + i], recv_sem.at[k, 24 + i]) for i in range(4)]
+        short = half_b[0][1]
+        arrive(None, side_b.at[pl.ds(0, short)], recv_sem.at[k, 24])
+        add(None, short, rows_of(mine, first + x_at, start=half_b[0][0]), rows_of(side_b))
+        send(None, mine.at[first + x_at, pl.ds(*whole_b)], side_b.at[pl.ds(2 * short, 2 * short)], *sems[2], to_x)
+        arrive(None, side_b.at[pl.ds(short, short)], recv_sem.at[k, 25])
+        add(None, short, rows_of(mine, first + y_at, start=half_b[1][0]), rows_of(side_b, start=short))
+        send(None, mine.at[first + y_at, pl.ds(*whole_b)], side_b.at[pl.ds(4 * short, 2 * short)], *sems[3], to_y)
+    finish_plane(LEVELS - 1)
+    base = core * rows if paired else 0
+    step = 16
+    for k in everyone:
+        mine, half_y, half_x, full_x, full_y, slots_a, slots_b, side_b = parts[k][:8]
+        out = outs[k]
+        for condition, slot in ((has_below, level), (has_above, LEVELS)):
+            arrive(condition, slots_a.at[slot], chain_recv.at[k, 0, slot])
+
+        def tail_a(i, carry, out=out, mine=mine, slots_a=slots_a, full_x=full_x, full_y=full_y):
+            at = pl.multiple_of(i * step, step)
+            span = pl.ds(at, step)
+            turn = LEVELS - 1
+            total = mine[first + own_at, span].astype(jnp.float32)
+            total = total + full_x[turn, span].astype(jnp.float32) + full_y[turn, span].astype(jnp.float32)
+            out[pl.ds(pl.multiple_of(base + at, step), step)] = total
+            return carry
+
+        lax.fori_loop(0, whole_a[1] // step, tail_a, 0)
+        for condition, slot in ((has_below, level), (has_above, LEVELS)):
+
+            def more(condition=condition, slot=slot, out=out, slots_a=slots_a):
+                def body(i, carry):
+                    at = pl.multiple_of(i * step, step)
+                    span = pl.ds(pl.multiple_of(base + at, step), step)
+                    out[span] = out[span] + slots_a[slot, pl.ds(at, step)].astype(jnp.float32)
+                    return carry
+
+                lax.fori_loop(0, whole_a[1] // step, body, 0)
+
+            when(condition, more)
+        short = half_b[0][1]
+        arrive(None, side_b.at[pl.ds(2 * short, 2 * short)], recv_sem.at[k, 26])
+        arrive(None, side_b.at[pl.ds(4 * short, 2 * short)], recv_sem.at[k, 27])
+
+        def tail_b(i, carry, out=out, mine=mine, side_b=side_b):
+            at = pl.multiple_of(i * step, step)
+            total = mine[first + own_at, pl.ds(whole_b[0] + at, step)].astype(jnp.float32)
+            total = total + side_b[pl.ds(2 * short + at, step)].astype(jnp.float32)
+            total = total + side_b[pl.ds(4 * short + at, step)].astype(jnp.float32)
+            out[pl.ds(pl.multiple_of(base + whole_b[0] + at, step), step)] = total
+            return carry
+
+        lax.fori_loop(0, whole_b[1] // step, tail_b, 0)
+        if paired:
+            ready_send, ready_recv = rest[7:9]
+            span = pl.ds(pl.multiple_of(base, rows), rows)
+            pltpu.make_async_remote_copy(
+                out.at[span],
+                out.at[span],
+                ready_send.at[k],
+                ready_recv.at[k],
+                device_id=(me, 1 - core),
+                device_id_type=MESH,
+            ).start()
+    for k in everyone:
+        if paired:
+            ready_send, ready_recv = rest[7:9]
+            there = pl.ds(pl.multiple_of((1 - core) * rows, rows), rows)
+            copy = pltpu.make_async_remote_copy(
+                outs[k].at[there],
+                outs[k].at[there],
+                ready_send.at[k],
+                ready_recv.at[k],
+                device_id=(me, 1 - core),
+                device_id_type=MESH,
+            )
+            copy.wait_send()
+            copy.wait_recv()
+    for condition, copy in sent:
+        when(condition, lambda copy=copy: copy().wait_send())
+
+
+def scatter_sums(arrays, collective_id, away=()):
+    count, paired = len(arrays), bool(away)
+    low = jnp.bfloat16
+    scratch = []
+    for a in arrays:
+        blocks, rows, width = a.shape
+        near, far = 3 * rows // 4, rows // 4
+        scratch += [
+            pltpu.VMEM((blocks, rows, width), low),
+            pltpu.VMEM((LEVELS, near // 2, width), low),
+            pltpu.VMEM((LEVELS, near // 2, width), low),
+            pltpu.VMEM((LEVELS, near, width), low),
+            pltpu.VMEM((LEVELS, near, width), low),
+            pltpu.VMEM((LEVELS + 1, near, width), low),
+            pltpu.VMEM((LEVELS + 1, PLANE, far, width), low),
+            pltpu.VMEM((3 * far, width), low),
+        ]
+        if paired:
+            scratch += [pltpu.VMEM((blocks, rows, width), low)]
+    dma = pltpu.SemaphoreType.DMA
+    scratch += [dma((count, 28)), dma((count, 28)), dma((count, 2, 5)), dma((count, 2, 5)), dma((count, LEVELS))]
+    if paired:
+        scratch += [dma((count, LEVELS)), dma((count, LEVELS)), dma((count,)), dma((count,))]
+    return pl.pallas_call(
+        functools.partial(scatter_kernel, count, paired),
+        out_shape=[
+            jax.ShapeDtypeStruct(((2 if paired else 1) * a.shape[1], a.shape[2]), jnp.float32) for a in arrays
+        ],
+        in_specs=[pl.BlockSpec(memory_space=pl.ANY)] * (count * (2 if paired else 1)),
+        out_specs=[pl.BlockSpec(memory_space=pltpu.VMEM)] * count,
+        scratch_shapes=scratch,
+        compiler_params=pltpu.CompilerParams(
+            collective_id=collective_id, has_side_effects=True, vmem_limit_bytes=60 * 1024 * 1024
+        ),
+    )(*arrays, *away)
+
+
+def total_kernel(in_ref, out_ref, slots, send_sem, recv_sem):
+    me, core, level, x_side, y_side = neighbours()
+    near = me + PLANE - 2 * PLANE * (level % 2)
+    far = me + 2 * PLANE - 4 * PLANE * (level // 2)
+    partners = ((me, 1 - core), (x_side, core), (y_side, core), (near, core), (far, core))
+    barrier = pltpu.get_barrier_semaphore()
+    for partner in partners:
+        pl.semaphore_signal(barrier, inc=1, device_id=partner, device_id_type=MESH)
+    pl.semaphore_wait(barrier, len(partners))
+    slots[0] = in_ref[...]
+    for turn, partner in enumerate(partners):
+        copy = pltpu.make_async_remote_copy(
+            slots.at[2 * turn],
+            slots.at[2 * turn + 1],
+            send_sem.at[turn],
+            recv_sem.at[turn],
+            device_id=partner,
+            device_id_type=MESH,
+        )
+        copy.start()
+        copy.wait_recv()
+        slots[2 * turn + 2] = slots[2 * turn] + slots[2 * turn + 1]
+        copy.wait_send()
+    out_ref[...] = slots[2 * len(partners)]
+
+
+def total_everywhere(rows, collective_id):
+    return pl.pallas_call(
+        total_kernel,
+        out_shape=jax.ShapeDtypeStruct(rows.shape, rows.dtype),
+        in_specs=[pl.BlockSpec(memory_space=pltpu.VMEM)],
+        out_specs=pl.BlockSpec(memory_space=pltpu.VMEM),
+        scratch_shapes=[
+            pltpu.VMEM((11, *rows.shape), rows.dtype),
+            pltpu.SemaphoreType.DMA((5,)),
+            pltpu.SemaphoreType.DMA((5,)),
+        ],
+        compiler_params=pltpu.CompilerParams(collective_id=collective_id, has_side_effects=True),
+    )(rows)
+
+
+def kernels_fit():
+    return lax.axis_size("gx") == LEVELS * PLANE and lax.axis_size("gy") == 2
+
+
+def gather_rows(arrays):
+    if kernels_fit():
+        return [rows.reshape(-1, rows.shape[-1]) for rows in gather_blocks(arrays, 1)]
+    return [lax.all_gather(rows, "gx", axis=0, tiled=True) for rows in arrays]
+
+
+def scatter_rows(terms):
+    if kernels_fit():
+        blocks = lax.axis_size("gx")
+        return scatter_sums([term.astype(jnp.bfloat16).reshape(blocks, -1, term.shape[-1]) for term in terms], 2)
+    return [lax.psum_scatter(term, "gx", scatter_dimension=0, tiled=True) for term in terms]
+
+
+def total_of(vectors):
+    if not kernels_fit():
+        return lax.psum(vectors, ("gx", "gy"))
+    lengths = [vector.shape[0] // HEAD_DIM for vector in vectors]
+    rows = jnp.concatenate([vector.reshape(-1, HEAD_DIM) for vector in vectors], axis=0)
+    rows = jnp.pad(rows, ((0, -rows.shape[0] % 8), (0, 0)))
+    rows = total_everywhere(rows, 3)
+    sums, at = [], 0
+    for length in lengths:
+        sums.append(rows[at : at + length].reshape(-1))
+        at += length
+    return sums
+
+
+def two_parts(values):
+    high = values.astype(jnp.bfloat16)
+    return high, (values - high.astype(jnp.float32)).astype(jnp.bfloat16)
 
 
 def sparse_experts(normed_ffn, logits, route_hits, routes, cotangent, w_gate, w_up, w_down):
@@ -146,39 +719,30 @@
     half_rows = sequence_length // lax.axis_size("gy")
     my_core = lax.axis_index("gy")
     my_expert = lax.axis_index("gx")
+    experts_all = logits.shape[1]
 
     def own_half(rows):
         return lax.dynamic_slice_in_dim(rows, my_core * half_rows, half_rows, 0)
 
-    def to_experts(rows):
-        own_rows = lax.all_gather(own_half(rows), "gx", axis=0, tiled=True)
-        return (own_rows, swap_cores(own_rows))
-
-    def both_halves(own_rows):
-        other = swap_cores(own_rows)
-        return jnp.where(
-            my_core == 0,
-            jnp.concatenate([own_rows, other], axis=0),
-            jnp.concatenate([other, own_rows], axis=0),
-        )
-
-    def from_experts(partial_rows):
-        there = swap_cores(partial_rows(1).astype(jnp.bfloat16))
-        own_rows = (partial_rows(0) + there).astype(jnp.bfloat16)
-        summed = lax.psum_scatter(own_rows, "gx", scatter_dimension=0, tiled=True)
-        return both_halves(summed).astype(jnp.float32)
-
     def dot(left, right):
         return jnp.dot(left, right, preferred_element_type=jnp.float32)
 
     gate_exps = jnp.exp(jnp.where(jnp.any(route_hits, axis=1), logits, -1e30))
     gate_all = gate_exps / jnp.sum(gate_exps, axis=1, keepdims=True)
-    grad_sets = to_experts(cotangent)
-    row_sets = to_experts(normed_ffn)
-    gate_sets = to_experts(gate_all)
+    gate_lanes = jnp.pad(jnp.concatenate(two_parts(gate_all), axis=1), ((0, 0), (0, LANES - 2 * experts_all)))
+    row_lanes = jnp.concatenate([own_half(normed_ffn), own_half(gate_lanes)], axis=1)
+    gathered = gather_blocks([row_lanes, own_half(cotangent)], 4, paired=True)
+    gathered = [rows.reshape(-1, rows.shape[-1]) for rows in gathered]
+    row_sets = [gathered[part][:, :model_width] for part in (0, 2)]
+    gate_sets = [gathered[part][:, model_width:] for part in (0, 2)]
+    grad_sets = [gathered[1], gathered[3]]
+    lane = jnp.arange(LANES)
+    gate_pick = ((lane % experts_all == my_expert) & (lane < 2 * experts_all)).astype(jnp.bfloat16)
+    high_lane = (lane == 2 * experts_all * my_core + my_expert).astype(jnp.bfloat16)
+    low_lane = (lane == 2 * experts_all * my_core + experts_all + my_expert).astype(jnp.bfloat16)
     weighted, gate_terms, grad_gate_in, grad_up_in = [], [], [], []
     for part in range(2):
-        gate_rows = lax.dynamic_slice_in_dim(gate_sets[part], my_expert, 1, 1)
+        gate_rows = jnp.sum(gate_sets[part].astype(jnp.float32) * gate_pick, axis=1, keepdims=True)
         gate_in = dot(row_sets[part], w_gate)
         up_in = dot(row_sets[part], w_up)
         grad_hidden = contract(grad_sets[part], w_down, 1, 1)
@@ -192,17 +756,23 @@
             (grad_act * up_in * gate_sigmoid * (1.0 + gate_in * (1.0 - gate_sigmoid))).astype(jnp.bfloat16)
         )
         grad_up_in.append((grad_act * gate_swish).astype(jnp.bfloat16))
-    mixed_rows = from_experts(lambda part: dot(weighted[part], w_down))
-    grad_rows_sum = from_experts(
-        lambda part: contract(grad_gate_in[part], w_gate, 1, 1) + contract(grad_up_in[part], w_up, 1, 1)
-    )
+    def blocks_of(rows):
+        return rows.reshape(devices_gx, half_rows, rows.shape[-1])
+
+    mixed_parts, term_parts, back_parts = [], [], []
+    for part in range(2):
+        mixed_parts.append(blocks_of(dot(weighted[part], w_down).astype(jnp.bfloat16)))
+        high, low = two_parts(gate_terms[part])
+        term_parts.append(blocks_of(high[:, None] * high_lane + low[:, None] * low_lane))
+        grad_in = contract(grad_gate_in[part], w_gate, 1, 1) + contract(grad_up_in[part], w_up, 1, 1)
+        back_parts.append(blocks_of(grad_in.astype(jnp.bfloat16)))
+    mixed_rows, term_lanes = scatter_sums([mixed_parts[0], term_parts[0]], 5, [mixed_parts[1], term_parts[1]])
+    (grad_rows_sum,) = scatter_sums([back_parts[0]], 6, [back_parts[1]])
     down_term, gate_term, up_term = (
         contract(first[0], second[0], 0, 0) + contract(first[1], second[1], 0, 0)
         for first, second in ((weighted, grad_sets), (row_sets, grad_gate_in), (row_sets, grad_up_in))
     )
-    own_terms = gate_terms[0] + swap_cores(gate_terms[1])
-    back = lax.all_to_all(own_terms.reshape(devices_gx, half_rows), "gx", split_axis=0, concat_axis=0, tiled=True)
-    grad_gates = both_halves(back.T)
+    grad_gates = jnp.sum(term_lanes[:, : 4 * experts_all].reshape(sequence_length, 4, experts_all), axis=1)
     grad_logits = (
         gate_all * (grad_gates - jnp.sum(gate_all * grad_gates, axis=1, keepdims=True))
     ).astype(jnp.bfloat16)
@@ -235,29 +805,25 @@
     experts_all = router_weight.shape[1]
     query_group_count = QUERY_HEADS // KEY_VALUE_HEADS
     inv_root = 1.0 / math.sqrt(HEAD_DIM)
-    q_full, k_full, v_full, o_full, router_full = (
-        lax.all_gather(q_weight, "gx", axis=0, tiled=True),
-        lax.all_gather(key_matrix, "gx", axis=0, tiled=True),
-        lax.all_gather(value_matrix, "gx", axis=0, tiled=True),
-        lax.all_gather(out_weight, "gx", axis=0, tiled=True),
-        lax.all_gather(router_weight, "gx", axis=0, tiled=True),
-    )
-    heads_local = q_full.shape[1] // HEAD_DIM
-    kv_local = k_full.shape[1] // HEAD_DIM
+    router_lanes = jnp.pad(router_weight, ((0, 0), (0, LANES - experts_all)))
+    in_full, o_full = gather_rows(
+        [jnp.concatenate([q_weight, key_matrix, value_matrix, router_lanes], axis=1), out_weight]
+    )
+    q_width, kv_width = q_weight.shape[1], key_matrix.shape[1]
+    qkv_width = q_width + 2 * kv_width
+    qkv_full = in_full[:, :qkv_width]
+    router_full = in_full[:, qkv_width : qkv_width + experts_all]
+    heads_local = q_width // HEAD_DIM
+    kv_local = kv_width // HEAD_DIM
     inputs_f = tokens_in.astype(jnp.float32)
     scale_one = root_mean_scale(inputs_f)
     unit_one = inputs_f * scale_one
     normalized_input = (unit_one * attn_gain).astype(jnp.bfloat16)
-    query_unrotated = jnp.dot(normalized_input, q_full, preferred_element_type=jnp.float32).reshape(
-        sequence_length, heads_local, HEAD_DIM
-    )
-    key_unrotated = jnp.dot(normalized_input, k_full, preferred_element_type=jnp.float32).reshape(
-        sequence_length, kv_local, HEAD_DIM
-    )
+    qkv_rows = jnp.dot(normalized_input, qkv_full, preferred_element_type=jnp.float32)
+    query_unrotated = qkv_rows[:, :q_width].reshape(sequence_length, heads_local, HEAD_DIM)
+    key_unrotated = qkv_rows[:, q_width : q_width + kv_width].reshape(sequence_length, kv_local, HEAD_DIM)
     value_rows = (
-        jnp.dot(normalized_input, v_full, preferred_element_type=jnp.float32)
-        .astype(jnp.bfloat16)
-        .reshape(sequence_length, kv_local, HEAD_DIM)
+        qkv_rows[:, q_width + kv_width :].astype(jnp.bfloat16).reshape(sequence_length, kv_local, HEAD_DIM)
     )
     cosine, sine_table = rotary_tables(sequence_length, HEAD_DIM)
     q_scale = root_mean_scale(query_unrotated)
@@ -357,30 +923,23 @@
         .reshape(sequence_length, kv_local * HEAD_DIM)
     )
     grad_v_raw = grad_values.astype(jnp.bfloat16).reshape(sequence_length, kv_local * HEAD_DIM)
-    q_term = contract(normalized_input, grad_q_raw, 0, 0)
-    k_term = contract(normalized_input, grad_k_raw, 0, 0)
-    v_term = contract(normalized_input, grad_v_raw, 0, 0)
-    grad_normed_part = (
-        contract(grad_q_raw, q_full, 1, 1)
-        + contract(grad_k_raw, k_full, 1, 1)
-        + contract(grad_v_raw, v_full, 1, 1)
-    )
+    grad_qkv = jnp.concatenate([grad_q_raw, grad_k_raw, grad_v_raw], axis=1)
+    qkv_term = contract(normalized_input, grad_qkv, 0, 0)
+    grad_normed_part = contract(grad_qkv, qkv_full, 1, 1)
     grad_normed = grad_normed_part + swap_cores(grad_normed_part)
     attn_gain_term = jnp.sum(grad_normed * unit_one, axis=0)
     grad_input = (grad_residual + norm_back(grad_normed * attn_gain, unit_one, scale_one)).astype(
         jnp.bfloat16
     )
-    grad_q, grad_k, grad_v, grad_out, grad_router = (
-        scatter_sum(q_term),
-        scatter_sum(k_term),
-        scatter_sum(v_term),
-        scatter_sum(out_term),
-        lax.psum_scatter(router_term, "gx", scatter_dimension=0, tiled=True),
-    )
+    router_lanes = jnp.pad(router_term, ((0, 0), (0, LANES - experts_all)))
+    grad_in, grad_out, grad_router = scatter_rows([qkv_term, out_term, router_lanes])
+    grad_q = grad_in[:, :q_width]
+    grad_k = grad_in[:, q_width : q_width + kv_width]
+    grad_v = grad_in[:, q_width + kv_width :]
+    grad_router = grad_router[:, :experts_all]
     own_mask = (jnp.arange(model_width) // part_width == lax.axis_index("gy")).astype(jnp.float32)
-    gain_attn, gain_ffn, gain_query, gain_key = lax.psum(
-        (attn_gain_term * own_mask, ffn_gain_term * own_mask, q_gain_term, k_gain_term),
-        ("gx", "gy"),
+    gain_attn, gain_ffn, gain_query, gain_key = total_of(
+        (attn_gain_term * own_mask, ffn_gain_term * own_mask, q_gain_term, k_gain_term)
     )
     return (
         output,

time: 1780 us -> 981 us (0.55)
  waiting for transfers between devices: 1340 us -> 0.01 us
  Pallas kernels: 0 us -> 689 us
  blocking collectives: 127 us -> 0 us
    reduce_scatter x7 -> x0, waiting for transfers between devices: 771 us -> none  [the longest x4 363 us: scatter_sum(): lax.psum_scatter(term.astype(jnp.bfloat16), 'gx', scatter_dimension=0, ti...]
    pallas_call x0 -> x6, Pallas kernels: none -> 689 us  [the longest x3 358 us: scatter_sums(): pl.pallas_call(functools.partial(scatter_kernel, count, paired), out_shap...]
    all_gather x6 -> x0, waiting for transfers between devices: 542 us -> none  [the longest x2 223 us: to_experts(): own_rows = lax.all_gather(own_half(rows), 'gx', axis=0, tiled=True)]
    all_gather x2 -> x0, blocking collectives: 77.5 us -> none  [the longest x1 41.3 us: on_device(): lax.all_gather(router_weight, 'gx', axis=0, tiled=True)]
    psum x1 -> x0, blocking collectives: 49.6 us -> none  [on_device(): lax.psum((attn_gain_term * own_mask, ffn_gain_term * own_mask, q_gain_ter...]
    convert_element_type x7, other arithmetic: 21.9 us -> 2.48 us  [the longest x1 2.45 us: on_device(): grad_scores = (probs_again * (grad_probs - prob_inner)).astype(jnp.bfloat16)]
    ppermute x11 -> x2, waiting for transfers between devices: 18.9 us -> 0.01 us  [swap_cores(): return lax.ppermute(rows, 'gy', [(0, 1), (1, 0)])]
    dot_general x22 -> x18, matrix products: 140 us -> 129 us  [contract(): lax.dot_general(first_op, second_op, (((first_dim,), (second_dim,)), ((),...]
  transfers between devices with their start and end apart: 25 -> 2, of which waited for: 15 -> 0; matrix products, arithmetic and copies ran while one was open for 11% -> 3% of each run, Pallas kernels for 0% -> 19%
where the time goes in v2:
time: 981 us; the launch traced here: 971 us
  Pallas kernels  689 us (70%)
  matrix products  196 us (20%)
  local copies, waits for them, and re-layouts  44.5 us (5%)
  other arithmetic  39.8 us (4%)
    pallas_call x3, Pallas kernels, scatter_sums(): pl.pallas_call(functools.partial(scatter_kernel, count, paired), out_shap...  358 us
    pallas_call x2, Pallas kernels, gather_blocks(): pl.pallas_call(functools.partial(gather_kernel, count, paired), out_shape...  315 us
    dot_general x18, matrix products, contract(): lax.dot_general(first_op, second_op, (((first_dim,), (second_dim,)), ((),...  129 us
    dot_general x6, matrix products, dot(): return jnp.dot(left, right, preferred_element_type=jnp.float32)  44.1 us
    unnamed x166, local copies, waits for them, and re-layouts  20.8 us
  transfers between devices with their start and end apart: 2, of which 0 were waited for; matrix products, arithmetic and copies ran while one was open for 3% of the time, Pallas kernels for 19%

profile of v2, /device:TPU:0, one launch (start us, length us, event | category | flops | bytes accessed | tf_op | source)
XLA Modules:
  0.0 971.2 jit_solution(8328990990222038927)
XLA Ops:
  5.2 164.9 %shard_map.263 = (bf16[16,128,2688]{2,1,0:T(8,128)(2,1)}, bf16[16,128,2048]{2,1,0:T(8,128)(2,1)}) custom-call(bf16[128,2688]{1,0:T(8,128)(2,1)} %fusion.73.refs_0_, bf16[128,2048]{1,0:T(8,128)(2,1)} %refs_1_.1), custom_call_target="tpu_custom_call" | custom-call | tf_op jit(solution)/shard_map/pallas_call | solution.py:260
  211.8 150.2 %shard_map.264 = (bf16[16,128,2176]{2,1,0:T(8,128)(2,1)}, bf16[16,128,2048]{2,1,0:T(8,128)(2,1)}, bf16[16,128,2176]{2,1,0:T(8,128)(2,1)}, bf16[16,128,2048]{2,1,0:T(8,128)(2,1)}) custom-call(bf16[128,2176]{1,0:T(8,128)(2,1)} %pad_maximum_fusion.3.refs_0_, bf16[128,2048]{1,0:T(8,128)(2,1)} %constant_dynamic-slice_fusion.refs_1_), custom_call_target="tpu_custom_call" | custom-call | tf_op jit(solution)/shard_map/pallas_call | solution.py:260
  362.1 8.7 fusion.16
  376.7 8.5 fusion.51
  385.1 9.0 multiply_convert_fusion.3
  394.1 9.1 fusion.112
  403.2 6.8 convolution_convert_fusion.3
  410.0 8.5 fusion.48
  418.4 7.6 multiply_convert_fusion.1
  426.1 6.3 fusion.6
  432.4 8.4 fusion.58
  447.2 6.8 convolution_convert_fusion.2
  456.0 95.4 %shard_map.265 = (f32[256,2048]{1,0:T(8,128)}, f32[256,128]{1,0:T(8,128)}) custom-call(bf16[16,128,2048]{2,1,0:T(8,128)(2,1)} %bitcast.242, bf16[16,128,128]{2,1,0:T(8,128)(2,1)} %get-tuple-element.173.refs_1_, bf16[16,128,2048]{2,1,0:T(8,128)(2,1)} %bitcast.243, bf16[16,128,128]{2,1,0:T(8,128)(2,1)} %get-tuple-element.172.refs_3_), custom_call_target="tpu_custom_call" | custom-call | tf_op jit(solution)/shard_map/pallas_call | solution.py:541
  552.5 10.7 %add_convert_fusion = bf16[2048,2048]{1,0:T(8,128)(2,1)} fusion(f32[2048,2048]{1,0:T(8,128)} %fusion.58, bf16[2048,384]{0,1:T(8,128)(2,1)} %copy-done.21, bf16[1,2048,384]{2,1,0:T(8,128)(2,1)S(1)} %copy-done.18), kind=kOutput, calls=%fused_computation | convolution fusion | flops 3229614080 | bytes 28311552 | tf_op jit(solution)/shard_map/dot_general | solution.py:50
  563.2 8.3 fusion.60
  571.5 10.3 %add_convert_fusion.1 = bf16[2048,2048]{1,0:T(8,128)(2,1)} fusion(f32[2048,2048]{1,0:T(8,128)} %fusion.60, bf16[2048,384]{0,1:T(8,128)(2,1)S(1)} %copy-done.19, bf16[1,2048,384]{2,1,0:T(8,128)(2,1)S(1)} %copy-done.18), kind=kOutput, calls=%fused_computation.1 | convolution fusion | flops 3229614080 | bytes 28311552 | tf_op jit(solution)/shard_map/dot_general | solution.py:50
  581.8 80.7 %shard_map.266 = f32[256,2048]{1,0:T(8,128)} custom-call(bf16[16,128,2048]{2,1,0:T(8,128)(2,1)} %bitcast.231, bf16[16,128,2048]{2,1,0:T(8,128)(2,1)} %bitcast.230), custom_call_target="tpu_custom_call" | custom-call | tf_op jit(solution)/shard_map/pallas_call | solution.py:541
  667.2 6.6 fusion.66
  708.5 8.3 fusion
  716.9 6.6 convolution_convert_fusion
  736.4 181.9 %shard_map.267 = (f32[128,2560]{1,0:T(8,128)}, f32[128,2048]{1,0:T(8,128)}, f32[128,128]{1,0:T(8,128)}) custom-call(bf16[16,128,2560]{2,1,0:T(8,128)(2,1)} %bitcast.232, bf16[16,128,2048]{2,1,0:T(8,128)(2,1)} %bitcast.233, bf16[16,128,128]{2,1,0:T(8,128)(2,1)} %bitcast.248), custom_call_target="tpu_custom_call" | custom-call | tf_op jit(solution)/shard_map/pallas_call | solution.py:541
  923.1 10.4 %add_bitcast_fusion.1 = f32[1,2048,384]{2,1,0:T(8,128)} fusion(f32[2048,384]{1,0:T(8,128)} %fusion.4, bf16[2048,384]{0,1:T(8,128)(2,1)S(1)} %copy-done.20, bf16[2048,2176]{1,0:T(8,128)(2,1)} %bitcast.264), kind=kOutput, calls=%fused_computation.38 | convolution fusion | flops 3222011904 | bytes 16252928 | tf_op jit(solution)/shard_map/dot_general | solution.py:50
  933.5 9.7 %add_bitcast_fusion.2 = f32[1,2048,384]{2,1,0:T(8,128)} fusion(f32[2048,384]{1,0:T(8,128)S(1)} %copy-done.69, bf16[2048,384]{0,1:T(8,128)(2,1)S(1)} %copy-done.25, bf16[2048,2176]{1,0:T(8,128)(2,1)} %bitcast.265), kind=kOutput, calls=%fused_computation.39 | convolution fusion | flops 3222011904 | bytes 16252928 | tf_op jit(solution)/shard_map/dot_general | solution.py:50
  946.9 15.7 %shard_map.268 = f32[40,128]{1,0:T(8,128)} custom-call(f32[40,128]{1,0:T(8,128)} %select_maximum_fusion.in_ref), custom_call_target="tpu_custom_call" | custom-call | tf_op jit(solution)/shard_map/pallas_call | solution.py:582
  (266 shorter events, 129.6 us)
Async XLA Ops:
  0.6 384.5 %copy-start = (bf16[1,2048,384]{2,1,0:T(8,128)(2,1)S(1)}, bf16[1,2048,384]{2,1,0:T(8,128)(2,1)}, u32[]{:S(2)}) copy-start(bf16[1,2048,384]{2,1,0:T(8,128)(2,1)} %param.28) | copy-start | bytes 4718596
  0.7 169.5 %copy-start.8 = (bf16[256,2048]{1,0:T(8,128)(2,1)S(1)}, bf16[256,2048]{1,0:T(8,128)(2,1)}, u32[]{:S(2)}) copy-start(bf16[256,2048]{1,0:T(8,128)(2,1)} %param.16) | copy-start | bytes 3145732
  0.7 169.5 %copy-start.44 = (f32[2048]{0:T(1024)S(1)}, f32[2048]{0:T(1024)}, u32[]{:S(2)}) copy-start(f32[2048]{0:T(1024)} %param.24) | copy-start | bytes 24580
  3.2 166.9 %copy-start.53 = (f32[256]{0:T(256)}, f32[256]{0:T(256)S(1)}, u32[]{:S(2)}) copy-start(f32[256]{0:T(256)S(1)} %add_rsqrt_fusion.3) | copy-start | bytes 3076
  178.6 20.8 %copy-start.49 = (f32[256,2]{0,1:T(2,128)}, f32[256,2]{0,1:T(2,128)S(1)}, u32[]{:S(2)}) copy-start(f32[256,2]{0,1:T(2,128)S(1)} %add_rsqrt_fusion.1) | copy-start | bytes 6148
  199.4 4.6 collective-permute-start
  208.1 153.9 %copy-start.18 = (bf16[1,2048,384]{2,1,0:T(8,128)(2,1)S(1)}, bf16[1,2048,384]{2,1,0:T(8,128)(2,1)}, u32[]{:S(2)}) copy-start(bf16[1,2048,384]{2,1,0:T(8,128)(2,1)} %param.29) | copy-start | bytes 4718596
  362.1 8.7 copy-start.52
  362.1 13.9 %slice-start = ((s8[8912896]{0:T(1024)(128)(4,1)}), s8[4194304]{0:T(1024)(128)(4,1)S(1)}, s32[]{:S(2)}) async-start(s8[8912896]{0:T(1024)(128)(4,1)} %bitcast.266), calls=%async_computation | async-start | bytes 8388608
  362.1 13.9 %slice-start.1 = ((s8[8912896]{0:T(1024)(128)(4,1)}), s8[4194304]{0:T(1024)(128)(4,1)S(1)}, s32[]{:S(2)}) async-start(s8[8912896]{0:T(1024)(128)(4,1)} %bitcast.266), calls=%async_computation.1 | async-start | bytes 8388608
  394.1 9.1 copy-start.65
  394.1 9.1 copy-start.68
  426.1 14.8 %copy-start.21 = (bf16[2048,384]{0,1:T(8,128)(2,1)}, bf16[2048,384]{0,1:T(8,128)(2,1)S(1)}, u32[]{:S(2)}) copy-start(bf16[2048,384]{0,1:T(8,128)(2,1)S(1)} %get-tuple-element.140) | copy-start | bytes 4718596
  426.1 21.1 %copy-start.66 = (bf16[2048,384]{0,1:T(8,128)(2,1)}, bf16[2048,384]{0,1:T(8,128)(2,1)S(1)}, u32[]{:S(2)}) copy-start(bf16[2048,384]{0,1:T(8,128)(2,1)S(1)} %get-tuple-element.141) | copy-start | bytes 4718596
  552.5 10.7 %copy-start.24 = (bf16[2048,384]{0,1:T(8,128)(2,1)S(1)}, bf16[2048,384]{0,1:T(8,128)(2,1)}, u32[]{:S(2)}) copy-start(bf16[2048,384]{0,1:T(8,128)(2,1)} %get-tuple-element.136) | copy-start | bytes 4718596
  581.8 80.7 %copy-start.7 = (f32[256,2048]{1,0:T(8,128)S(1)}, f32[256,2048]{1,0:T(8,128)}, u32[]{:S(2)}) copy-start(f32[256,2048]{1,0:T(8,128)} %copy-done.6) | copy-start | bytes 6291460
  581.8 80.7 %copy-start.47 = (f32[2048]{0:T(1024)S(1)}, f32[2048]{0:T(1024)}, u32[]{:S(2)}) copy-start(f32[2048]{0:T(1024)} %param.25) | copy-start | bytes 24580
  581.8 80.8 %copy-start.56 = (f32[256]{0:T(256)S(1)}, f32[256]{0:T(256)}, u32[]{:S(2)}) copy-start(f32[256]{0:T(256)} %copy-done.55) | copy-start | bytes 3076
  708.5 8.3 copy-start.9
  708.5 8.3 copy-start.45
  716.9 12.7 %slice-start.5 = ((s8[8388608]{0:T(1024)(128)(4,1)}), s8[4194304]{0:T(1024)(128)(4,1)S(1)}, s32[]{:S(2)}) async-start(s8[8388608]{0:T(1024)(128)(4,1)} %bitcast.283), calls=%async_computation.5 | async-start | bytes 8388608
  734.8 208.4 %collective-permute-start.1 = (f32[256,2048]{1,0:T(8,128)}, f32[256,2048]{1,0:T(8,128)}, u32[]{:S(2)}, u32[]{:S(2)}) collective-permute-start(f32[256,2048]{1,0:T(8,128)} %fusion), channel_id=1, source_target_pairs={{0,1},{1,0},{2,3},{3,2},{4,5},{5,4},{6,7},{7,6},{8,9},{9,8},{10,11... | collective-permute-start | bytes 6291464 | tf_op jit(solution)/shard_map/ppermute | solution.py:713
  923.1 10.4 %copy-start.25 = (bf16[2048,384]{0,1:T(8,128)(2,1)S(1)}, bf16[2048,384]{0,1:T(8,128)(2,1)}, u32[]{:S(2)}) copy-start(bf16[2048,384]{0,1:T(8,128)(2,1)} %get-tuple-element.136) | copy-start | bytes 4718596
  923.1 10.4 %copy-start.69 = (f32[2048,384]{1,0:T(8,128)S(1)}, f32[2048,384]{1,0:T(8,128)}, u32[]{:S(2)}) copy-start(f32[2048,384]{1,0:T(8,128)} %fusion.6) | copy-start | bytes 9437188
  (56 other events, 208.3 us)

commit v3 on v1

--- a/solution.py
+++ b/solution.py
@@ -1,13 +1,17 @@
+import functools
 import math
 
 import jax
 import jax.numpy as jnp
 from jax import lax
+from jax.experimental import pallas as pl
+from jax.experimental.pallas import tpu as pltpu
 from jax.sharding import PartitionSpec as P
 
 QUERY_HEADS = 32
 KEY_VALUE_HEADS = 4
 HEAD_DIM = 128
+LANES = 128
 TOP = 8
 
 
@@ -51,9 +55,944 @@
     )
 
 
-def scatter_sum(term):
-    low = lax.psum_scatter(term.astype(jnp.bfloat16), "gx", scatter_dimension=0, tiled=True)
-    return low.astype(jnp.float32)
+MESH = pl.DeviceIdType.MESH
+LEVELS = 4
+PLANE = 4
+
+
+def cut_rows(rows):
+    near, far = 3 * rows // 4, rows // 4
+    return (
+        (0, near),
+        ((0, near // 2), (near // 2, near // 2)),
+        (near, far),
+        ((near, far // 2), (near + far // 2, far // 2)),
+    )
+
+
+def neighbours():
+    me, core = lax.axis_index("gx"), lax.axis_index("gy")
+    level = me // PLANE
+    x_side = me + 1 - 2 * (me % 2)
+    y_side = me + 2 - 4 * ((me // 2) % 2)
+    return me, core, level, x_side, y_side
+
+
+def greet(level, targets, with_core, me, core):
+    barrier = pltpu.get_barrier_semaphore()
+
+    def hello(device):
+        pl.semaphore_signal(barrier, inc=1, device_id=device, device_id_type=MESH)
+
+    for target in targets:
+        hello((target, core))
+    if with_core:
+        hello((me, 1 - core))
+
+    @pl.when(level > 0)
+    def _():
+        hello((me - PLANE, core))
+
+    @pl.when(level < LEVELS - 1)
+    def _():
+        hello((me + PLANE, core))
+
+    inner = jnp.where(level > 0, 1, 0) + jnp.where(level < LEVELS - 1, 1, 0)
+    pl.semaphore_wait(barrier, len(targets) + int(with_core) + inner)
+
+
+def when(condition, action):
+    if condition is None:
+        action()
+    else:
+        pl.when(condition)(action)
+
+
+def gather_kernel(count, with_pair, *refs):
+    paired = sum(with_pair)
+    ins, outs, pairs = refs[:count], refs[count : 2 * count], list(refs[2 * count : 2 * count + paired])
+    pairs = [pairs.pop(0) if wanted else None for wanted in with_pair]
+    sems = refs[2 * count + paired :]
+    steps = gather_steps(ins, outs, pairs, sems)
+    for step in steps.order:
+        step()
+    steps.end()
+
+
+class gather_steps:
+    def __init__(self, ins, outs, pairs, sems):
+        self.ins, self.outs, self.pairs = ins, outs, pairs
+        self.send_sem, self.recv_sem, self.local_sem, self.pair_send, self.pair_recv = sems
+        self.me, self.core, self.level, self.x_side, self.y_side = neighbours()
+        self.diagonal = self.x_side + self.y_side - self.me
+        self.spans = cut_rows(ins[0].shape[0])
+        self.has_up, self.has_down = self.level < LEVELS - 1, self.level > 0
+        self.up, self.down = (self.me + PLANE, self.core), (self.me - PLANE, self.core)
+        self.to_x, self.to_y = (self.x_side, self.core), (self.y_side, self.core)
+        self.sent, self.mirrored, self.everyone = [], [], range(len(ins))
+        greet(self.level, (self.x_side, self.y_side), any(p is not None for p in pairs), self.me, self.core)
+        self.order = [
+            self.start,
+            self.side_small,
+            lambda: self.column(1),
+            lambda: self.cross(0),
+            lambda: self.column(2),
+            self.start_planes,
+            lambda: self.cross(1),
+            lambda: self.column(3),
+            lambda: self.planes(1),
+            lambda: self.cross(2),
+            lambda: self.planes(2),
+            lambda: self.cross(3),
+            lambda: self.planes(3),
+            lambda: [self.halves(step) for step in range(LEVELS)],
+        ]
+
+    def send(self, condition, k, slot, source, first, number, span, target):
+        def copy():
+            there = self.outs[k].at[pl.ds(first, number), pl.ds(*span)]
+            here = there
+            if source == "own":
+                here, there = self.ins[k].at[pl.ds(*span)], self.outs[k].at[first, pl.ds(*span)]
+            return pltpu.make_async_remote_copy(
+                here,
+                there,
+                self.send_sem.at[k, slot],
+                self.recv_sem.at[k, slot],
+                device_id=target,
+                device_id_type=MESH,
+            )
+
+        when(condition, lambda: copy().start())
+        self.sent.append((condition, copy))
+
+    def mirror(self, condition, k, first, number, span, group):
+        if self.pairs[k] is None:
+            return
+        slot = len(self.mirrored)
+
+        def copy():
+            return pltpu.make_async_remote_copy(
+                self.outs[k].at[pl.ds(first, number), pl.ds(*span)],
+                self.pairs[k].at[pl.ds(first, number), pl.ds(*span)],
+                self.pair_send.at[slot],
+                self.pair_recv.at[slot],
+                device_id=(self.me, 1 - self.core),
+                device_id_type=MESH,
+            )
+
+        when(condition, lambda: copy().start())
+        self.mirrored.append((condition, copy, group))
+
+    def arrive(self, condition, k, slot, first, number, span, group):
+        place = self.outs[k].at[pl.ds(first, number), pl.ds(*span)]
+
+        def wait():
+            pltpu.make_async_remote_copy(
+                place,
+                place,
+                self.send_sem.at[k, slot],
+                self.recv_sem.at[k, slot],
+                device_id=self.to_x,
+                device_id_type=MESH,
+            ).wait_recv()
+
+        when(condition, wait)
+        self.mirror(condition, k, first, number, span, group)
+
+    def members(self, step):
+        if step == 0:
+            return [(None, 0, 0)]
+        return [(self.level >= step, step, -step), (self.level + step < LEVELS, 3 + step, step)]
+
+    def slot_of(self, group, index):
+        return 6 + 7 * group + index
+
+    last = 6 + 28
+
+    def own_copy(self, k):
+        return pltpu.make_async_copy(self.ins[k], self.outs[k].at[self.me], self.local_sem.at[k])
+
+    def start(self):
+        whole_a, half_a, whole_b, half_b = self.spans
+        last, me = self.last, self.me
+        for k in self.everyone:
+            self.own_copy(k).start()
+            self.send(None, k, last, "own", me, 1, whole_b, self.to_x)
+            self.send(None, k, last + 1, "own", me, 1, whole_b, self.to_y)
+            self.send(self.has_up, k, 0, "own", me, 1, whole_a, self.up)
+            self.send(self.has_down, k, 3, "own", me, 1, whole_a, self.down)
+            self.send(None, k, self.slot_of(0, 0), "own", me, 1, whole_a, self.to_x)
+            self.send(None, k, self.slot_of(1, 0), "own", me, 1, whole_a, self.to_y)
+
+    def side_small(self):
+        whole_a, half_a, whole_b, half_b = self.spans
+        last = self.last
+        for k in self.everyone:
+            self.arrive(None, k, last, self.x_side, 1, whole_b, 0)
+            self.send(None, k, last + 3, "out", self.x_side, 1, half_b[1], self.to_y)
+            self.arrive(None, k, last + 1, self.y_side, 1, whole_b, 0)
+            self.send(None, k, last + 2, "out", self.y_side, 1, half_b[0], self.to_x)
+        for k in self.everyone:
+            self.own_copy(k).wait()
+            self.mirror(None, k, self.me, 1, (0, self.ins[k].shape[0]), 0)
+            self.arrive(None, k, last + 2, self.diagonal, 1, half_b[0], 0)
+            self.arrive(None, k, last + 3, self.diagonal, 1, half_b[1], 0)
+
+    def start_planes(self):
+        whole_b = self.spans[2]
+        for k in self.everyone:
+            self.send(self.has_up, k, self.last + 4, "out", PLANE * self.level, PLANE, whole_b, self.up)
+            self.send(self.has_down, k, self.last + 7, "out", PLANE * self.level, PLANE, whole_b, self.down)
+
+    def cross(self, step):
+        whole_a, half_a = self.spans[:2]
+        for k in self.everyone:
+            for condition, index, distance in self.members(step):
+                first = self.x_side + PLANE * distance
+                self.arrive(condition, k, self.slot_of(0, index), first, 1, whole_a, distance)
+                self.send(condition, k, self.slot_of(3, index), "out", first, 1, half_a[1], self.to_y)
+                first = self.y_side + PLANE * distance
+                self.arrive(condition, k, self.slot_of(1, index), first, 1, whole_a, distance)
+                self.send(condition, k, self.slot_of(2, index), "out", first, 1, half_a[0], self.to_x)
+
+    def halves(self, step):
+        half_a = self.spans[1]
+        for k in self.everyone:
+            for condition, index, distance in self.members(step):
+                first = self.diagonal + PLANE * distance
+                self.arrive(condition, k, self.slot_of(2, index), first, 1, half_a[0], distance)
+                self.arrive(condition, k, self.slot_of(3, index), first, 1, half_a[1], distance)
+
+    def column(self, step):
+        whole_a = self.spans[0]
+        for k in self.everyone:
+            for condition, index, distance in self.members(step):
+                first = self.me + PLANE * distance
+                rising = distance < 0
+                self.arrive(condition, k, step - 1 if rising else 2 + step, first, 1, whole_a, distance)
+                if step < LEVELS - 1:
+                    onward = condition & (self.has_up if rising else self.has_down)
+                    slot = step if rising else 3 + step
+                    self.send(onward, k, slot, "out", first, 1, whole_a, self.up if rising else self.down)
+                self.send(condition, k, self.slot_of(0, index), "out", first, 1, whole_a, self.to_x)
+                self.send(condition, k, self.slot_of(1, index), "out", first, 1, whole_a, self.to_y)
+
+    def planes(self, step):
+        whole_b = self.spans[2]
+        for k in self.everyone:
+            for condition, index, distance in self.members(step):
+                first = PLANE * (self.level + distance)
+                rising = distance < 0
+                self.arrive(condition, k, self.last + (3 if rising else 6) + step, first, PLANE, whole_b, distance)
+                if step < LEVELS - 1:
+                    onward = condition & (self.has_up if rising else self.has_down)
+                    slot = self.last + (4 if rising else 7) + step
+                    self.send(onward, k, slot, "out", first, PLANE, whole_b, self.up if rising else self.down)
+
+    def paired_level(self, distance):
+        for condition, copy, group in self.mirrored:
+            if group == distance:
+                when(condition, lambda copy=copy: copy().wait_recv())
+
+    def end(self, levels_waited=False):
+        for condition, copy in self.sent:
+            when(condition, lambda copy=copy: copy().wait_send())
+        for condition, copy, group in self.mirrored:
+            when(condition, lambda copy=copy: copy().wait_send())
+            if not levels_waited:
+                when(condition, lambda copy=copy: copy().wait_recv())
+
+
+GATHER_SLOTS = 6 + 28 + 10
+
+
+def gather_semaphores(count, paired):
+    dma = pltpu.SemaphoreType.DMA
+    slots = (count, GATHER_SLOTS)
+    pair_slots = (max(1, paired * (GATHER_SLOTS + 1)),)
+    return [dma(slots), dma(slots), dma((count,)), dma(pair_slots), dma(pair_slots)]
+
+
+def gather_blocks(arrays, with_pair, collective_id):
+    count, blocks, paired = len(arrays), lax.axis_size("gx"), sum(with_pair)
+    shapes = [jax.ShapeDtypeStruct((blocks, *a.shape), a.dtype) for a in arrays]
+    shapes += [shape for shape, wanted in zip(shapes, with_pair) if wanted]
+    return pl.pallas_call(
+        functools.partial(gather_kernel, count, with_pair),
+        out_shape=shapes,
+        in_specs=[pl.BlockSpec(memory_space=pl.ANY)] * count,
+        out_specs=[pl.BlockSpec(memory_space=pl.ANY)] * len(shapes),
+        scratch_shapes=gather_semaphores(count, paired),
+        compiler_params=pltpu.CompilerParams(collective_id=collective_id, has_side_effects=True),
+    )(*arrays)
+
+
+def dot_nn(left, right):
+    return lax.dot_general(left, right, (((1,), (0,)), ((), ())), preferred_element_type=jnp.float32)
+
+
+def dot_nt(left, right):
+    return lax.dot_general(left, right, (((1,), (1,)), ((), ())), preferred_element_type=jnp.float32)
+
+
+def experts_kernel(experts_all, *refs):
+    rows_ref, grads_own, grads_pair, w_gate, w_up, w_down = refs[:6]
+    weighted_out, grad_in_out, terms_out, gate_out, up_out, down_out = refs[6:12]
+    held, grads, w_in, left_in, left_down, weighted_ref, grad_in_ref, terms_ref = refs[12:20]
+    sums_in, sums_down, turned, grad_sem, w_sem, out_sem, sum_sem = refs[20:27]
+    steps = gather_steps([rows_ref], [held.at[0]], [held.at[1]], refs[27:])
+    level, core = steps.level, steps.core
+    hidden, width = w_down.shape
+    tiles = hidden // LANES
+    rows = rows_ref.shape[0]
+    visits = [
+        level,
+        jnp.where(level == 0, 1, level - 1),
+        jnp.where(level == 0, 2, jnp.where(level == 3, 1, level + 1)),
+        jnp.where(level < 2, 3, 0),
+    ]
+
+    def fetch(turn, half):
+        return pltpu.make_async_copy(
+            (grads_own, grads_pair)[half].at[pl.ds(PLANE * visits[turn], PLANE)],
+            grads.at[turn % 2, half],
+            grad_sem.at[turn % 2, half],
+        )
+
+    def fetch_start(turn):
+        fetch(turn, 0).start()
+        fetch(turn, 1).start()
+
+    joins = [
+        pltpu.make_async_copy(part, w_in.at[:, pl.ds(i * hidden, hidden)], w_sem.at[i])
+        for i, part in enumerate((w_gate, w_up))
+    ]
+    lane = lax.broadcasted_iota(jnp.int32, (1, LANES), 1)
+    expert = steps.me
+    gate_pick = (((lane == expert) | (lane == experts_all + expert))).astype(jnp.float32)
+    high_lane = (lane == 2 * experts_all * core + expert).astype(jnp.float32)
+    low_lane = (lane == 2 * experts_all * core + experts_all + expert).astype(jnp.float32)
+    group = 2 * rows
+
+    def leave(turn):
+        span = pl.ds(PLANE * visits[turn], PLANE)
+        pairs = ((weighted_ref, weighted_out), (grad_in_ref, grad_in_out), (terms_ref, terms_out))
+        return [
+            pltpu.make_async_copy(here.at[:, span], there.at[:, span], out_sem.at[turn, i])
+            for i, (here, there) in enumerate(pairs)
+        ]
+
+    def forward(turn, begin, end):
+        first = PLANE * visits[turn]
+        if begin == 0:
+            fetch(turn, 0).wait()
+            fetch(turn, 1).wait()
+
+        def body(step, carry):
+            half, pair = step // 2, step % 2
+            at = first + 2 * pair
+            lanes = held[half, pl.ds(at, 2), :, pl.ds(width, LANES)].reshape(group, LANES)
+            gate_rows = jnp.sum(lanes.astype(jnp.float32) * gate_pick, axis=1, keepdims=True)
+            grad_rows = grads[turn % 2, half, pl.ds(2 * pair, 2)].reshape(group, width)
+            token_rows = held[half, pl.ds(at, 2), :, pl.ds(0, width)].reshape(group, width)
+            grad_hidden = dot_nt(grad_rows, w_down[...])
+            both = dot_nn(token_rows, w_in[...])
+            terms = jnp.zeros((group, 1), jnp.float32)
+            column = pl.multiple_of(step * group, group)
+            for j in range(tiles):
+                gate_in = both[:, j * LANES : (j + 1) * LANES]
+                up_in = both[:, hidden + j * LANES : hidden + (j + 1) * LANES]
+                back = grad_hidden[:, j * LANES : (j + 1) * LANES]
+                gate_sigmoid = 1.0 / (1.0 + jnp.exp(-gate_in))
+                gate_swish = gate_in * gate_sigmoid
+                activated = gate_swish * up_in
+                terms = terms + jnp.sum(activated * back, axis=1, keepdims=True)
+                grad_act = gate_rows * back
+                weighted = gate_rows * activated
+                grad_gate = grad_act * up_in * gate_sigmoid * (1.0 + gate_in * (1.0 - gate_sigmoid))
+                grad_up = grad_act * gate_swish
+                for value, array, tile, left in (
+                    (weighted, weighted_ref, j, left_down),
+                    (grad_gate, grad_in_ref, j, left_in),
+                    (grad_up, grad_in_ref, tiles + j, left_in),
+                ):
+                    span = pl.ds(tile * LANES, LANES)
+                    array[half, pl.ds(at, 2), :, span] = value.astype(jnp.bfloat16).reshape(2, rows, LANES)
+                    left[span, pl.ds(column, group)] = value.T.astype(jnp.bfloat16)
+            high = terms.astype(jnp.bfloat16).astype(jnp.float32)
+            spread = high * high_lane + (terms - high) * low_lane
+            terms_ref[half, pl.ds(at, 2)] = spread.astype(jnp.bfloat16).reshape(2, rows, LANES)
+            return carry
+
+        lax.fori_loop(begin, end, body, 0)
+        if end == 4:
+            for copy in leave(turn):
+                copy.start()
+
+    wide = 256
+
+    def weights(turn, begin, end):
+        first = PLANE * visits[turn]
+
+        def body(step, carry):
+            span = pl.ds(pl.multiple_of(step * wide, wide), wide)
+            token_rows = held[:, pl.ds(first, PLANE), :, span].reshape(2 * PLANE * rows, wide)
+            grad_rows = grads[turn % 2, :, :, :, span].reshape(2 * PLANE * rows, wide)
+            part_in = dot_nn(left_in[...], token_rows)
+            part_down = dot_nn(left_down[...], grad_rows)
+            if turn:
+                part_in = sums_in[:, span] + part_in
+                part_down = sums_down[:, span] + part_down
+            sums_down[:, span] = part_down
+            if turn < LEVELS - 1:
+                sums_in[:, span] = part_in
+            else:
+                for i in range(2):
+                    turned[i, span] = part_in[i * hidden : (i + 1) * hidden].T
+                for copy in leave_sums(step):
+                    copy.start()
+            return carry
+
+        lax.fori_loop(begin, end, body, 0)
+        if end == width // wide and turn + 2 < LEVELS:
+            fetch_start(turn + 2)
+
+    def leave_sums(step):
+        span = pl.ds(pl.multiple_of(step * wide, wide), wide)
+        return [
+            pltpu.make_async_copy(turned.at[0, span], gate_out.at[span], sum_sem.at[step, 0]),
+            pltpu.make_async_copy(turned.at[1, span], up_out.at[span], sum_sem.at[step, 1]),
+            pltpu.make_async_copy(sums_down.at[:, span], down_out.at[:, span], sum_sem.at[step, 2]),
+        ]
+
+    def level_ready(turn):
+        if turn == 0:
+            steps.paired_level(0)
+            return
+        for distance in range(-3, 4):
+            if distance:
+                wanted = visits[turn] == level + distance
+                pl.when(wanted)(lambda distance=distance: steps.paired_level(distance))
+
+    steps.start()
+    fetch_start(0)
+    for join in joins:
+        join.start()
+    fetch_start(1)
+    steps.side_small()
+    steps.column(1)
+    steps.cross(0)
+    for join in joins:
+        join.wait()
+    steps.column(2)
+    steps.start_planes()
+    steps.halves(0)
+    level_ready(0)
+    forward(0, 0, 2)
+    steps.cross(1)
+    forward(0, 2, 4)
+    steps.column(3)
+    weights(0, 0, 4)
+    steps.planes(1)
+    weights(0, 4, 8)
+    steps.cross(2)
+    steps.halves(1)
+    level_ready(1)
+    forward(1, 0, 2)
+    steps.planes(2)
+    forward(1, 2, 4)
+    steps.cross(3)
+    weights(1, 0, 4)
+    weights(1, 4, 8)
+    steps.halves(2)
+    level_ready(2)
+    forward(2, 0, 4)
+    weights(2, 0, 8)
+    steps.planes(3)
+    steps.halves(3)
+    level_ready(3)
+    forward(3, 0, 4)
+    weights(3, 0, 8)
+    for turn in range(LEVELS):
+        for copy in leave(turn):
+            copy.wait()
+
+    def last_sums(step, carry):
+        for copy in leave_sums(step):
+            copy.wait()
+        return carry
+
+    lax.fori_loop(0, width // wide, last_sums, 0)
+    steps.end(levels_waited=True)
+
+
+def experts_products(rows, grads_own, grads_pair, w_gate, w_up, w_down, experts_all, collective_id):
+    blocks, low, count = lax.axis_size("gx"), jnp.bfloat16, rows.shape[0]
+    hidden, width = w_down.shape
+    everywhere = pl.BlockSpec(memory_space=pl.ANY)
+    block_shape = (2, blocks, count)
+    shapes = [
+        jax.ShapeDtypeStruct((*block_shape, hidden), low),
+        jax.ShapeDtypeStruct((*block_shape, 2 * hidden), low),
+        jax.ShapeDtypeStruct((*block_shape, LANES), low),
+        jax.ShapeDtypeStruct((width, hidden), jnp.float32),
+        jax.ShapeDtypeStruct((width, hidden), jnp.float32),
+        jax.ShapeDtypeStruct((hidden, width), jnp.float32),
+    ]
+    level_rows = 2 * PLANE * count
+    dma = pltpu.SemaphoreType.DMA
+    return pl.pallas_call(
+        functools.partial(experts_kernel, experts_all),
+        out_shape=shapes,
+        in_specs=[everywhere] * 5 + [pl.BlockSpec(memory_space=pltpu.VMEM)],
+        out_specs=[everywhere] * 6,
+        scratch_shapes=[
+            pltpu.VMEM((*block_shape, rows.shape[1]), low),
+            pltpu.VMEM((2, 2, PLANE, count, width), low),
+            pltpu.VMEM((width, 2 * hidden), low),
+            pltpu.VMEM((2 * hidden, level_rows), low),
+            pltpu.VMEM((hidden, level_rows), low),
+            *[pltpu.VMEM(shape.shape, low) for shape in shapes[:3]],
+            pltpu.VMEM((2 * hidden, width), jnp.float32),
+            pltpu.VMEM((hidden, width), jnp.float32),
+            pltpu.VMEM((2, width, hidden), jnp.float32),
+            dma((2, 2)),
+            dma((2,)),
+            dma((LEVELS, 3)),
+            dma((width // 256, 3)),
+            *gather_semaphores(1, 1),
+        ],
+        compiler_params=pltpu.CompilerParams(
+            collective_id=collective_id, has_side_effects=True, vmem_limit_bytes=63 * 1024 * 1024
+        ),
+    )(rows, grads_own, grads_pair, w_gate, w_up, w_down)
+
+
+def scatter_kernel(plan, *refs):
+    paired, factors, turned, count, gains = plan
+    refs = list(refs)
+
+    def take(number):
+        taken = refs[:number]
+        del refs[:number]
+        return taken
+
+    left = take(1)[0] if factors else None
+    rights = take(factors)
+    pieces = [take(count) for _ in range(1 + paired)]
+    gain_ref = take(1)[0] if gains else None
+    (out,) = take(1)
+    gain_out = take(1)[0] if gains else None
+    mine, half_y, half_x, full_x, full_y, slots_a, slots_b, side_b = take(8)
+    send_sem, recv_sem, chain_send, chain_recv, load_sem = take(5)
+    if paired:
+        sibling, away, pair_send, pair_recv, ready_sem = take(5)
+    if factors:
+        right, right_sem = take(2)
+    if gains:
+        gain_slots, gain_send, gain_recv = take(3)
+    me, core, level, x_side, y_side = neighbours()
+    rows, width = mine.shape[1:]
+    whole_a, half_a, whole_b, half_b = cut_rows(rows)
+    far = me + 2 * PLANE - 4 * PLANE * (level // 2)
+    greet(level, (x_side, y_side) + ((far,) if gains else ()), paired or gains, me, core)
+    up, down = (me + PLANE, core), (me - PLANE, core)
+    to_x, to_y = (x_side, core), (y_side, core)
+    x_at, y_at, own_at = x_side % PLANE, y_side % PLANE, me % PLANE
+    diagonal_at = (x_side + y_side - me) % PLANE
+    forward = jnp.where(level < 2, 1, 0)
+    order = [3 * forward, 2 * forward + (1 - forward), level + 1 - 2 * (level % 2), level]
+    turns = range(LEVELS)
+    sent = []
+
+    def send(condition, source, target_ref, ssem, rsem, target):
+        def copy():
+            return pltpu.make_async_remote_copy(
+                source, target_ref, ssem, rsem, device_id=target, device_id_type=MESH
+            )
+
+        when(condition, lambda: copy().start())
+        sent.append((condition, copy))
+
+    def arrive(condition, target_ref, rsem):
+        def wait():
+            pltpu.make_async_remote_copy(
+                target_ref, target_ref, rsem, rsem, device_id=to_x, device_id_type=MESH
+            ).wait_recv()
+
+        when(condition, wait)
+
+    def add(condition, height, target, *terms, step=16):
+        def run():
+            def body(i, carry):
+                at = pl.multiple_of(i * step, step)
+                total = target(at, step)[...].astype(jnp.float32)
+                for term in terms:
+                    total = total + term(at, step)[...].astype(jnp.float32)
+                target(at, step)[...] = total.astype(jnp.bfloat16)
+                return carry
+
+            lax.fori_loop(0, height // step, body, 0)
+
+        when(condition, run)
+
+    def rows_of(ref, *index, start=0):
+        return lambda at, step: ref.at[(*index, pl.ds(start + at, step))]
+
+    def level_of(ref, turn):
+        return ref.at[pl.ds(PLANE * order[turn], PLANE)]
+
+    def load(half, turn):
+        copies, lane = [], width - sum(piece.shape[2] for piece in pieces[half])
+        for i, piece in enumerate(pieces[half]):
+            place = (away if half else mine).at[pl.ds(PLANE * order[turn], PLANE), :, pl.ds(lane, piece.shape[2])]
+            copies.append(pltpu.make_async_copy(level_of(piece, turn), place, load_sem.at[half, i, turn]))
+            lane += piece.shape[2]
+        return copies
+
+    def right_copy(i):
+        depth = rights[i].shape[1] if turned else rights[i].shape[0]
+        place = right.at[:, pl.ds(i * depth, depth)] if turned else right
+        return pltpu.make_async_copy(rights[i], place, right_sem.at[i])
+
+    def hand(turn):
+        return pltpu.make_async_remote_copy(
+            level_of(away, turn),
+            level_of(sibling, turn),
+            pair_send.at[turn],
+            pair_recv.at[turn],
+            device_id=(me, 1 - core),
+            device_id_type=MESH,
+        )
+
+    def produce(half, turn):
+        first = PLANE * order[turn]
+        wide = 256
+        factor = left[half, pl.ds(first, PLANE)].reshape(PLANE * rows, left.shape[-1])
+
+        def body(step, carry):
+            span = pl.ds(pl.multiple_of(step * wide, wide), wide)
+            value = dot_nt(factor, right[span]) if turned else dot_nn(factor, right[:, span])
+            value = value.reshape(PLANE, rows, wide)
+            if half == 0:
+                value = value + sibling[pl.ds(first, PLANE), :, span].astype(jnp.float32)
+            target = away if half else mine
+            target[pl.ds(first, PLANE), :, span] = value.astype(jnp.bfloat16)
+            return carry
+
+        lax.fori_loop(0, (right.shape[0] if turned else right.shape[1]) // wide, body, 0)
+
+    def hand_over(turn):
+        if not paired:
+            return
+        if factors:
+            produce(1, turn)
+        for copy in load(1, turn):
+            copy.wait()
+        hand(turn).start()
+
+    def settle(turn):
+        for copy in load(0, turn):
+            copy.wait()
+        if not paired:
+            return
+        hand(turn).wait()
+        if factors:
+            produce(0, turn)
+            lane = right.shape[0] if turned else right.shape[1]
+        else:
+            lane = 0
+        if lane < width:
+            first = PLANE * order[turn]
+            span = pl.ds(lane, width - lane)
+            for column in range(PLANE):
+                mine[first + column, :, span] = (
+                    mine[first + column, :, span].astype(jnp.float32)
+                    + sibling[first + column, :, span].astype(jnp.float32)
+                ).astype(jnp.bfloat16)
+
+    sems = [[(send_sem.at[6 * turn + i], recv_sem.at[6 * turn + i]) for i in range(6)] for turn in turns]
+    height = half_a[0][1]
+
+    def scatter_first(turn):
+        first = PLANE * order[turn]
+        at, lower, upper = sems[turn], pl.ds(*half_a[0]), pl.ds(*half_a[1])
+        send(None, mine.at[first + diagonal_at, lower], half_y.at[turn], *at[0], to_y)
+        send(None, mine.at[first + diagonal_at, upper], half_x.at[turn], *at[1], to_x)
+        send(None, mine.at[first + x_at, upper], full_x.at[turn, upper], *at[2], to_x)
+        send(None, mine.at[first + y_at, lower], full_y.at[turn, lower], *at[3], to_y)
+
+    def scatter_second(turn):
+        first = PLANE * order[turn]
+        at, lower, upper = sems[turn], pl.ds(*half_a[0]), pl.ds(*half_a[1])
+        arrive(None, half_y.at[turn], at[0][1])
+        add(None, height, rows_of(mine, first + x_at), rows_of(half_y, turn))
+        send(None, mine.at[first + x_at, lower], full_x.at[turn, lower], *at[4], to_x)
+        arrive(None, half_x.at[turn], at[1][1])
+        add(None, height, rows_of(mine, first + y_at, start=height), rows_of(half_x, turn))
+        send(None, mine.at[first + y_at, upper], full_y.at[turn, upper], *at[5], to_y)
+
+    def chain(which, turn, block, slots, spread):
+        to_level = order[turn]
+        rising, falling = to_level > level, to_level < level
+        begins = (rising & (level == 0)) | (falling & (level == LEVELS - 1))
+        middle = (rising | falling) & jnp.logical_not(begins)
+        arrive(middle, slots.at[to_level], chain_recv.at[which, to_level])
+        spread(middle, to_level)
+        outgoing = chain_send.at[which, to_level]
+        send(rising, block, slots.at[to_level], outgoing, chain_recv.at[which, to_level], up)
+        at = jnp.where(to_level == level - 1, LEVELS, to_level)
+        send(falling, block, slots.at[at], outgoing, chain_recv.at[which, at], down)
+
+    def add_small(condition, first, slot):
+        for column in range(PLANE):
+            add(
+                condition,
+                whole_b[1],
+                rows_of(mine, first + column, start=whole_b[0]),
+                rows_of(slots_b, slot, column),
+            )
+
+    def chain_small(turn):
+        first = PLANE * order[turn]
+        block = mine.at[pl.ds(first, PLANE), pl.ds(*whole_b)]
+        chain(1, turn, block, slots_b, lambda condition, slot: add_small(condition, first, slot))
+
+    def plane_arrives(turn):
+        at, lower, upper = sems[turn], pl.ds(*half_a[0]), pl.ds(*half_a[1])
+        arrive(None, full_x.at[turn, upper], at[2][1])
+        arrive(None, full_y.at[turn, lower], at[3][1])
+        arrive(None, full_x.at[turn, lower], at[4][1])
+        arrive(None, full_y.at[turn, upper], at[5][1])
+
+    def chain_large(turn):
+        own = PLANE * order[turn] + own_at
+        plane_arrives(turn)
+        add(None, whole_a[1], rows_of(mine, own), rows_of(full_x, turn), rows_of(full_y, turn))
+        chain(
+            0,
+            turn,
+            mine.at[own, pl.ds(*whole_a)],
+            slots_a,
+            lambda condition, slot: add(condition, whole_a[1], rows_of(mine, own), rows_of(slots_a, slot)),
+        )
+
+    gain_partners = ((me, 1 - core), to_x, to_y, (me + PLANE - 2 * PLANE * (level % 2), core), (far, core))
+
+    def gain_copy(turn):
+        return pltpu.make_async_remote_copy(
+            gain_slots.at[2 * turn],
+            gain_slots.at[2 * turn + 1],
+            gain_send.at[turn],
+            gain_recv.at[turn],
+            device_id=gain_partners[turn],
+            device_id_type=MESH,
+        )
+
+    def gain_step(turn):
+        if not gains:
+            return
+        if turn == 0:
+            gain_slots[0] = gain_ref[...]
+        else:
+            gain_copy(turn - 1).wait_recv()
+            gain_slots[2 * turn] = gain_slots[2 * turn - 2] + gain_slots[2 * turn - 1]
+        if turn < len(gain_partners):
+            gain_copy(turn).start()
+        else:
+            gain_out[...] = gain_slots[2 * turn]
+
+    if factors:
+        for i in range(factors):
+            right_copy(i).start()
+    for turn in turns:
+        for half in range(1 + paired):
+            for copy in load(half, turn):
+                copy.start()
+    if factors:
+        for i in range(factors):
+            right_copy(i).wait()
+    gain_step(0)
+    hand_over(0)
+    if paired:
+        hand_over(1)
+    for turn in turns:
+        settle(turn)
+        scatter_first(turn)
+        if turn < LEVELS - 1 and not paired:
+            chain_small(turn)
+        if turn + 2 < LEVELS:
+            hand_over(turn + 2)
+        if paired:
+            if turn < LEVELS - 1:
+                chain_small(turn)
+            if turn >= 1:
+                scatter_second(turn - 1)
+            if turn >= 2:
+                chain_large(turn - 2)
+    if not paired:
+        for turn in range(LEVELS - 1):
+            scatter_second(turn)
+            gain_step(turn + 1)
+            if turn:
+                chain_large(turn - 1)
+    scatter_second(LEVELS - 1)
+    gain_step(4)
+    chain_large(LEVELS - 2)
+
+    first = PLANE * level
+    own = first + own_at
+    arrivals = ((level > 0, level), (level < LEVELS - 1, LEVELS))
+    for condition, slot in arrivals:
+        arrive(condition, slots_b.at[slot], chain_recv.at[1, slot])
+        add_small(condition, first, slot)
+    side = [(send_sem.at[24 + i], recv_sem.at[24 + i]) for i in range(4)]
+    short = half_b[0][1]
+    spans = [pl.ds(0, short), pl.ds(short, short), pl.ds(2 * short, 2 * short), pl.ds(4 * short, 2 * short)]
+    send(None, mine.at[first + diagonal_at, pl.ds(*half_b[0])], side_b.at[spans[0]], *side[0], to_y)
+    send(None, mine.at[first + diagonal_at, pl.ds(*half_b[1])], side_b.at[spans[1]], *side[1], to_x)
+    plane_arrives(LEVELS - 1)
+    arrive(None, side_b.at[spans[0]], side[0][1])
+    add(None, short, rows_of(mine, first + x_at, start=half_b[0][0]), rows_of(side_b))
+    send(None, mine.at[first + x_at, pl.ds(*whole_b)], side_b.at[spans[2]], *side[2], to_x)
+    arrive(None, side_b.at[spans[1]], side[1][1])
+    add(None, short, rows_of(mine, first + y_at, start=half_b[1][0]), rows_of(side_b, start=short))
+    send(None, mine.at[first + y_at, pl.ds(*whole_b)], side_b.at[spans[3]], *side[3], to_y)
+    gain_step(5)
+    base = core * rows if paired else 0
+    step = 16
+
+    def tail_a(i, carry):
+        at = pl.multiple_of(i * step, step)
+        span = pl.ds(at, step)
+        total = mine[own, span].astype(jnp.float32)
+        total = total + full_x[LEVELS - 1, span].astype(jnp.float32) + full_y[LEVELS - 1, span].astype(jnp.float32)
+        out[pl.ds(pl.multiple_of(base + at, step), step)] = total
+        return carry
+
+    lax.fori_loop(0, whole_a[1] // step, tail_a, 0)
+    for condition, slot in arrivals:
+        arrive(condition, slots_a.at[slot], chain_recv.at[0, slot])
+
+        def more(slot=slot):
+            def body(i, carry):
+                at = pl.multiple_of(i * step, step)
+                span = pl.ds(pl.multiple_of(base + at, step), step)
+                out[span] = out[span] + slots_a[slot, pl.ds(at, step)].astype(jnp.float32)
+                return carry
+
+            lax.fori_loop(0, whole_a[1] // step, body, 0)
+
+        when(condition, more)
+    arrive(None, side_b.at[spans[2]], side[2][1])
+    arrive(None, side_b.at[spans[3]], side[3][1])
+
+    def tail_b(i, carry):
+        at = pl.multiple_of(i * step, step)
+        total = mine[own, pl.ds(whole_b[0] + at, step)].astype(jnp.float32)
+        total = total + side_b[pl.ds(2 * short + at, step)].astype(jnp.float32)
+        total = total + side_b[pl.ds(4 * short + at, step)].astype(jnp.float32)
+        out[pl.ds(pl.multiple_of(base + whole_b[0] + at, step), step)] = total
+        return carry
+
+    lax.fori_loop(0, whole_b[1] // step, tail_b, 0)
+    if paired:
+
+        def exchange(core_of_rows):
+            span = pl.ds(pl.multiple_of(core_of_rows * rows, rows), rows)
+            return pltpu.make_async_remote_copy(
+                out.at[span],
+                out.at[span],
+                ready_sem.at[0],
+                ready_sem.at[1],
+                device_id=(me, 1 - core),
+                device_id_type=MESH,
+            )
+
+        exchange(core).start()
+        exchange(1 - core).wait_recv()
+        exchange(core).wait_send()
+    if gains:
+        for turn in range(len(gain_partners)):
+            gain_copy(turn).wait_send()
+    for condition, copy in sent:
+        when(condition, lambda copy=copy: copy().wait_send())
+
+
+def scatter_sums(pieces, collective_id, away=(), product=None, gains=None):
+    paired, low = bool(away) or product is not None, jnp.bfloat16
+    operands, factors, turned, features = [], 0, False, 0
+    if product:
+        left, rights, turned = product
+        features, factors = rights[0].shape[0 if turned else 1], len(rights)
+        operands, (blocks, rows) = [left, *rights], left.shape[1:3]
+    else:
+        blocks, rows = pieces[0].shape[:2]
+    width = features + sum(piece.shape[2] for piece in pieces)
+    near, remote = 3 * rows // 4, rows // 4
+    dma = pltpu.SemaphoreType.DMA
+    scratch = [
+        pltpu.VMEM((blocks, rows, width), low),
+        pltpu.VMEM((LEVELS, near // 2, width), low),
+        pltpu.VMEM((LEVELS, near // 2, width), low),
+        pltpu.VMEM((LEVELS, near, width), low),
+        pltpu.VMEM((LEVELS, near, width), low),
+        pltpu.VMEM((LEVELS + 1, near, width), low),
+        pltpu.VMEM((LEVELS + 1, PLANE, remote, width), low),
+        pltpu.VMEM((3 * remote, width), low),
+        *[dma((28,)), dma((28,)), dma((2, 5)), dma((2, 5)), dma((2, max(1, len(pieces)), LEVELS))],
+    ]
+    if paired:
+        whole = pltpu.VMEM((blocks, rows, width), low)
+        scratch += [whole, whole, dma((LEVELS,)), dma((LEVELS,)), dma((2,))]
+    if factors:
+        depth = left.shape[-1]
+        scratch += [pltpu.VMEM((features, depth) if turned else (depth, features), low), dma((factors,))]
+    vmem, everywhere = pl.BlockSpec(memory_space=pltpu.VMEM), pl.BlockSpec(memory_space=pl.ANY)
+    operands += [*pieces, *away]
+    in_specs = [everywhere] * len(operands)
+    if factors:
+        in_specs[0] = vmem
+    shapes = [jax.ShapeDtypeStruct(((2 if paired else 1) * rows, width), jnp.float32)]
+    if gains is not None:
+        operands, in_specs = operands + [gains], in_specs + [vmem]
+        shapes.append(jax.ShapeDtypeStruct(gains.shape, gains.dtype))
+        scratch += [pltpu.VMEM((11, *gains.shape), gains.dtype), dma((5,)), dma((5,))]
+    plan = (paired, factors, turned, len(pieces), gains is not None)
+    return pl.pallas_call(
+        functools.partial(scatter_kernel, plan),
+        out_shape=shapes,
+        in_specs=in_specs,
+        out_specs=[vmem] * len(shapes),
+        scratch_shapes=scratch,
+        compiler_params=pltpu.CompilerParams(
+            collective_id=collective_id, has_side_effects=True, vmem_limit_bytes=60 * 1024 * 1024
+        ),
+    )(*operands)
+
+
+def kernels_fit():
+    return lax.axis_size("gx") == LEVELS * PLANE and lax.axis_size("gy") == 2
+
+
+def packed_gains(vectors):
+    rows = jnp.concatenate([vector.reshape(-1, HEAD_DIM) for vector in vectors], axis=0)
+    return jnp.pad(rows, ((0, -rows.shape[0] % 8), (0, 0)))
+
+
+def unpacked_gains(rows, vectors):
+    sums, at = [], 0
+    for vector in vectors:
+        length = vector.shape[0] // HEAD_DIM
+        sums.append(rows[at : at + length].reshape(-1))
+        at += length
+    return sums
+
+
+def two_parts(values):
+    high = lax.reduce_precision(values, 8, 7)
+    return high.astype(jnp.bfloat16), (values - high).astype(jnp.bfloat16)
 
 
 def sparse_experts(normed_ffn, logits, route_hits, routes, cotangent, w_gate, w_up, w_down):
@@ -140,73 +1079,29 @@
     return lax.ppermute(rows, "gy", [(0, 1), (1, 0)])
 
 
-def dense_experts(normed_ffn, logits, route_hits, cotangent, w_gate, w_up, w_down):
+def own_half(rows):
+    count = rows.shape[0] // lax.axis_size("gy")
+    return lax.dynamic_slice_in_dim(rows, lax.axis_index("gy") * count, count, 0)
+
+
+def dense_experts(normed_ffn, logits, route_hits, grads_own, grads_pair, w_gate, w_up, w_down):
     sequence_length, model_width = normed_ffn.shape
-    devices_gx = lax.axis_size("gx")
-    half_rows = sequence_length // lax.axis_size("gy")
-    my_core = lax.axis_index("gy")
-    my_expert = lax.axis_index("gx")
-
-    def own_half(rows):
-        return lax.dynamic_slice_in_dim(rows, my_core * half_rows, half_rows, 0)
-
-    def to_experts(rows):
-        own_rows = lax.all_gather(own_half(rows), "gx", axis=0, tiled=True)
-        return (own_rows, swap_cores(own_rows))
-
-    def both_halves(own_rows):
-        other = swap_cores(own_rows)
-        return jnp.where(
-            my_core == 0,
-            jnp.concatenate([own_rows, other], axis=0),
-            jnp.concatenate([other, own_rows], axis=0),
-        )
-
-    def from_experts(partial_rows):
-        there = swap_cores(partial_rows(1).astype(jnp.bfloat16))
-        own_rows = (partial_rows(0) + there).astype(jnp.bfloat16)
-        summed = lax.psum_scatter(own_rows, "gx", scatter_dimension=0, tiled=True)
-        return both_halves(summed).astype(jnp.float32)
-
-    def dot(left, right):
-        return jnp.dot(left, right, preferred_element_type=jnp.float32)
-
+    experts_all = logits.shape[1]
     gate_exps = jnp.exp(jnp.where(jnp.any(route_hits, axis=1), logits, -1e30))
     gate_all = gate_exps / jnp.sum(gate_exps, axis=1, keepdims=True)
-    grad_sets = to_experts(cotangent)
-    row_sets = to_experts(normed_ffn)
-    gate_sets = to_experts(gate_all)
-    weighted, gate_terms, grad_gate_in, grad_up_in = [], [], [], []
-    for part in range(2):
-        gate_rows = lax.dynamic_slice_in_dim(gate_sets[part], my_expert, 1, 1)
-        gate_in = dot(row_sets[part], w_gate)
-        up_in = dot(row_sets[part], w_up)
-        grad_hidden = contract(grad_sets[part], w_down, 1, 1)
-        gate_sigmoid = jax.nn.sigmoid(gate_in)
-        gate_swish = gate_in * gate_sigmoid
-        activated = gate_swish * up_in
-        gate_terms.append(jnp.sum(activated * grad_hidden, axis=1))
-        weighted.append((gate_rows * activated).astype(jnp.bfloat16))
-        grad_act = gate_rows * grad_hidden
-        grad_gate_in.append(
-            (grad_act * up_in * gate_sigmoid * (1.0 + gate_in * (1.0 - gate_sigmoid))).astype(jnp.bfloat16)
-        )
-        grad_up_in.append((grad_act * gate_swish).astype(jnp.bfloat16))
-    mixed_rows = from_experts(lambda part: dot(weighted[part], w_down))
-    grad_rows_sum = from_experts(
-        lambda part: contract(grad_gate_in[part], w_gate, 1, 1) + contract(grad_up_in[part], w_up, 1, 1)
-    )
-    down_term, gate_term, up_term = (
-        contract(first[0], second[0], 0, 0) + contract(first[1], second[1], 0, 0)
-        for first, second in ((weighted, grad_sets), (row_sets, grad_gate_in), (row_sets, grad_up_in))
-    )
-    own_terms = gate_terms[0] + swap_cores(gate_terms[1])
-    back = lax.all_to_all(own_terms.reshape(devices_gx, half_rows), "gx", split_axis=0, concat_axis=0, tiled=True)
-    grad_gates = both_halves(back.T)
+    gate_lanes = jnp.pad(jnp.concatenate(two_parts(gate_all), axis=1), ((0, 0), (0, LANES - 2 * experts_all)))
+    row_lanes = jnp.concatenate([own_half(normed_ffn), own_half(gate_lanes)], axis=1)
+    weighted, grad_in, terms, gate_term, up_term, down_term = experts_products(
+        row_lanes, grads_own, grads_pair, w_gate, w_up, w_down, experts_all, 2
+    )
+    (back,) = scatter_sums([terms[0]], 3, [terms[1]], (grad_in, (w_gate, w_up), True))
+    (mixed_rows,) = scatter_sums([], 4, [], (weighted, (w_down,), False))
+    term_lanes = back[:, model_width : model_width + 4 * experts_all]
+    grad_gates = jnp.sum(term_lanes.reshape(sequence_length, 4, experts_all), axis=1)
     grad_logits = (
         gate_all * (grad_gates - jnp.sum(gate_all * grad_gates, axis=1, keepdims=True))
     ).astype(jnp.bfloat16)
-    return mixed_rows, grad_rows_sum, grad_logits, (gate_term[None], up_term[None], down_term[None])
+    return mixed_rows, back[:, :model_width], grad_logits, (gate_term[None], up_term[None], down_term[None])
 
 
 def on_device(
@@ -235,29 +1130,30 @@
     experts_all = router_weight.shape[1]
     query_group_count = QUERY_HEADS // KEY_VALUE_HEADS
     inv_root = 1.0 / math.sqrt(HEAD_DIM)
-    q_full, k_full, v_full, o_full, router_full = (
-        lax.all_gather(q_weight, "gx", axis=0, tiled=True),
-        lax.all_gather(key_matrix, "gx", axis=0, tiled=True),
-        lax.all_gather(value_matrix, "gx", axis=0, tiled=True),
-        lax.all_gather(out_weight, "gx", axis=0, tiled=True),
-        lax.all_gather(router_weight, "gx", axis=0, tiled=True),
-    )
-    heads_local = q_full.shape[1] // HEAD_DIM
-    kv_local = k_full.shape[1] // HEAD_DIM
+    router_lanes = jnp.pad(router_weight, ((0, 0), (0, LANES - experts_all)))
+    rows_local = jnp.concatenate([q_weight, key_matrix, value_matrix, router_lanes, out_weight], axis=1)
+    dense = kernels_fit() and experts_all <= 2 * TOP
+    if dense:
+        weights_all, grads_own, grads_pair = gather_blocks([rows_local, own_half(cotangent)], (0, 1), 1)
+        weights_all = weights_all.reshape(-1, rows_local.shape[1])
+    else:
+        weights_all = lax.all_gather(rows_local, "gx", axis=0, tiled=True)
+    q_width, kv_width = q_weight.shape[1], key_matrix.shape[1]
+    qkv_width = q_width + 2 * kv_width
+    qkv_full = weights_all[:, :qkv_width]
+    router_full = weights_all[:, qkv_width : qkv_width + experts_all]
+    o_full = weights_all[:, qkv_width + LANES :]
+    heads_local = q_width // HEAD_DIM
+    kv_local = kv_width // HEAD_DIM
     inputs_f = tokens_in.astype(jnp.float32)
     scale_one = root_mean_scale(inputs_f)
     unit_one = inputs_f * scale_one
     normalized_input = (unit_one * attn_gain).astype(jnp.bfloat16)
-    query_unrotated = jnp.dot(normalized_input, q_full, preferred_element_type=jnp.float32).reshape(
-        sequence_length, heads_local, HEAD_DIM
-    )
-    key_unrotated = jnp.dot(normalized_input, k_full, preferred_element_type=jnp.float32).reshape(
-        sequence_length, kv_local, HEAD_DIM
-    )
+    qkv_rows = jnp.dot(normalized_input, qkv_full, preferred_element_type=jnp.float32)
+    query_unrotated = qkv_rows[:, :q_width].reshape(sequence_length, heads_local, HEAD_DIM)
+    key_unrotated = qkv_rows[:, q_width : q_width + kv_width].reshape(sequence_length, kv_local, HEAD_DIM)
     value_rows = (
-        jnp.dot(normalized_input, v_full, preferred_element_type=jnp.float32)
-        .astype(jnp.bfloat16)
-        .reshape(sequence_length, kv_local, HEAD_DIM)
+        qkv_rows[:, q_width + kv_width :].astype(jnp.bfloat16).reshape(sequence_length, kv_local, HEAD_DIM)
     )
     cosine, sine_table = rotary_tables(sequence_length, HEAD_DIM)
     q_scale = root_mean_scale(query_unrotated)
@@ -302,9 +1198,9 @@
     logits = jnp.dot(normed_ffn, router_full, preferred_element_type=jnp.float32)
     expert_iota = jnp.arange(experts_all, dtype=jnp.int32)
     route_hits = routes[:, :, None] == expert_iota
-    if experts_all <= 2 * TOP:
+    if dense:
         mixed_rows, grad_rows_sum, grad_logits, expert_grads = dense_experts(
-            normed_ffn, logits, route_hits, cotangent, gate_weight[0], up_weight[0], down_weight[0]
+            normed_ffn, logits, route_hits, grads_own, grads_pair, gate_weight[0], up_weight[0], down_weight[0]
         )
     else:
         mixed_rows, grad_rows_sum, grad_logits, expert_grads = sparse_experts(
@@ -357,31 +1253,39 @@
         .reshape(sequence_length, kv_local * HEAD_DIM)
     )
     grad_v_raw = grad_values.astype(jnp.bfloat16).reshape(sequence_length, kv_local * HEAD_DIM)
-    q_term = contract(normalized_input, grad_q_raw, 0, 0)
-    k_term = contract(normalized_input, grad_k_raw, 0, 0)
-    v_term = contract(normalized_input, grad_v_raw, 0, 0)
-    grad_normed_part = (
-        contract(grad_q_raw, q_full, 1, 1)
-        + contract(grad_k_raw, k_full, 1, 1)
-        + contract(grad_v_raw, v_full, 1, 1)
-    )
+    grad_qkv = jnp.concatenate([grad_q_raw, grad_k_raw, grad_v_raw], axis=1)
+    qkv_term = contract(normalized_input, grad_qkv, 0, 0)
+    grad_normed_part = contract(grad_qkv, qkv_full, 1, 1)
     grad_normed = grad_normed_part + swap_cores(grad_normed_part)
     attn_gain_term = jnp.sum(grad_normed * unit_one, axis=0)
     grad_input = (grad_residual + norm_back(grad_normed * attn_gain, unit_one, scale_one)).astype(
         jnp.bfloat16
     )
-    grad_q, grad_k, grad_v, grad_out, grad_router = (
-        scatter_sum(q_term),
-        scatter_sum(k_term),
-        scatter_sum(v_term),
-        scatter_sum(out_term),
-        lax.psum_scatter(router_term, "gx", scatter_dimension=0, tiled=True),
-    )
     own_mask = (jnp.arange(model_width) // part_width == lax.axis_index("gy")).astype(jnp.float32)
-    gain_attn, gain_ffn, gain_query, gain_key = lax.psum(
-        (attn_gain_term * own_mask, ffn_gain_term * own_mask, q_gain_term, k_gain_term),
-        ("gx", "gy"),
-    )
+    gains = (attn_gain_term * own_mask, ffn_gain_term * own_mask, q_gain_term, k_gain_term)
+    router_lanes = jnp.pad(router_term, ((0, 0), (0, LANES - experts_all)))
+    if dense:
+        pieces = [
+            term.astype(jnp.bfloat16).reshape(devices_gx, -1, term.shape[1])
+            for term in (qkv_term, router_lanes, out_term)
+        ]
+        sums, gain_rows = scatter_sums(pieces, 5, gains=packed_gains(gains))
+        gains = unpacked_gains(gain_rows, gains)
+    else:
+        sums = jnp.concatenate(
+            [
+                lax.psum_scatter(term, "gx", scatter_dimension=0, tiled=True)
+                for term in (qkv_term, router_lanes, out_term)
+            ],
+            axis=1,
+        )
+        gains = lax.psum(gains, ("gx", "gy"))
+    gain_attn, gain_ffn, gain_query, gain_key = gains
+    grad_q = sums[:, :q_width]
+    grad_k = sums[:, q_width : q_width + kv_width]
+    grad_v = sums[:, q_width + kv_width : qkv_width]
+    grad_router = sums[:, qkv_width : qkv_width + experts_all]
+    grad_out = sums[:, qkv_width + LANES :]
     return (
         output,
         grad_input,

time: 1780 us -> 861 us (0.48)
  waiting for transfers between devices: 1340 us -> 0.52 us
  Pallas kernels: 0 us -> 700 us
  matrix products: 208 us -> 55.9 us
  blocking collectives: 127 us -> 0 us
  local copies, waits for them, and re-layouts: 32 us -> 55.8 us
    reduce_scatter x7 -> x0, waiting for transfers between devices: 771 us -> none  [the longest x4 363 us: scatter_sum(): lax.psum_scatter(term.astype(jnp.bfloat16), 'gx', scatter_dimension=0, ti...]
    pallas_call x0 -> x5, Pallas kernels: none -> 700 us  [the longest x3 352 us: scatter_sums(): pl.pallas_call(functools.partial(scatter_kernel, plan), out_shape=shapes,...]
    all_gather x6 -> x0, waiting for transfers between devices: 542 us -> none  [the longest x2 223 us: to_experts(): own_rows = lax.all_gather(own_half(rows), 'gx', axis=0, tiled=True)]
    dot_general x22 -> x6, matrix products: 140 us -> 32.9 us  [contract(): lax.dot_general(first_op, second_op, (((first_dim,), (second_dim,)), ((),...]
    all_gather x2 -> x0, blocking collectives: 77.5 us -> none  [the longest x1 41.3 us: on_device(): lax.all_gather(router_weight, 'gx', axis=0, tiled=True)]
    psum x1 -> x0, blocking collectives: 49.6 us -> none  [on_device(): lax.psum((attn_gain_term * own_mask, ffn_gain_term * own_mask, q_gain_ter...]
    dot_general x9 -> x1, matrix products: 50.3 us -> 5.68 us  [on_device(): jnp.dot(normalized_input, qkv_full, preferred_element_type=jnp.float32)]
    convert_element_type x7 -> x2, other arithmetic: 21.9 us -> 2.46 us  [the longest x1 2.45 us: on_device(): grad_scores = (probs_again * (grad_probs - prob_inner)).astype(jnp.bfloat16)]
  transfers between devices with their start and end apart: 25 -> 2, of which waited for: 15 -> 1; matrix products, arithmetic and copies ran while one was open for 11% -> 2% of each run, Pallas kernels for 0% -> 0%
where the time goes in v3:
time: 861 us; the launch traced here: 850 us
  Pallas kernels  700 us (81%)
  matrix products  55.9 us (6%)
  local copies, waits for them, and re-layouts  55.8 us (6%)
  other arithmetic  35.9 us (4%)
    pallas_call x3, Pallas kernels, scatter_sums(): pl.pallas_call(functools.partial(scatter_kernel, plan), out_shape=shapes,...  352 us
    pallas_call x1, Pallas kernels, gather_blocks(): pl.pallas_call(functools.partial(gather_kernel, count, with_pair), out_sh...  233 us
    pallas_call x1, Pallas kernels, experts_products(): pl.pallas_call(functools.partial(experts_kernel, experts_all), out_shape=...  115 us
    dot_general x6, matrix products, contract(): lax.dot_general(first_op, second_op, (((first_dim,), (second_dim,)), ((),...  32.9 us
    unnamed x150, local copies, waits for them, and re-layouts  25.4 us
  transfers between devices with their start and end apart: 2, of which 1 were waited for; matrix products, arithmetic and copies ran while one was open for 2% of the time, Pallas kernels for 0%

profile of v3, /device:TPU:0, one launch (start us, length us, event | category | flops | bytes accessed | tf_op | source)
XLA Modules:
  0.0 850.5 jit_solution(10114091568534662704)
XLA Ops:
  7.3 233.0 %shard_map.263 = (bf16[16,128,4736]{2,1,0:T(8,128)(2,1)}, bf16[16,128,2048]{2,1,0:T(8,128)(2,1)}, bf16[16,128,2048]{2,1,0:T(8,128)(2,1)}) custom-call(bf16[128,4736]{1,0:T(8,128)(2,1)} %copy-done.23, bf16[128,2048]{1,0:T(8,128)(2,1)} %constant_dynamic-slice_fusion.1.refs_1_), custom_call_target="tpu_custom_call" | custom-call | tf_op jit(solution)/shard_map/pallas_call | solution.py:321
  240.3 5.7 fusion.2
  259.6 2.3 fusion.76
  265.0 6.1 fusion.6
  281.7 115.1 %shard_map.264 = (bf16[2,16,128,384]{3,2,1,0:T(8,128)(2,1)}, bf16[2,16,128,768]{3,2,1,0:T(8,128)(2,1)}, bf16[2,16,128,128]{3,2,1,0:T(8,128)(2,1)}, f32[2048,384]...) custom-call(bf16[128,2176]{1,0:T(8,128)(2,1)} %pad_maximum_fusion.3.refs_0_, ...), custom_call_target="tpu_custom_call" | custom-call | tf_op jit(solution)/shard_map/pallas_call | solution.py:545
  396.8 2.3 slice_bitcast_fusion.1
  399.1 100.6 %shard_map.266 = f32[256,2176]{1,0:T(8,128)} custom-call(bf16[2,16,128,768]{3,2,1,0:T(8,128)(2,1)} %get-tuple-element.29.refs_0_, bf16[2048,384]{1,0:T(8,128)(2,1)} %bitcast.177, bf16[2048,384]{1,0:T(8,128)(2,1)} %bitcast.179, bf16[16,128,128]{2,1,0:T(8,128)(2,1)} %get-tuple-element.149.refs_3_, bf16[16,128,128]{2,1,0:T(8,128)(2,1)} %get-tuple-element.148.refs_4_), custom_call_target="tpu_custom_call" | custom-call | tf_op jit(solution)/shard_map/pallas_call | solution.py:963
  500.8 4.5 multiply_reduce_fusion
  505.3 91.3 %shard_map.265 = f32[256,2048]{1,0:T(8,128)} custom-call(bf16[2,16,128,384]{3,2,1,0:T(8,128)(2,1)} %get-tuple-element.28.refs_0_, bf16[384,2048]{1,0:T(8,128)(2,1)} %bitcast.181), custom_call_target="tpu_custom_call" | custom-call | tf_op jit(solution)/shard_map/pallas_call | solution.py:963
  596.6 3.9 multiply_add_fusion.1
  600.5 6.6 fusion.34
  609.1 2.5 fusion.10
  616.2 2.5 copy.201
  618.7 3.7 copy.202
  629.1 4.9 copy.180
  634.1 2.8 fusion.39
  639.7 3.3 fusion.31
  643.9 8.4 fusion
  654.2 7.1 convolution_convert_fusion.1
  661.3 6.6 convolution_convert_fusion
  667.8 3.0 fusion.26
  671.5 159.7 %shard_map.267 = (f32[128,4736]{1,0:T(8,128)}, f32[40,128]{1,0:T(8,128)}) custom-call(bf16[16,128,2560]{2,1,0:T(8,128)(2,1)} %bitcast.162, bf16[16,128,128]{2,1,0:T(8,128)(2,1)} %bitcast.185, bf16[16,128,2048]{2,1,0:T(8,128)(2,1)} %bitcast.163, f32[40,128]{1,0:T(8,128)} %select_maximum_fusion.refs_3_), custom_call_target="tpu_custom_call" | custom-call | tf_op jit(solution)/shard_map/pallas_call | solution.py:963
  831.2 3.1 fusion.73
  838.6 4.0 fusion.25
  (224 shorter events, 65.7 us)
Async XLA Ops:
  4.2 236.1 %copy-start.6 = (bf16[256,2048]{1,0:T(8,128)(2,1)S(1)}, bf16[256,2048]{1,0:T(8,128)(2,1)}, u32[]{:S(2)}) copy-start(bf16[256,2048]{1,0:T(8,128)(2,1)} %param.16) | copy-start | bytes 3145732
  4.2 236.1 %copy-start.41 = (f32[2048]{0:T(1024)S(1)}, f32[2048]{0:T(1024)}, u32[]{:S(2)}) copy-start(f32[2048]{0:T(1024)} %param.24) | copy-start | bytes 24580
  4.2 236.1 %copy-start.55 = (f32[256]{0:T(256)}, f32[256]{0:T(256)S(1)}, u32[]{:S(2)}) copy-start(f32[256]{0:T(256)S(1)} %add_rsqrt_fusion.3) | copy-start | bytes 3076
  251.4 20.1 %copy-start.51 = (f32[256,2]{0,1:T(2,128)}, f32[256,2]{0,1:T(2,128)S(1)}, u32[]{:S(2)}) copy-start(f32[256,2]{0,1:T(2,128)S(1)} %add_rsqrt_fusion.1) | copy-start | bytes 6148
  264.9 6.2 copy-start.34
  265.0 7.4 copy-start.60
  271.1 4.4 collective-permute-start
  277.5 223.2 %copy-start.57 = (f32[256]{0:T(256)}, f32[256]{0:T(256)S(1)}, u32[]{:S(2)}) copy-start(f32[256]{0:T(256)S(1)} %add_rsqrt_fusion.2) | copy-start | bytes 3076
  399.1 101.7 %copy-start.5 = (f32[256,2048]{1,0:T(8,128)S(1)}, f32[256,2048]{1,0:T(8,128)}, u32[]{:S(2)}) copy-start(f32[256,2048]{1,0:T(8,128)} %copy-done.4) | copy-start | bytes 6291460
  399.1 101.7 %copy-start.44 = (f32[2048]{0:T(1024)S(1)}, f32[2048]{0:T(1024)}, u32[]{:S(2)}) copy-start(f32[2048]{0:T(1024)} %param.25) | copy-start | bytes 24580
  505.3 91.3 %copy-start.25 = (bf16[256,2048]{1,0:T(8,128)(2,1)S(1)}, bf16[256,2048]{1,0:T(8,128)(2,1)}, u32[]{:S(2)}) copy-start(bf16[256,2048]{1,0:T(8,128)(2,1)} %param.31) | copy-start | bytes 3145732
  505.3 91.3 %copy-start.45 = (f32[2048]{0:T(1024)S(1)}, f32[2048]{0:T(1024)}, u32[]{:S(2)}) copy-start(f32[2048]{0:T(1024)} %param.25) | copy-start | bytes 24580
  505.3 91.3 %copy-start.58 = (f32[256]{0:T(256)S(1)}, f32[256]{0:T(256)}, u32[]{:S(2)}) copy-start(f32[256]{0:T(256)} %copy-done.57) | copy-start | bytes 3076
  600.5 6.6 copy-start.8
  600.5 6.8 copy-start.1
  643.1 9.2 %copy-start.18 = (bf16[256,2048]{1,0:T(8,128)(2,1)}, bf16[256,2048]{1,0:T(8,128)(2,1)S(1)}, u32[]{:S(2)}) copy-start(bf16[256,2048]{1,0:T(8,128)(2,1)S(1)} %get-tuple-element.129) | copy-start | bytes 3145732
  643.9 8.8 %copy-start.11 = (bf16[256,2048]{1,0:T(8,128)(2,1)S(1)}, bf16[256,2048]{1,0:T(8,128)(2,1)}, u32[]{:S(2)}) copy-start(bf16[256,2048]{1,0:T(8,128)(2,1)} %copy-done.10) | copy-start | bytes 3145732
  643.9 8.8 %copy-start.47 = (bf16[256,16]{0,1:T(8,128)(2,1)S(1)}, bf16[256,16]{0,1:T(8,128)(2,1)}, u32[]{:S(2)}) copy-start(bf16[256,16]{0,1:T(8,128)(2,1)} %copy-done.46) | copy-start | bytes 24580
  652.3 15.6 %collective-permute-start.1 = (f32[256,2048]{1,0:T(8,128)}, f32[256,2048]{1,0:T(8,128)}, u32[]{:S(2)}, u32[]{:S(2)}) collective-permute-start(f32[256,2048]{1,0:T(8,128)} %fusion), channel_id=1, source_target_pairs={{0,1},{1,0},{2,3},{3,2},{4,5},{5,4},{6,7},{7,6},{8,9},{9,8},{10,11... | collective-permute-start | bytes 6291464 | tf_op jit(solution)/shard_map/ppermute | solution.py:1079
  654.1 7.1 copy-start.7
  654.1 7.1 copy-start.19
  654.1 7.1 copy-start.42
  654.1 7.1 copy-start.56
  831.2 5.6 copy-start.59
  (45 other events, 117.8 us)

commit v4 on v3

--- a/solution.py
+++ b/solution.py
@@ -28,16 +28,6 @@
     frequencies = THETA ** (-(2.0 * jnp.arange(half_width, dtype=jnp.float32)) / head_width)
     angles = jnp.arange(sequence_length, dtype=jnp.float32)[:, None] * frequencies[None, :]
     return (jnp.cos(angles)[:, None, :], jnp.sin(angles)[:, None, :])
-
-
-def rotate(values, cosine, sine_table):
-    half_width = values.shape[-1] // 2
-    lead_half = values[..., :half_width]
-    tail_half = values[..., half_width:]
-    return jnp.concatenate(
-        [lead_half * cosine - tail_half * sine_table, tail_half * cosine + lead_half * sine_table],
-        axis=-1,
-    )
 
 
 def norm_back(grad_normed, normed_unit, scale_rows):
@@ -337,11 +327,13 @@
 
 
 def experts_kernel(experts_all, *refs):
-    rows_ref, grads_own, grads_pair, w_gate, w_up, w_down = refs[:6]
-    weighted_out, grad_in_out, terms_out, gate_out, up_out, down_out = refs[6:12]
-    held, grads, w_in, left_in, left_down, weighted_ref, grad_in_ref, terms_ref = refs[12:20]
-    sums_in, sums_down, turned, grad_sem, w_sem, out_sem, sum_sem = refs[20:27]
-    steps = gather_steps([rows_ref], [held.at[0]], [held.at[1]], refs[27:])
+    rows_ref, grad_rows_ref, w_gate, w_up, w_down = refs[:5]
+    weighted_out, grad_in_out, terms_out, gate_out, up_out, down_out, grads_own, grads_pair = refs[5:13]
+    held, grads, w_in, left_in, left_down, weighted_ref, grad_in_ref, terms_ref = refs[13:21]
+    sums_in, sums_down, turned, grad_sem, w_sem, out_sem, sum_sem = refs[21:28]
+    steps = gather_steps(
+        [rows_ref, grad_rows_ref], [held.at[0], grads_own], [held.at[1], grads_pair], refs[28:]
+    )
     level, core = steps.level, steps.core
     hidden, width = w_down.shape
     tiles = hidden // LANES
@@ -455,8 +447,6 @@
             return carry
 
         lax.fori_loop(begin, end, body, 0)
-        if end == width // wide and turn + 2 < LEVELS:
-            fetch_start(turn + 2)
 
     def leave_sums(step):
         span = pl.ds(pl.multiple_of(step * wide, wide), wide)
@@ -469,17 +459,15 @@
     def level_ready(turn):
         if turn == 0:
             steps.paired_level(0)
-            return
         for distance in range(-3, 4):
-            if distance:
+            if turn and distance:
                 wanted = visits[turn] == level + distance
                 pl.when(wanted)(lambda distance=distance: steps.paired_level(distance))
+        fetch_start(turn)
 
     steps.start()
-    fetch_start(0)
     for join in joins:
         join.start()
-    fetch_start(1)
     steps.side_small()
     steps.column(1)
     steps.cross(0)
@@ -488,25 +476,23 @@
     steps.column(2)
     steps.start_planes()
     steps.halves(0)
+    steps.cross(1)
     level_ready(0)
-    forward(0, 0, 2)
-    steps.cross(1)
-    forward(0, 2, 4)
+    forward(0, 0, 4)
     steps.column(3)
+    steps.planes(1)
     weights(0, 0, 4)
-    steps.planes(1)
-    weights(0, 4, 8)
     steps.cross(2)
     steps.halves(1)
     level_ready(1)
-    forward(1, 0, 2)
+    weights(0, 4, 8)
+    forward(1, 0, 4)
     steps.planes(2)
-    forward(1, 2, 4)
+    weights(1, 0, 4)
     steps.cross(3)
-    weights(1, 0, 4)
-    weights(1, 4, 8)
     steps.halves(2)
     level_ready(2)
+    weights(1, 4, 8)
     forward(2, 0, 4)
     weights(2, 0, 8)
     steps.planes(3)
@@ -527,7 +513,7 @@
     steps.end(levels_waited=True)
 
 
-def experts_products(rows, grads_own, grads_pair, w_gate, w_up, w_down, experts_all, collective_id):
+def experts_products(rows, grad_rows, w_gate, w_up, w_down, experts_all, collective_id):
     blocks, low, count = lax.axis_size("gx"), jnp.bfloat16, rows.shape[0]
     hidden, width = w_down.shape
     everywhere = pl.BlockSpec(memory_space=pl.ANY)
@@ -539,14 +525,15 @@
         jax.ShapeDtypeStruct((width, hidden), jnp.float32),
         jax.ShapeDtypeStruct((width, hidden), jnp.float32),
         jax.ShapeDtypeStruct((hidden, width), jnp.float32),
+        *[jax.ShapeDtypeStruct((blocks, count, width), low)] * 2,
     ]
     level_rows = 2 * PLANE * count
     dma = pltpu.SemaphoreType.DMA
     return pl.pallas_call(
         functools.partial(experts_kernel, experts_all),
         out_shape=shapes,
-        in_specs=[everywhere] * 5 + [pl.BlockSpec(memory_space=pltpu.VMEM)],
-        out_specs=[everywhere] * 6,
+        in_specs=[everywhere] * 4 + [pl.BlockSpec(memory_space=pltpu.VMEM)],
+        out_specs=[everywhere] * 8,
         scratch_shapes=[
             pltpu.VMEM((*block_shape, rows.shape[1]), low),
             pltpu.VMEM((2, 2, PLANE, count, width), low),
@@ -561,12 +548,12 @@
             dma((2,)),
             dma((LEVELS, 3)),
             dma((width // 256, 3)),
-            *gather_semaphores(1, 1),
+            *gather_semaphores(2, 2),
         ],
         compiler_params=pltpu.CompilerParams(
             collective_id=collective_id, has_side_effects=True, vmem_limit_bytes=63 * 1024 * 1024
         ),
-    )(rows, grads_own, grads_pair, w_gate, w_up, w_down)
+    )(rows, grad_rows, w_gate, w_up, w_down)[:6]
 
 
 def scatter_kernel(plan, *refs):
@@ -1084,7 +1071,7 @@
     return lax.dynamic_slice_in_dim(rows, lax.axis_index("gy") * count, count, 0)
 
 
-def dense_experts(normed_ffn, logits, route_hits, grads_own, grads_pair, w_gate, w_up, w_down):
+def dense_experts(normed_ffn, logits, route_hits, cotangent, w_gate, w_up, w_down):
     sequence_length, model_width = normed_ffn.shape
     experts_all = logits.shape[1]
     gate_exps = jnp.exp(jnp.where(jnp.any(route_hits, axis=1), logits, -1e30))
@@ -1092,7 +1079,7 @@
     gate_lanes = jnp.pad(jnp.concatenate(two_parts(gate_all), axis=1), ((0, 0), (0, LANES - 2 * experts_all)))
     row_lanes = jnp.concatenate([own_half(normed_ffn), own_half(gate_lanes)], axis=1)
     weighted, grad_in, terms, gate_term, up_term, down_term = experts_products(
-        row_lanes, grads_own, grads_pair, w_gate, w_up, w_down, experts_all, 2
+        row_lanes, own_half(cotangent), w_gate, w_up, w_down, experts_all, 2
     )
     (back,) = scatter_sums([terms[0]], 3, [terms[1]], (grad_in, (w_gate, w_up), True))
     (mixed_rows,) = scatter_sums([], 4, [], (weighted, (w_down,), False))
@@ -1102,6 +1089,138 @@
         gate_all * (grad_gates - jnp.sum(gate_all * grad_gates, axis=1, keepdims=True))
     ).astype(jnp.bfloat16)
     return mixed_rows, back[:, :model_width], grad_logits, (gate_term[None], up_term[None], down_term[None])
+
+
+def turn_lanes(values, cosine, sine_table):
+    return values * cosine + pltpu.roll(values, HEAD_DIM // 2, 1) * sine_table
+
+
+def unit_rows(values):
+    scale = lax.rsqrt(jnp.mean(values * values, axis=1, keepdims=True) + EPSILON)
+    return values * scale, scale
+
+
+def allowed_pairs(docs_column, docs_row):
+    shape = (docs_column.shape[0], docs_row.shape[1])
+    keys_at, queries_at = lax.broadcasted_iota(jnp.int32, shape, 0), lax.broadcasted_iota(jnp.int32, shape, 1)
+    return (keys_at <= queries_at) & (docs_column == docs_row)
+
+
+def head_span(head):
+    return pl.ds(pl.multiple_of(head * HEAD_DIM, HEAD_DIM), HEAD_DIM)
+
+
+def attend_kernel(
+    q_heads, kv_heads, raw_ref, cosine_ref, sine_ref, docs_column, docs_row, q_gain, k_gain,
+    attended_ref, query_ref, key_ref, value_ref, totals_ref,
+):
+    cosine, sine_table = cosine_ref[...], sine_ref[...]
+    allowed = allowed_pairs(docs_column[...], docs_row[...])
+    group, inv_root = q_heads // kv_heads, 1.0 / math.sqrt(HEAD_DIM)
+    for kv in range(kv_heads):
+        unit, _ = unit_rows(raw_ref[:, head_span(q_heads + kv)])
+        key_rows = turn_lanes(unit * k_gain[...], cosine, sine_table).astype(jnp.bfloat16)
+        value_rows = raw_ref[:, head_span(q_heads + kv_heads + kv)]
+        key_ref[:, head_span(kv)] = key_rows
+        value_ref[:, head_span(kv)] = value_rows.astype(jnp.bfloat16)
+        value_columns = value_rows.T.astype(jnp.bfloat16)
+
+        def body(index, carry, kv=kv, key_rows=key_rows, value_columns=value_columns):
+            head = kv * group + index
+            unit, _ = unit_rows(raw_ref[:, head_span(head)])
+            query_rows = turn_lanes(unit * q_gain[...], cosine, sine_table).astype(jnp.bfloat16)
+            query_ref[:, head_span(head)] = query_rows
+            scores = jnp.where(allowed, dot_nt(key_rows, query_rows) * inv_root, -1e30)
+            peak = jnp.max(scores, axis=0, keepdims=True)
+            exps = jnp.exp(scores - peak)
+            total = jnp.sum(exps, axis=0, keepdims=True)
+            totals_ref[pl.ds(head, 1), :] = peak + jnp.log(total)
+            probs = (exps / total).astype(jnp.bfloat16)
+            attended_ref[:, head_span(head)] = dot_nn(value_columns, probs).T.astype(jnp.bfloat16)
+            return carry
+
+        lax.fori_loop(0, group, body, 0, unroll=2)
+
+
+def attend_back_kernel(
+    q_heads, kv_heads, raw_ref, cosine_ref, sine_ref, docs_column, docs_row, q_gain, k_gain,
+    query_ref, key_ref, value_ref, totals_ref, grad_ref, grad_raw_ref, gains_ref, sums_ref,
+):
+    cosine, sine_table = cosine_ref[...], sine_ref[...]
+    allowed = allowed_pairs(docs_column[...], docs_row[...])
+    group, inv_root = q_heads // kv_heads, 1.0 / math.sqrt(HEAD_DIM)
+    gains_ref[...] = jnp.zeros_like(gains_ref)
+
+    def back_to_raw(grad, head, gain, gain_row):
+        grad = turn_lanes(grad, cosine, -sine_table)
+        unit, scale = unit_rows(raw_ref[:, head_span(head)])
+        gains_ref[pl.ds(gain_row, 1), :] += jnp.sum(grad * unit, axis=0, keepdims=True)
+        grad = grad * gain
+        grad = scale * (grad - unit * jnp.mean(grad * unit, axis=1, keepdims=True))
+        grad_raw_ref[:, head_span(head)] = grad.astype(jnp.bfloat16)
+
+    for kv in range(kv_heads):
+        key_rows, value_rows = key_ref[:, head_span(kv)], value_ref[:, head_span(kv)]
+        key_columns = key_rows.astype(jnp.float32).T.astype(jnp.bfloat16)
+        sums_ref[...] = jnp.zeros_like(sums_ref)
+
+        def body(index, carry, kv=kv, key_rows=key_rows, value_rows=value_rows, key_columns=key_columns):
+            head = kv * group + index
+            query_rows, grad_rows = query_ref[:, head_span(head)], grad_ref[:, head_span(head)]
+            scores = jnp.where(allowed, dot_nt(key_rows, query_rows) * inv_root, -1e30)
+            probs = jnp.exp(scores - totals_ref[pl.ds(head, 1), :])
+            sums_ref[0] += dot_nn(probs.astype(jnp.bfloat16), grad_rows)
+            grad_probs = dot_nt(value_rows, grad_rows)
+            inner = jnp.sum(probs * grad_probs, axis=0, keepdims=True)
+            grad_scores = (probs * (grad_probs - inner)).astype(jnp.bfloat16)
+            sums_ref[1] += dot_nn(grad_scores, query_rows)
+            grad_queries = dot_nn(key_columns, grad_scores).T * inv_root
+            back_to_raw(grad_queries, head, q_gain[...], 0)
+            return carry
+
+        lax.fori_loop(0, group, body, 0, unroll=2)
+        back_to_raw(sums_ref[1] * inv_root, q_heads + kv, k_gain[...], 1)
+        grad_raw_ref[:, head_span(q_heads + kv_heads + kv)] = sums_ref[0].astype(jnp.bfloat16)
+
+
+def attention_shared(qkv_rows, doc_ids, query_norm_gain, k_gain):
+    length = qkv_rows.shape[0]
+    cosine, sine_table = rotary_tables(length, HEAD_DIM)
+    cosine, sine_table = cosine[:, 0], sine_table[:, 0]
+    return (
+        qkv_rows,
+        jnp.concatenate([cosine, cosine], axis=1),
+        jnp.concatenate([-sine_table, sine_table], axis=1),
+        doc_ids.reshape(length, 1),
+        doc_ids.reshape(1, length),
+        query_norm_gain.reshape(1, HEAD_DIM),
+        k_gain.reshape(1, HEAD_DIM),
+    )
+
+
+def attend(shared, q_heads, kv_heads):
+    length, low, shape = shared[0].shape[0], jnp.bfloat16, jax.ShapeDtypeStruct
+    return pl.pallas_call(
+        functools.partial(attend_kernel, q_heads, kv_heads),
+        out_shape=[
+            shape((length, q_heads * HEAD_DIM), low),
+            shape((length, q_heads * HEAD_DIM), low),
+            shape((length, kv_heads * HEAD_DIM), low),
+            shape((length, kv_heads * HEAD_DIM), low),
+            shape((q_heads, length), jnp.float32),
+        ],
+        compiler_params=pltpu.CompilerParams(vmem_limit_bytes=48 * 1024 * 1024),
+    )(*shared)
+
+
+def attend_back(shared, kept, grad_attended, q_heads, kv_heads):
+    length, shape = shared[0].shape[0], jax.ShapeDtypeStruct
+    return pl.pallas_call(
+        functools.partial(attend_back_kernel, q_heads, kv_heads),
+        out_shape=[shape(shared[0].shape, jnp.bfloat16), shape((8, HEAD_DIM), jnp.float32)],
+        scratch_shapes=[pltpu.VMEM((2, length, HEAD_DIM), jnp.float32)],
+        compiler_params=pltpu.CompilerParams(vmem_limit_bytes=48 * 1024 * 1024),
+    )(*shared, *kept, grad_attended)
 
 
 def on_device(
@@ -1128,13 +1247,11 @@
     devices_gy = lax.axis_size("gy")
     part_width = model_width // devices_gy
     experts_all = router_weight.shape[1]
-    query_group_count = QUERY_HEADS // KEY_VALUE_HEADS
-    inv_root = 1.0 / math.sqrt(HEAD_DIM)
     router_lanes = jnp.pad(router_weight, ((0, 0), (0, LANES - experts_all)))
     rows_local = jnp.concatenate([q_weight, key_matrix, value_matrix, router_lanes, out_weight], axis=1)
     dense = kernels_fit() and experts_all <= 2 * TOP
     if dense:
-        weights_all, grads_own, grads_pair = gather_blocks([rows_local, own_half(cotangent)], (0, 1), 1)
+        (weights_all,) = gather_blocks([rows_local], (0,), 1)
         weights_all = weights_all.reshape(-1, rows_local.shape[1])
     else:
         weights_all = lax.all_gather(rows_local, "gx", axis=0, tiled=True)
@@ -1150,45 +1267,8 @@
     unit_one = inputs_f * scale_one
     normalized_input = (unit_one * attn_gain).astype(jnp.bfloat16)
     qkv_rows = jnp.dot(normalized_input, qkv_full, preferred_element_type=jnp.float32)
-    query_unrotated = qkv_rows[:, :q_width].reshape(sequence_length, heads_local, HEAD_DIM)
-    key_unrotated = qkv_rows[:, q_width : q_width + kv_width].reshape(sequence_length, kv_local, HEAD_DIM)
-    value_rows = (
-        qkv_rows[:, q_width + kv_width :].astype(jnp.bfloat16).reshape(sequence_length, kv_local, HEAD_DIM)
-    )
-    cosine, sine_table = rotary_tables(sequence_length, HEAD_DIM)
-    q_scale = root_mean_scale(query_unrotated)
-    q_unit = query_unrotated * q_scale
-    query_rows = (
-        rotate(q_unit * query_norm_gain, cosine, sine_table)
-        .astype(jnp.bfloat16)
-        .reshape(sequence_length, kv_local, query_group_count, HEAD_DIM)
-    )
-    k_scale = root_mean_scale(key_unrotated)
-    k_unit = key_unrotated * k_scale
-    keys_rows = rotate(k_unit * k_gain, cosine, sine_table).astype(jnp.bfloat16)
-    positions = jnp.arange(sequence_length)
-    documents = doc_ids[0]
-    allowed = (positions[None, :] <= positions[:, None]) & (
-        documents[None, :] == documents[:, None]
-    )
-
-    def score_block():
-        raw_scores = (
-            jnp.einsum("qngd,knd->ngqk", query_rows, keys_rows, preferred_element_type=jnp.float32)
-            * inv_root
-        )
-        return jnp.where(allowed, raw_scores, -1e30)
-
-    scores = score_block()
-    row_peak = jnp.max(scores, axis=-1, keepdims=True)
-    attn_exps = jnp.exp(scores - row_peak)
-    row_total = jnp.sum(attn_exps, axis=-1, keepdims=True)
-    log_total = row_peak + jnp.log(row_total)
-    probs_low = (attn_exps / row_total).astype(jnp.bfloat16)
-    attended = jnp.einsum(
-        "ngqk,knd->qngd", probs_low, value_rows, preferred_element_type=jnp.float32
-    )
-    attended = attended.reshape(sequence_length, heads_local * HEAD_DIM).astype(jnp.bfloat16)
+    shared = attention_shared(qkv_rows, doc_ids, query_norm_gain, k_gain)
+    attended, *kept = attend(shared, heads_local, kv_local)
     attn_part = contract(attended, o_full, 1, 1)
     attn_total = attn_part + swap_cores(attn_part)
     residual = inputs_f + attn_total
@@ -1200,7 +1280,7 @@
     route_hits = routes[:, :, None] == expert_iota
     if dense:
         mixed_rows, grad_rows_sum, grad_logits, expert_grads = dense_experts(
-            normed_ffn, logits, route_hits, grads_own, grads_pair, gate_weight[0], up_weight[0], down_weight[0]
+            normed_ffn, logits, route_hits, cotangent, gate_weight[0], up_weight[0], down_weight[0]
         )
     else:
         mixed_rows, grad_rows_sum, grad_logits, expert_grads = sparse_experts(
@@ -1217,43 +1297,8 @@
     grad_attended = jnp.dot(grad_attn, o_full, preferred_element_type=jnp.float32).astype(
         jnp.bfloat16
     )
-    grad_attended = grad_attended.reshape(sequence_length, kv_local, query_group_count, HEAD_DIM)
-    probs_again = jnp.exp(score_block() - log_total)
-    probs_again_low = probs_again.astype(jnp.bfloat16)
-    grad_values = jnp.einsum(
-        "ngqk,qngd->knd", probs_again_low, grad_attended, preferred_element_type=jnp.float32
-    )
-    grad_probs = jnp.einsum(
-        "qngd,knd->ngqk", grad_attended, value_rows, preferred_element_type=jnp.float32
-    )
-    prob_inner = jnp.sum(probs_again * grad_probs, axis=-1, keepdims=True)
-    grad_scores = (probs_again * (grad_probs - prob_inner)).astype(jnp.bfloat16)
-    grad_queries = (
-        jnp.einsum("ngqk,knd->qngd", grad_scores, keys_rows, preferred_element_type=jnp.float32)
-        * inv_root
-    )
-    grad_keys = (
-        jnp.einsum("ngqk,qngd->knd", grad_scores, query_rows, preferred_element_type=jnp.float32)
-        * inv_root
-    )
-    grad_q_rot = rotate(
-        grad_queries.reshape(sequence_length, heads_local, HEAD_DIM), cosine, -sine_table
-    )
-    grad_k_rot = rotate(grad_keys, cosine, -sine_table)
-    q_gain_term = jnp.sum(grad_q_rot * q_unit, axis=(0, 1))
-    k_gain_term = jnp.sum(grad_k_rot * k_unit, axis=(0, 1))
-    grad_q_raw = (
-        norm_back(grad_q_rot * query_norm_gain, q_unit, q_scale)
-        .astype(jnp.bfloat16)
-        .reshape(sequence_length, heads_local * HEAD_DIM)
-    )
-    grad_k_raw = (
-        norm_back(grad_k_rot * k_gain, k_unit, k_scale)
-        .astype(jnp.bfloat16)
-        .reshape(sequence_length, kv_local * HEAD_DIM)
-    )
-    grad_v_raw = grad_values.astype(jnp.bfloat16).reshape(sequence_length, kv_local * HEAD_DIM)
-    grad_qkv = jnp.concatenate([grad_q_raw, grad_k_raw, grad_v_raw], axis=1)
+    grad_qkv, head_gains = attend_back(shared, kept, grad_attended, heads_local, kv_local)
+    q_gain_term, k_gain_term = head_gains[0], head_gains[1]
     qkv_term = contract(normalized_input, grad_qkv, 0, 0)
     grad_normed_part = contract(grad_qkv, qkv_full, 1, 1)
     grad_normed = grad_normed_part + swap_cores(grad_normed_part)

time: 861 us -> 805 us (0.935)
  local copies, waits for them, and re-layouts: 55.8 us -> 27 us
  other arithmetic: 35.9 us -> 15.5 us
  matrix products: 55.9 us -> 46 us
    pallas_call x1, Pallas kernels: 233 us -> 163 us  [gather_blocks(): pl.pallas_call(functools.partial(gather_kernel, count, with_pair), out_sh...]
    pallas_call x1, Pallas kernels: 115 us -> 169 us  [experts_products(): pl.pallas_call(functools.partial(experts_kernel, experts_all), out_shape=...]
    pallas_call x0 -> x2, Pallas kernels: none -> 21.1 us  [the longest x1 12.5 us: attend_back(): pl.pallas_call(functools.partial(attend_back_kernel, q_heads, kv_heads),...]
    unnamed x150 -> x72, local copies, waits for them, and re-layouts: 25.4 us -> 12.7 us
    dot_general x6 -> x0, matrix products: 9.32 us -> none  [the longest x1 2.84 us: on_device(): jnp.einsum('ngqk,qngd->knd', probs_again_low, grad_attended, preferred_el...]
where the time goes in v4:
time: 805 us; the launch traced here: 799 us
  Pallas kernels  706 us (88%)
  matrix products  46 us (6%)
  local copies, waits for them, and re-layouts  27 us (3%)
  other arithmetic  15.5 us (2%)
    pallas_call x3, Pallas kernels, scatter_sums(): pl.pallas_call(functools.partial(scatter_kernel, plan), out_shape=shapes,...  354 us
    pallas_call x1, Pallas kernels, experts_products(): pl.pallas_call(functools.partial(experts_kernel, experts_all), out_shape=...  169 us
    pallas_call x1, Pallas kernels, gather_blocks(): pl.pallas_call(functools.partial(gather_kernel, count, with_pair), out_sh...  163 us
    dot_general x6, matrix products, contract(): lax.dot_general(first_op, second_op, (((first_dim,), (second_dim,)), ((),...  32.4 us
  transfers between devices with their start and end apart: 2, of which 1 were waited for; matrix products, arithmetic and copies ran while one was open for 2% of the time, Pallas kernels for 0%

profile of v4, /device:TPU:0, one launch (start us, length us, event | category | flops | bytes accessed | tf_op | source)
XLA Modules:
  0.0 798.9 jit_solution(7945419437015992433)
XLA Ops:
  6.7 162.6 %shard_map.263 = bf16[16,128,4736]{2,1,0:T(8,128)(2,1)} custom-call(bf16[128,4736]{1,0:T(8,128)(2,1)} %copy-done.20), custom_call_target="tpu_custom_call" | custom-call | tf_op jit(solution)/shard_map/pallas_call | solution.py:311
  169.5 5.7 fusion.2.raw_ref
  175.2 8.6 %shard_map.264 = (bf16[256,2048]{1,0:T(8,128)(2,1)S(1)}, bf16[256,2048]{1,0:T(8,128)(2,1)S(1)}, bf16[256,256]{1,0:T(8,128)(2,1)S(1)}, bf16[256,256]{1,0:T(8,128)(2,1)S(1)}, f32[16,256]{1,0:T(8,128)S(1)}) custom-call(f32[256,2560]{1,0:T(8,128)S(1)} %fusion.2.raw_ref, f32[256,128]{1,0:T(8,128)S(1)} %get-tuple-element.126.cosine_ref, ...), custom_call_target="tpu_custom_call" | custom-call | tf_op jit(solution)/shard_map/pallas_call | solution.py:1203
  183.9 7.8 fusion.6
  191.9 1.9 constant_dynamic-slice_fusion.refs_1_
  193.8 2.6 collective-permute-done
  196.3 2.6 multiply_reduce_fusion.2
  202.8 168.7 %shard_map.265 = (bf16[2,16,128,384]{3,2,1,0:T(8,128)(2,1)}, bf16[2,16,128,768]{3,2,1,0:T(8,128)(2,1)}, bf16[2,16,128,128]{3,2,1,0:T(8,128)(2,1)}, f32[2048,384]...) custom-call(bf16[128,2176]{1,0:T(8,128)(2,1)} %pad_maximum_fusion.re, ...), custom_call_target="tpu_custom_call" | custom-call | tf_op jit(solution)/shard_map/pallas_call | solution.py:532
  371.5 92.9 %shard_map.266 = f32[256,2048]{1,0:T(8,128)} custom-call(bf16[2,16,128,384]{3,2,1,0:T(8,128)(2,1)} %get-tuple-element.30.refs_0_, bf16[384,2048]{1,0:T(8,128)(2,1)} %bitcast.56), custom_call_target="tpu_custom_call" | custom-call | tf_op jit(solution)/shard_map/pallas_call | solution.py:950
  465.5 101.6 %shard_map.267 = f32[256,2176]{1,0:T(8,128)} custom-call(bf16[2,16,128,768]{3,2,1,0:T(8,128)(2,1)} %get-tuple-element.31.refs_0_, bf16[2048,384]{1,0:T(8,128)(2,1)} %bitcast.52, bf16[2048,384]{1,0:T(8,128)(2,1)} %bitcast.54, bf16[16,128,128]{2,1,0:T(8,128)(2,1)} %get-tuple-element.113.refs_3_, bf16[16,128,128]{2,1,0:T(8,128)(2,1)} %get-tuple-element.112.refs_4_), custom_call_target="tpu_custom_call" | custom-call | tf_op jit(solution)/shard_map/pallas_call | solution.py:950
  568.2 2.8 multiply_reduce_fusion
  571.0 1.8 multiply_add_fusion
  572.8 6.5 fusion.12.grad_ref
  579.3 12.5 %shard_map.268 = (bf16[256,2560]{1,0:T(8,128)(2,1)S(1)}, f32[8,128]{1,0:T(8,128)S(1)}) custom-call(f32[256,2560]{1,0:T(8,128)} %copy-done, f32[256,128]{1,0:T(8,128)S(1)} %get-tuple-element.126.cosine_ref, f32[256,128]{1,0:T(8,128)S(1)} %get-tuple-element.127.sine_ref, s32[256,1]{1,0:T(8,128)S(1)} %copy.52.docs_column, s32[1,256]{1,0:T(1,128)S(1)} %copy-done.5, ...), custom_call_target="tpu_custom_call" | custom-call | tf_op jit(solution)/shard_map/pallas_call | solution.py:1218
  591.8 8.3 %fusion = f32[256,2048]{1,0:T(8,128)} fusion(bf16[256,2560]{1,0:T(8,128)(2,1)S(1)} %get-tuple-element.37, bf16[2048,4736]{1,0:T(8,128)(2,1)} %bitcast.50), kind=kOutput, calls=%fused_computation.1 | convolution fusion | flops 2684354560 | bytes 13893632 | tf_op jit(solution)/shard_map/dot_general | solution.py:40
  602.0 7.4 convolution_convert_fusion.1
  609.4 5.9 convolution_convert_fusion
  615.3 3.0 fusion.21
  618.9 159.0 %shard_map.269 = (f32[128,4736]{1,0:T(8,128)}, f32[40,128]{1,0:T(8,128)}) custom-call(bf16[16,128,2560]{2,1,0:T(8,128)(2,1)} %bitcast.43, bf16[16,128,128]{2,1,0:T(8,128)(2,1)} %bitcast.60, bf16[16,128,2048]{2,1,0:T(8,128)(2,1)} %bitcast.44, f32[40,128]{1,0:T(8,128)} %select_maximum_fusion.refs_3_), custom_call_target="tpu_custom_call" | custom-call | tf_op jit(solution)/shard_map/pallas_call | solution.py:950
  781.4 1.7 fusion.40
  783.1 3.2 fusion.39
  787.0 4.0 fusion.20
  791.0 1.7 copy.66
  797.0 1.7 copy.68
  (107 shorter events, 23.1 us)
Async XLA Ops:
  0.6 4.9 copy-start.26
  0.7 4.9 copy-start.27
  0.7 4.9 copy-start.23
  2.3 167.2 %copy-start.28 = (f32[256]{0:T(256)}, f32[256]{0:T(256)S(1)}, u32[]{:S(2)}) copy-start(f32[256]{0:T(256)S(1)} %add_rsqrt_fusion.1) | copy-start | bytes 3076
  6.7 162.8 %copy-start.10 = (bf16[256,2048]{1,0:T(8,128)(2,1)S(1)}, bf16[256,2048]{1,0:T(8,128)(2,1)}, u32[]{:S(2)}) copy-start(bf16[256,2048]{1,0:T(8,128)(2,1)} %param.16) | copy-start | bytes 3145732
  6.7 162.8 %copy-start.24 = (f32[2048]{0:T(1024)S(1)}, f32[2048]{0:T(1024)}, u32[]{:S(2)}) copy-start(f32[2048]{0:T(1024)} %param.24) | copy-start | bytes 24580
  169.5 5.7 copy-start.5
  169.5 5.7 copy-start.6
  169.5 5.7 copy-start.7
  175.2 16.6 %copy-start = (f32[256,2560]{1,0:T(8,128)}, f32[256,2560]{1,0:T(8,128)S(1)}, u32[]{:S(2)}) copy-start(f32[256,2560]{1,0:T(8,128)S(1)} %fusion.2.raw_ref) | copy-start | bytes 7864324
  183.9 7.9 copy-start.1
  183.9 7.9 copy-start.3
  183.9 7.9 copy-start.30
  191.8 4.6 collective-permute-start
  193.8 5.2 copy-start.25
  371.5 92.9 %copy-start.22 = (bf16[2,16,128,128]{3,2,1,0:T(8,128)(2,1)S(1)}, bf16[2,16,128,128]{3,2,1,0:T(8,128)(2,1)}, u32[]{:S(2)}) copy-start(bf16[2,16,128,128]{3,2,1,0:T(8,128)(2,1)} %get-tuple-element.32) | copy-start | bytes 3145732
  465.5 102.7 %copy-start.9 = (f32[256,2048]{1,0:T(8,128)S(1)}, f32[256,2048]{1,0:T(8,128)}, u32[]{:S(2)}) copy-start(f32[256,2048]{1,0:T(8,128)} %copy-done.8) | copy-start | bytes 6291460
  572.8 6.5 copy-start.12
  572.8 6.5 copy-start.2
  591.8 8.7 %copy-start.15 = (bf16[256,2048]{1,0:T(8,128)(2,1)S(1)}, bf16[256,2048]{1,0:T(8,128)(2,1)}, u32[]{:S(2)}) copy-start(bf16[256,2048]{1,0:T(8,128)(2,1)} %copy-done.14) | copy-start | bytes 3145732
  600.1 15.2 %collective-permute-start.1 = (f32[256,2048]{1,0:T(8,128)}, f32[256,2048]{1,0:T(8,128)}, u32[]{:S(2)}, u32[]{:S(2)}) collective-permute-start(f32[256,2048]{1,0:T(8,128)} %fusion), channel_id=1, source_target_pairs={{0,1},{1,0},{2,3},{3,2},{4,5},{5,4},{6,7},{7,6},{8,9},{9,8},{10,11... | collective-permute-start | bytes 6291464 | tf_op jit(solution)/shard_map/ppermute | solution.py:1066
  602.0 7.4 copy-start.11
  602.0 7.4 copy-start.29
  787.0 4.0 copy-start.19
  (9 other events, 22.3 us)

commit v5 on v4

--- a/solution.py
+++ b/solution.py
@@ -556,61 +556,41 @@
     )(rows, grad_rows, w_gate, w_up, w_down)[:6]
 
 
-def scatter_kernel(plan, *refs):
-    paired, factors, turned, count, gains = plan
-    refs = list(refs)
-
-    def take(number):
-        taken = refs[:number]
-        del refs[:number]
-        return taken
-
-    left = take(1)[0] if factors else None
-    rights = take(factors)
-    pieces = [take(count) for _ in range(1 + paired)]
-    gain_ref = take(1)[0] if gains else None
-    (out,) = take(1)
-    gain_out = take(1)[0] if gains else None
-    mine, half_y, half_x, full_x, full_y, slots_a, slots_b, side_b = take(8)
-    send_sem, recv_sem, chain_send, chain_recv, load_sem = take(5)
-    if paired:
-        sibling, away, pair_send, pair_recv, ready_sem = take(5)
-    if factors:
-        right, right_sem = take(2)
-    if gains:
-        gain_slots, gain_send, gain_recv = take(3)
-    me, core, level, x_side, y_side = neighbours()
-    rows, width = mine.shape[1:]
-    whole_a, half_a, whole_b, half_b = cut_rows(rows)
-    far = me + 2 * PLANE - 4 * PLANE * (level // 2)
-    greet(level, (x_side, y_side) + ((far,) if gains else ()), paired or gains, me, core)
-    up, down = (me + PLANE, core), (me - PLANE, core)
-    to_x, to_y = (x_side, core), (y_side, core)
-    x_at, y_at, own_at = x_side % PLANE, y_side % PLANE, me % PLANE
-    diagonal_at = (x_side + y_side - me) % PLANE
-    forward = jnp.where(level < 2, 1, 0)
-    order = [3 * forward, 2 * forward + (1 - forward), level + 1 - 2 * (level % 2), level]
-    turns = range(LEVELS)
-    sent = []
-
-    def send(condition, source, target_ref, ssem, rsem, target):
+class scatter_moves:
+    def __init__(self, held, out):
+        self.mine, self.half_y, self.half_x, self.full_x, self.full_y, self.slots_a, self.slots_b, self.side_b = held[:8]
+        self.send_sem, self.recv_sem, self.chain_send, self.chain_recv = held[8:12]
+        self.out = out
+        self.me, self.core, level, x_side, y_side = neighbours()
+        self.level = level
+        self.up, self.down = (self.me + PLANE, self.core), (self.me - PLANE, self.core)
+        self.to_x, self.to_y = (x_side, self.core), (y_side, self.core)
+        self.x_at, self.y_at, self.own_at = x_side % PLANE, y_side % PLANE, self.me % PLANE
+        self.diagonal_at = (x_side + y_side - self.me) % PLANE
+        forward = jnp.where(level < 2, 1, 0)
+        self.order = [3 * forward, 2 * forward + (1 - forward), level + 1 - 2 * (level % 2), level]
+        self.rows, self.width = self.mine.shape[1:]
+        self.spans = cut_rows(self.rows)
+        self.sent = []
+
+    def send(self, condition, source, target_ref, ssem, rsem, target):
         def copy():
             return pltpu.make_async_remote_copy(
                 source, target_ref, ssem, rsem, device_id=target, device_id_type=MESH
             )
 
         when(condition, lambda: copy().start())
-        sent.append((condition, copy))
-
-    def arrive(condition, target_ref, rsem):
+        self.sent.append((condition, copy))
+
+    def arrive(self, condition, target_ref, rsem):
         def wait():
             pltpu.make_async_remote_copy(
-                target_ref, target_ref, rsem, rsem, device_id=to_x, device_id_type=MESH
+                target_ref, target_ref, rsem, rsem, device_id=self.to_x, device_id_type=MESH
             ).wait_recv()
 
         when(condition, wait)
 
-    def add(condition, height, target, *terms, step=16):
+    def add(self, condition, height, target, *terms, step=16):
         def run():
             def body(i, carry):
                 at = pl.multiple_of(i * step, step)
@@ -624,148 +604,191 @@
 
         when(condition, run)
 
-    def rows_of(ref, *index, start=0):
+    def rows_of(self, ref, *index, start=0):
         return lambda at, step: ref.at[(*index, pl.ds(start + at, step))]
 
-    def level_of(ref, turn):
-        return ref.at[pl.ds(PLANE * order[turn], PLANE)]
-
-    def load(half, turn):
-        copies, lane = [], width - sum(piece.shape[2] for piece in pieces[half])
-        for i, piece in enumerate(pieces[half]):
-            place = (away if half else mine).at[pl.ds(PLANE * order[turn], PLANE), :, pl.ds(lane, piece.shape[2])]
-            copies.append(pltpu.make_async_copy(level_of(piece, turn), place, load_sem.at[half, i, turn]))
-            lane += piece.shape[2]
-        return copies
-
-    def right_copy(i):
-        depth = rights[i].shape[1] if turned else rights[i].shape[0]
-        place = right.at[:, pl.ds(i * depth, depth)] if turned else right
-        return pltpu.make_async_copy(rights[i], place, right_sem.at[i])
-
-    def hand(turn):
-        return pltpu.make_async_remote_copy(
-            level_of(away, turn),
-            level_of(sibling, turn),
-            pair_send.at[turn],
-            pair_recv.at[turn],
-            device_id=(me, 1 - core),
-            device_id_type=MESH,
-        )
-
-    def produce(half, turn):
-        first = PLANE * order[turn]
-        wide = 256
-        factor = left[half, pl.ds(first, PLANE)].reshape(PLANE * rows, left.shape[-1])
-
-        def body(step, carry):
-            span = pl.ds(pl.multiple_of(step * wide, wide), wide)
-            value = dot_nt(factor, right[span]) if turned else dot_nn(factor, right[:, span])
-            value = value.reshape(PLANE, rows, wide)
-            if half == 0:
-                value = value + sibling[pl.ds(first, PLANE), :, span].astype(jnp.float32)
-            target = away if half else mine
-            target[pl.ds(first, PLANE), :, span] = value.astype(jnp.bfloat16)
-            return carry
-
-        lax.fori_loop(0, (right.shape[0] if turned else right.shape[1]) // wide, body, 0)
-
-    def hand_over(turn):
-        if not paired:
-            return
-        if factors:
-            produce(1, turn)
-        for copy in load(1, turn):
-            copy.wait()
-        hand(turn).start()
-
-    def settle(turn):
-        for copy in load(0, turn):
-            copy.wait()
-        if not paired:
-            return
-        hand(turn).wait()
-        if factors:
-            produce(0, turn)
-            lane = right.shape[0] if turned else right.shape[1]
-        else:
-            lane = 0
-        if lane < width:
-            first = PLANE * order[turn]
-            span = pl.ds(lane, width - lane)
-            for column in range(PLANE):
-                mine[first + column, :, span] = (
-                    mine[first + column, :, span].astype(jnp.float32)
-                    + sibling[first + column, :, span].astype(jnp.float32)
-                ).astype(jnp.bfloat16)
-
-    sems = [[(send_sem.at[6 * turn + i], recv_sem.at[6 * turn + i]) for i in range(6)] for turn in turns]
-    height = half_a[0][1]
-
-    def scatter_first(turn):
-        first = PLANE * order[turn]
-        at, lower, upper = sems[turn], pl.ds(*half_a[0]), pl.ds(*half_a[1])
-        send(None, mine.at[first + diagonal_at, lower], half_y.at[turn], *at[0], to_y)
-        send(None, mine.at[first + diagonal_at, upper], half_x.at[turn], *at[1], to_x)
-        send(None, mine.at[first + x_at, upper], full_x.at[turn, upper], *at[2], to_x)
-        send(None, mine.at[first + y_at, lower], full_y.at[turn, lower], *at[3], to_y)
-
-    def scatter_second(turn):
-        first = PLANE * order[turn]
-        at, lower, upper = sems[turn], pl.ds(*half_a[0]), pl.ds(*half_a[1])
-        arrive(None, half_y.at[turn], at[0][1])
-        add(None, height, rows_of(mine, first + x_at), rows_of(half_y, turn))
-        send(None, mine.at[first + x_at, lower], full_x.at[turn, lower], *at[4], to_x)
-        arrive(None, half_x.at[turn], at[1][1])
-        add(None, height, rows_of(mine, first + y_at, start=height), rows_of(half_x, turn))
-        send(None, mine.at[first + y_at, upper], full_y.at[turn, upper], *at[5], to_y)
-
-    def chain(which, turn, block, slots, spread):
-        to_level = order[turn]
+    def turn_sems(self, turn):
+        return [(self.send_sem.at[6 * turn + i], self.recv_sem.at[6 * turn + i]) for i in range(6)]
+
+    def half_spans(self):
+        half_a = self.spans[1]
+        return half_a[0][1], pl.ds(*half_a[0]), pl.ds(*half_a[1])
+
+    def first(self, turn):
+        base, at = PLANE * self.order[turn], self.turn_sems(turn)
+        _, lower, upper = self.half_spans()
+        mine, to_x, to_y = self.mine, self.to_x, self.to_y
+        self.send(None, mine.at[base + self.diagonal_at, lower], self.half_y.at[turn], *at[0], to_y)
+        self.send(None, mine.at[base + self.diagonal_at, upper], self.half_x.at[turn], *at[1], to_x)
+        self.send(None, mine.at[base + self.x_at, upper], self.full_x.at[turn, upper], *at[2], to_x)
+        self.send(None, mine.at[base + self.y_at, lower], self.full_y.at[turn, lower], *at[3], to_y)
+
+    def second(self, turn):
+        base, at = PLANE * self.order[turn], self.turn_sems(turn)
+        height, lower, upper = self.half_spans()
+        mine, rows_of = self.mine, self.rows_of
+        self.arrive(None, self.half_y.at[turn], at[0][1])
+        self.add(None, height, rows_of(mine, base + self.x_at), rows_of(self.half_y, turn))
+        self.send(None, mine.at[base + self.x_at, lower], self.full_x.at[turn, lower], *at[4], self.to_x)
+        self.arrive(None, self.half_x.at[turn], at[1][1])
+        self.add(None, height, rows_of(mine, base + self.y_at, start=height), rows_of(self.half_x, turn))
+        self.send(None, mine.at[base + self.y_at, upper], self.full_y.at[turn, upper], *at[5], self.to_y)
+
+    def chain(self, which, turn, block, slots, spread):
+        to_level, level = self.order[turn], self.level
         rising, falling = to_level > level, to_level < level
         begins = (rising & (level == 0)) | (falling & (level == LEVELS - 1))
         middle = (rising | falling) & jnp.logical_not(begins)
-        arrive(middle, slots.at[to_level], chain_recv.at[which, to_level])
+        self.arrive(middle, slots.at[to_level], self.chain_recv.at[which, to_level])
         spread(middle, to_level)
-        outgoing = chain_send.at[which, to_level]
-        send(rising, block, slots.at[to_level], outgoing, chain_recv.at[which, to_level], up)
+        outgoing = self.chain_send.at[which, to_level]
+        self.send(rising, block, slots.at[to_level], outgoing, self.chain_recv.at[which, to_level], self.up)
         at = jnp.where(to_level == level - 1, LEVELS, to_level)
-        send(falling, block, slots.at[at], outgoing, chain_recv.at[which, at], down)
-
-    def add_small(condition, first, slot):
+        self.send(falling, block, slots.at[at], outgoing, self.chain_recv.at[which, at], self.down)
+
+    def add_small(self, condition, base, slot):
+        start, number = self.spans[2]
         for column in range(PLANE):
-            add(
+            self.add(
                 condition,
-                whole_b[1],
-                rows_of(mine, first + column, start=whole_b[0]),
-                rows_of(slots_b, slot, column),
+                number,
+                self.rows_of(self.mine, base + column, start=start),
+                self.rows_of(self.slots_b, slot, column),
             )
 
-    def chain_small(turn):
-        first = PLANE * order[turn]
-        block = mine.at[pl.ds(first, PLANE), pl.ds(*whole_b)]
-        chain(1, turn, block, slots_b, lambda condition, slot: add_small(condition, first, slot))
-
-    def plane_arrives(turn):
-        at, lower, upper = sems[turn], pl.ds(*half_a[0]), pl.ds(*half_a[1])
-        arrive(None, full_x.at[turn, upper], at[2][1])
-        arrive(None, full_y.at[turn, lower], at[3][1])
-        arrive(None, full_x.at[turn, lower], at[4][1])
-        arrive(None, full_y.at[turn, upper], at[5][1])
-
-    def chain_large(turn):
-        own = PLANE * order[turn] + own_at
-        plane_arrives(turn)
-        add(None, whole_a[1], rows_of(mine, own), rows_of(full_x, turn), rows_of(full_y, turn))
-        chain(
+    def chain_small(self, turn):
+        if turn == LEVELS - 1:
+            return
+        base = PLANE * self.order[turn]
+        block = self.mine.at[pl.ds(base, PLANE), pl.ds(*self.spans[2])]
+        self.chain(1, turn, block, self.slots_b, lambda condition, slot: self.add_small(condition, base, slot))
+
+    def plane_arrives(self, turn):
+        at = self.turn_sems(turn)
+        _, lower, upper = self.half_spans()
+        self.arrive(None, self.full_x.at[turn, upper], at[2][1])
+        self.arrive(None, self.full_y.at[turn, lower], at[3][1])
+        self.arrive(None, self.full_x.at[turn, lower], at[4][1])
+        self.arrive(None, self.full_y.at[turn, upper], at[5][1])
+
+    def chain_large(self, turn):
+        if turn == LEVELS - 1:
+            return
+        own, number = PLANE * self.order[turn] + self.own_at, self.spans[0][1]
+        rows_of, mine = self.rows_of, self.mine
+        self.plane_arrives(turn)
+        self.add(None, number, rows_of(mine, own), rows_of(self.full_x, turn), rows_of(self.full_y, turn))
+        self.chain(
             0,
             turn,
-            mine.at[own, pl.ds(*whole_a)],
-            slots_a,
-            lambda condition, slot: add(condition, whole_a[1], rows_of(mine, own), rows_of(slots_a, slot)),
+            mine.at[own, pl.ds(*self.spans[0])],
+            self.slots_a,
+            lambda condition, slot: self.add(condition, number, rows_of(mine, own), rows_of(self.slots_a, slot)),
         )
 
-    gain_partners = ((me, 1 - core), to_x, to_y, (me + PLANE - 2 * PLANE * (level % 2), core), (far, core))
+    def side(self):
+        short = self.spans[3][0][1]
+        spans = [pl.ds(0, short), pl.ds(short, short), pl.ds(2 * short, 2 * short), pl.ds(4 * short, 2 * short)]
+        return [(self.side_b.at[span], self.send_sem.at[24 + i], self.recv_sem.at[24 + i]) for i, span in enumerate(spans)]
+
+    def arrivals(self):
+        return ((self.level > 0, self.level), (self.level < LEVELS - 1, LEVELS))
+
+    def end_small(self):
+        base, mine, half_b = PLANE * self.level, self.mine, self.spans[3]
+        for condition, slot in self.arrivals():
+            self.arrive(condition, self.slots_b.at[slot], self.chain_recv.at[1, slot])
+            self.add_small(condition, base, slot)
+        side = self.side()
+        self.send(None, mine.at[base + self.diagonal_at, pl.ds(*half_b[0])], *side[0], self.to_y)
+        self.send(None, mine.at[base + self.diagonal_at, pl.ds(*half_b[1])], *side[1], self.to_x)
+
+    def end_sides(self):
+        base, mine, rows_of = PLANE * self.level, self.mine, self.rows_of
+        whole_b, half_b = self.spans[2:]
+        side, short = self.side(), half_b[0][1]
+        self.plane_arrives(LEVELS - 1)
+        self.arrive(None, side[0][0], side[0][2])
+        self.add(None, short, rows_of(mine, base + self.x_at, start=half_b[0][0]), rows_of(self.side_b))
+        self.send(None, mine.at[base + self.x_at, pl.ds(*whole_b)], *side[2], self.to_x)
+        self.arrive(None, side[1][0], side[1][2])
+        self.add(None, short, rows_of(mine, base + self.y_at, start=half_b[1][0]), rows_of(self.side_b, start=short))
+        self.send(None, mine.at[base + self.y_at, pl.ds(*whole_b)], *side[3], self.to_y)
+
+    def end_sums(self, base):
+        whole_a, half_a, whole_b, half_b = self.spans
+        own, out, mine, step = PLANE * self.level + self.own_at, self.out, self.mine, 16
+        full_x, full_y, slots_a, side_b = self.full_x, self.full_y, self.slots_a, self.side_b
+
+        def place(at):
+            return pl.ds(pl.multiple_of(base + at, step), step)
+
+        def tail_a(i, carry):
+            at = pl.multiple_of(i * step, step)
+            span, turn = pl.ds(at, step), LEVELS - 1
+            total = mine[own, span].astype(jnp.float32)
+            total = total + full_x[turn, span].astype(jnp.float32) + full_y[turn, span].astype(jnp.float32)
+            out[place(at)] = total
+            return carry
+
+        lax.fori_loop(0, whole_a[1] // step, tail_a, 0)
+        for condition, slot in self.arrivals():
+            self.arrive(condition, slots_a.at[slot], self.chain_recv.at[0, slot])
+
+            def more(slot=slot):
+                def body(i, carry):
+                    at = pl.multiple_of(i * step, step)
+                    out[place(at)] = out[place(at)] + slots_a[slot, pl.ds(at, step)].astype(jnp.float32)
+                    return carry
+
+                lax.fori_loop(0, whole_a[1] // step, body, 0)
+
+            when(condition, more)
+        side, short = self.side(), half_b[0][1]
+        self.arrive(None, side[2][0], side[2][2])
+        self.arrive(None, side[3][0], side[3][2])
+
+        def tail_b(i, carry):
+            at = pl.multiple_of(i * step, step)
+            total = mine[own, pl.ds(whole_b[0] + at, step)].astype(jnp.float32)
+            total = total + side_b[pl.ds(2 * short + at, step)].astype(jnp.float32)
+            total = total + side_b[pl.ds(4 * short + at, step)].astype(jnp.float32)
+            out[place(whole_b[0] + at)] = total
+            return carry
+
+        lax.fori_loop(0, whole_b[1] // step, tail_b, 0)
+
+    def end_waits(self):
+        for condition, copy in self.sent:
+            when(condition, lambda copy=copy: copy().wait_send())
+
+
+def scatter_places(blocks, rows, width):
+    near, far, low, dma = 3 * rows // 4, rows // 4, jnp.bfloat16, pltpu.SemaphoreType.DMA
+    shapes = [
+        (blocks, rows, width),
+        (LEVELS, near // 2, width),
+        (LEVELS, near // 2, width),
+        (LEVELS, near, width),
+        (LEVELS, near, width),
+        (LEVELS + 1, near, width),
+        (LEVELS + 1, PLANE, far, width),
+        (3 * far, width),
+    ]
+    return [pltpu.VMEM(shape, low) for shape in shapes] + [dma((28,)), dma((28,)), dma((2, 5)), dma((2, 5))]
+
+
+PLACES = 12
+
+
+def scatter_kernel(count, *refs):
+    pieces, gain_ref, out, gain_out = refs[:count], *refs[count : count + 3]
+    held, (load_sem, gain_slots, gain_send, gain_recv) = refs[count + 3 : -4], refs[-4:]
+    moves = scatter_moves(held, out)
+    me, core, level = moves.me, moves.core, moves.level
+    far = me + 2 * PLANE - 4 * PLANE * (level // 2)
+    greet(level, (moves.to_x[0], moves.to_y[0], far), True, me, core)
+    partners = ((me, 1 - core), moves.to_x, moves.to_y, (me + PLANE - 2 * PLANE * (level % 2), core), (far, core))
 
     def gain_copy(turn):
         return pltpu.make_async_remote_copy(
@@ -773,190 +796,262 @@
             gain_slots.at[2 * turn + 1],
             gain_send.at[turn],
             gain_recv.at[turn],
-            device_id=gain_partners[turn],
+            device_id=partners[turn],
             device_id_type=MESH,
         )
 
     def gain_step(turn):
-        if not gains:
-            return
         if turn == 0:
             gain_slots[0] = gain_ref[...]
         else:
             gain_copy(turn - 1).wait_recv()
             gain_slots[2 * turn] = gain_slots[2 * turn - 2] + gain_slots[2 * turn - 1]
-        if turn < len(gain_partners):
+        if turn < len(partners):
             gain_copy(turn).start()
         else:
             gain_out[...] = gain_slots[2 * turn]
 
-    if factors:
-        for i in range(factors):
-            right_copy(i).start()
-    for turn in turns:
-        for half in range(1 + paired):
-            for copy in load(half, turn):
-                copy.start()
-    if factors:
-        for i in range(factors):
-            right_copy(i).wait()
+    def load(turn):
+        copies, lane = [], 0
+        span = pl.ds(PLANE * moves.order[turn], PLANE)
+        for i, piece in enumerate(pieces):
+            place = moves.mine.at[span, :, pl.ds(lane, piece.shape[2])]
+            copies.append(pltpu.make_async_copy(piece.at[span], place, load_sem.at[i, turn]))
+            lane += piece.shape[2]
+        return copies
+
+    for turn in range(LEVELS):
+        for copy in load(turn):
+            copy.start()
     gain_step(0)
-    hand_over(0)
-    if paired:
-        hand_over(1)
-    for turn in turns:
-        settle(turn)
-        scatter_first(turn)
-        if turn < LEVELS - 1 and not paired:
-            chain_small(turn)
-        if turn + 2 < LEVELS:
-            hand_over(turn + 2)
-        if paired:
-            if turn < LEVELS - 1:
-                chain_small(turn)
-            if turn >= 1:
-                scatter_second(turn - 1)
-            if turn >= 2:
-                chain_large(turn - 2)
-    if not paired:
-        for turn in range(LEVELS - 1):
-            scatter_second(turn)
-            gain_step(turn + 1)
-            if turn:
-                chain_large(turn - 1)
-    scatter_second(LEVELS - 1)
+    for turn in range(LEVELS):
+        for copy in load(turn):
+            copy.wait()
+        moves.first(turn)
+        moves.chain_small(turn)
+    for turn in range(LEVELS - 1):
+        moves.second(turn)
+        gain_step(turn + 1)
+        if turn:
+            moves.chain_large(turn - 1)
+    moves.second(LEVELS - 1)
     gain_step(4)
-    chain_large(LEVELS - 2)
-
-    first = PLANE * level
-    own = first + own_at
-    arrivals = ((level > 0, level), (level < LEVELS - 1, LEVELS))
-    for condition, slot in arrivals:
-        arrive(condition, slots_b.at[slot], chain_recv.at[1, slot])
-        add_small(condition, first, slot)
-    side = [(send_sem.at[24 + i], recv_sem.at[24 + i]) for i in range(4)]
-    short = half_b[0][1]
-    spans = [pl.ds(0, short), pl.ds(short, short), pl.ds(2 * short, 2 * short), pl.ds(4 * short, 2 * short)]
-    send(None, mine.at[first + diagonal_at, pl.ds(*half_b[0])], side_b.at[spans[0]], *side[0], to_y)
-    send(None, mine.at[first + diagonal_at, pl.ds(*half_b[1])], side_b.at[spans[1]], *side[1], to_x)
-    plane_arrives(LEVELS - 1)
-    arrive(None, side_b.at[spans[0]], side[0][1])
-    add(None, short, rows_of(mine, first + x_at, start=half_b[0][0]), rows_of(side_b))
-    send(None, mine.at[first + x_at, pl.ds(*whole_b)], side_b.at[spans[2]], *side[2], to_x)
-    arrive(None, side_b.at[spans[1]], side[1][1])
-    add(None, short, rows_of(mine, first + y_at, start=half_b[1][0]), rows_of(side_b, start=short))
-    send(None, mine.at[first + y_at, pl.ds(*whole_b)], side_b.at[spans[3]], *side[3], to_y)
+    moves.chain_large(LEVELS - 2)
+    moves.end_small()
+    moves.end_sides()
     gain_step(5)
-    base = core * rows if paired else 0
-    step = 16
-
-    def tail_a(i, carry):
-        at = pl.multiple_of(i * step, step)
-        span = pl.ds(at, step)
-        total = mine[own, span].astype(jnp.float32)
-        total = total + full_x[LEVELS - 1, span].astype(jnp.float32) + full_y[LEVELS - 1, span].astype(jnp.float32)
-        out[pl.ds(pl.multiple_of(base + at, step), step)] = total
-        return carry
-
-    lax.fori_loop(0, whole_a[1] // step, tail_a, 0)
-    for condition, slot in arrivals:
-        arrive(condition, slots_a.at[slot], chain_recv.at[0, slot])
-
-        def more(slot=slot):
-            def body(i, carry):
-                at = pl.multiple_of(i * step, step)
-                span = pl.ds(pl.multiple_of(base + at, step), step)
-                out[span] = out[span] + slots_a[slot, pl.ds(at, step)].astype(jnp.float32)
-                return carry
-
-            lax.fori_loop(0, whole_a[1] // step, body, 0)
-
-        when(condition, more)
-    arrive(None, side_b.at[spans[2]], side[2][1])
-    arrive(None, side_b.at[spans[3]], side[3][1])
-
-    def tail_b(i, carry):
-        at = pl.multiple_of(i * step, step)
-        total = mine[own, pl.ds(whole_b[0] + at, step)].astype(jnp.float32)
-        total = total + side_b[pl.ds(2 * short + at, step)].astype(jnp.float32)
-        total = total + side_b[pl.ds(4 * short + at, step)].astype(jnp.float32)
-        out[pl.ds(pl.multiple_of(base + whole_b[0] + at, step), step)] = total
-        return carry
-
-    lax.fori_loop(0, whole_b[1] // step, tail_b, 0)
-    if paired:
-
-        def exchange(core_of_rows):
-            span = pl.ds(pl.multiple_of(core_of_rows * rows, rows), rows)
-            return pltpu.make_async_remote_copy(
-                out.at[span],
-                out.at[span],
-                ready_sem.at[0],
-                ready_sem.at[1],
-                device_id=(me, 1 - core),
-                device_id_type=MESH,
-            )
-
-        exchange(core).start()
-        exchange(1 - core).wait_recv()
-        exchange(core).wait_send()
-    if gains:
-        for turn in range(len(gain_partners)):
-            gain_copy(turn).wait_send()
-    for condition, copy in sent:
-        when(condition, lambda copy=copy: copy().wait_send())
-
-
-def scatter_sums(pieces, collective_id, away=(), product=None, gains=None):
-    paired, low = bool(away) or product is not None, jnp.bfloat16
-    operands, factors, turned, features = [], 0, False, 0
-    if product:
-        left, rights, turned = product
-        features, factors = rights[0].shape[0 if turned else 1], len(rights)
-        operands, (blocks, rows) = [left, *rights], left.shape[1:3]
-    else:
-        blocks, rows = pieces[0].shape[:2]
-    width = features + sum(piece.shape[2] for piece in pieces)
-    near, remote = 3 * rows // 4, rows // 4
+    moves.end_sums(0)
+    for turn in range(len(partners)):
+        gain_copy(turn).wait_send()
+    moves.end_waits()
+
+
+def scatter_sums(pieces, gains, collective_id):
+    blocks, rows = pieces[0].shape[:2]
+    width = sum(piece.shape[2] for piece in pieces)
     dma = pltpu.SemaphoreType.DMA
-    scratch = [
-        pltpu.VMEM((blocks, rows, width), low),
-        pltpu.VMEM((LEVELS, near // 2, width), low),
-        pltpu.VMEM((LEVELS, near // 2, width), low),
-        pltpu.VMEM((LEVELS, near, width), low),
-        pltpu.VMEM((LEVELS, near, width), low),
-        pltpu.VMEM((LEVELS + 1, near, width), low),
-        pltpu.VMEM((LEVELS + 1, PLANE, remote, width), low),
-        pltpu.VMEM((3 * remote, width), low),
-        *[dma((28,)), dma((28,)), dma((2, 5)), dma((2, 5)), dma((2, max(1, len(pieces)), LEVELS))],
-    ]
-    if paired:
-        whole = pltpu.VMEM((blocks, rows, width), low)
-        scratch += [whole, whole, dma((LEVELS,)), dma((LEVELS,)), dma((2,))]
-    if factors:
-        depth = left.shape[-1]
-        scratch += [pltpu.VMEM((features, depth) if turned else (depth, features), low), dma((factors,))]
     vmem, everywhere = pl.BlockSpec(memory_space=pltpu.VMEM), pl.BlockSpec(memory_space=pl.ANY)
-    operands += [*pieces, *away]
-    in_specs = [everywhere] * len(operands)
-    if factors:
-        in_specs[0] = vmem
-    shapes = [jax.ShapeDtypeStruct(((2 if paired else 1) * rows, width), jnp.float32)]
-    if gains is not None:
-        operands, in_specs = operands + [gains], in_specs + [vmem]
-        shapes.append(jax.ShapeDtypeStruct(gains.shape, gains.dtype))
-        scratch += [pltpu.VMEM((11, *gains.shape), gains.dtype), dma((5,)), dma((5,))]
-    plan = (paired, factors, turned, len(pieces), gains is not None)
     return pl.pallas_call(
-        functools.partial(scatter_kernel, plan),
-        out_shape=shapes,
-        in_specs=in_specs,
-        out_specs=[vmem] * len(shapes),
-        scratch_shapes=scratch,
+        functools.partial(scatter_kernel, len(pieces)),
+        out_shape=[
+            jax.ShapeDtypeStruct((rows, width), jnp.float32),
+            jax.ShapeDtypeStruct(gains.shape, gains.dtype),
+        ],
+        in_specs=[everywhere] * len(pieces) + [vmem],
+        out_specs=[vmem] * 2,
+        scratch_shapes=[
+            *scatter_places(blocks, rows, width),
+            dma((len(pieces), LEVELS)),
+            pltpu.VMEM((11, *gains.shape), gains.dtype),
+            dma((5,)),
+            dma((5,)),
+        ],
         compiler_params=pltpu.CompilerParams(
             collective_id=collective_id, has_side_effects=True, vmem_limit_bytes=60 * 1024 * 1024
         ),
-    )(*operands)
+    )(*pieces, gains)
+
+
+def return_kernel(grad_in, weighted, terms, w_gate, w_up, w_down, back_out, mixed_out, *refs):
+    streams = [
+        scatter_moves(refs[:PLACES], back_out),
+        scatter_moves(refs[PLACES : 2 * PLACES], mixed_out),
+    ]
+    sibling, away, left, right_in, right_down = refs[2 * PLACES : 2 * PLACES + 5]
+    pair_send, pair_recv, left_sem, right_sem, term_sem, ready_sem, credit = refs[2 * PLACES + 5 :]
+    me, core, order, rows = streams[0].me, streams[0].core, streams[0].order, streams[0].rows
+    greet(streams[0].level, (streams[0].to_x[0], streams[0].to_y[0]), True, me, core)
+    hidden, features = w_down.shape
+    depths, lefts = (2 * hidden, hidden), (grad_in, weighted)
+    turns, wide = 2 * LEVELS, 256
+    rights = [
+        pltpu.make_async_copy(w_gate, right_in.at[:, pl.ds(0, hidden)], right_sem.at[0]),
+        pltpu.make_async_copy(w_up, right_in.at[:, pl.ds(hidden, hidden)], right_sem.at[1]),
+        pltpu.make_async_copy(w_down, right_down, right_sem.at[2]),
+    ]
+
+    def level_span(turn):
+        return pl.ds(PLANE * order[turn % LEVELS], PLANE)
+
+    def left_copy(turn):
+        stream = turn // LEVELS
+        return pltpu.make_async_copy(
+            lefts[stream].at[:, level_span(turn)],
+            left.at[turn % 2, :, :, :, pl.ds(0, depths[stream])],
+            left_sem.at[turn % 2],
+        )
+
+    def term_copy(turn, half):
+        lanes = pl.ds(features, LANES)
+        place = away.at[turn % 2, :, :, lanes] if half else streams[0].mine.at[level_span(turn), :, lanes]
+        return pltpu.make_async_copy(terms.at[half, level_span(turn)], place, term_sem.at[half])
+
+    def width_of(turn):
+        return streams[turn // LEVELS].width
+
+    def hand(turn):
+        lanes = pl.ds(0, width_of(turn))
+        return pltpu.make_async_remote_copy(
+            away.at[turn % 2, :, :, lanes],
+            sibling.at[turn % 2, :, :, lanes],
+            pair_send.at[turn],
+            pair_recv.at[turn],
+            device_id=(me, 1 - core),
+            device_id_type=MESH,
+        )
+
+    def product(turn, half, store):
+        stream, slot = turn // LEVELS, turn % 2
+        factor = left[slot, half, :, :, pl.ds(0, depths[stream])].reshape(PLANE * rows, depths[stream])
+
+        def body(step, carry):
+            span = pl.ds(pl.multiple_of(step * wide, wide), wide)
+            value = dot_nt(factor, right_in[span]) if stream == 0 else dot_nn(factor, right_down[:, span])
+            store(span, value.reshape(PLANE, rows, wide))
+            return carry
+
+        lax.fori_loop(0, features // wide, body, 0)
+
+    def hand_over(turn):
+        left_copy(turn).wait()
+        if turn + 1 < turns:
+            left_copy(turn + 1).start()
+        if turn < LEVELS:
+            term_copy(turn, 1).start()
+            term_copy(turn, 0).start()
+
+        def store(span, value):
+            away[turn % 2, :, :, span] = value.astype(jnp.bfloat16)
+
+        product(turn, 1, store)
+        if turn < LEVELS:
+            term_copy(turn, 1).wait()
+            term_copy(turn, 0).wait()
+        if turn >= 2:
+            pl.semaphore_wait(credit, 1)
+        hand(turn).start()
+
+    def settle(turn):
+        hand(turn).wait()
+        mine, slot = streams[turn // LEVELS].mine, turn % 2
+
+        def store(span, value):
+            value = value + sibling[slot, :, :, span].astype(jnp.float32)
+            mine[level_span(turn), :, span] = value.astype(jnp.bfloat16)
+
+        product(turn, 0, store)
+        if turn < LEVELS:
+            lanes = pl.ds(features, LANES)
+            value = mine[level_span(turn), :, lanes].astype(jnp.float32)
+            value = value + sibling[slot, :, :, lanes].astype(jnp.float32)
+            mine[level_span(turn), :, lanes] = value.astype(jnp.bfloat16)
+        if turn + 2 < turns:
+            pl.semaphore_signal(credit, inc=1, device_id=(me, 1 - core), device_id_type=MESH)
+
+    def exchange(stream, core_of_rows):
+        out = streams[stream].out
+        span = pl.ds(pl.multiple_of(core_of_rows * rows, rows), rows)
+        return pltpu.make_async_remote_copy(
+            out.at[span],
+            out.at[span],
+            ready_sem.at[stream, 0],
+            ready_sem.at[stream, 1],
+            device_id=(me, 1 - core),
+            device_id_type=MESH,
+        )
+
+    def end(stream):
+        streams[stream].end_sums(core * rows)
+        exchange(stream, core).start()
+
+    left_copy(0).start()
+    for copy in rights:
+        copy.start()
+    for copy in rights:
+        copy.wait()
+    hand_over(0)
+    for turn in range(turns + 2):
+        if turn < turns:
+            stream = streams[turn // LEVELS]
+            settle(turn)
+            stream.first(turn % LEVELS)
+            if turn + 1 < turns:
+                hand_over(turn + 1)
+            stream.chain_small(turn % LEVELS)
+        if 1 <= turn <= turns:
+            streams[(turn - 1) // LEVELS].second((turn - 1) % LEVELS)
+        if turn >= 2:
+            streams[(turn - 2) // LEVELS].chain_large((turn - 2) % LEVELS)
+        if turn == LEVELS + 1:
+            streams[0].end_small()
+        if turn == LEVELS + 2:
+            streams[0].end_sides()
+        if turn == LEVELS + 3:
+            end(0)
+    streams[1].end_small()
+    streams[1].end_sides()
+    end(1)
+    for stream in range(2):
+        exchange(stream, 1 - core).wait_recv()
+        exchange(stream, core).wait_send()
+        streams[stream].end_waits()
+
+
+def return_sums(grad_in, weighted, terms, w_gate, w_up, w_down, collective_id):
+    low, dma = jnp.bfloat16, pltpu.SemaphoreType.DMA
+    blocks, rows, depth = grad_in.shape[1:]
+    hidden, features = w_down.shape
+    wide = features + LANES
+    vmem, everywhere = pl.BlockSpec(memory_space=pltpu.VMEM), pl.BlockSpec(memory_space=pl.ANY)
+    slots = pltpu.VMEM((2, PLANE, rows, wide), low)
+    return pl.pallas_call(
+        return_kernel,
+        out_shape=[
+            jax.ShapeDtypeStruct((2 * rows, wide), jnp.float32),
+            jax.ShapeDtypeStruct((2 * rows, features), jnp.float32),
+        ],
+        in_specs=[everywhere] * 6,
+        out_specs=[vmem] * 2,
+        scratch_shapes=[
+            *scatter_places(blocks, rows, wide),
+            *scatter_places(blocks, rows, features),
+            slots,
+            slots,
+            pltpu.VMEM((2, 2, PLANE, rows, depth), low),
+            pltpu.VMEM((features, depth), low),
+            pltpu.VMEM((hidden, features), low),
+            dma((2 * LEVELS,)),
+            dma((2 * LEVELS,)),
+            dma((2,)),
+            dma((3,)),
+            dma((2,)),
+            dma((2, 2)),
+            pltpu.SemaphoreType.REGULAR,
+        ],
+        compiler_params=pltpu.CompilerParams(
+            collective_id=collective_id, has_side_effects=True, vmem_limit_bytes=63 * 1024 * 1024
+        ),
+    )(grad_in, weighted, terms, w_gate, w_up, w_down)
 
 
 def kernels_fit():
@@ -1081,8 +1176,7 @@
     weighted, grad_in, terms, gate_term, up_term, down_term = experts_products(
         row_lanes, own_half(cotangent), w_gate, w_up, w_down, experts_all, 2
     )
-    (back,) = scatter_sums([terms[0]], 3, [terms[1]], (grad_in, (w_gate, w_up), True))
-    (mixed_rows,) = scatter_sums([], 4, [], (weighted, (w_down,), False))
+    back, mixed_rows = return_sums(grad_in, weighted, terms, w_gate, w_up, w_down, 3)
     term_lanes = back[:, model_width : model_width + 4 * experts_all]
     grad_gates = jnp.sum(term_lanes.reshape(sequence_length, 4, experts_all), axis=1)
     grad_logits = (
@@ -1314,7 +1408,7 @@
             term.astype(jnp.bfloat16).reshape(devices_gx, -1, term.shape[1])
             for term in (qkv_term, router_lanes, out_term)
         ]
-        sums, gain_rows = scatter_sums(pieces, 5, gains=packed_gains(gains))
+        sums, gain_rows = scatter_sums(pieces, packed_gains(gains), 4)
         gains = unpacked_gains(gain_rows, gains)
     else:
         sums = jnp.concatenate(

time: 805 us -> 772 us (0.959)
  Pallas kernels: 706 us -> 672 us
    pallas_call x3 -> x2, Pallas kernels: 354 us -> 320 us  [the longest x1 161 us: return_sums(): pl.pallas_call(return_kernel, out_shape=[jax.ShapeDtypeStruct((2 * rows,...]
where the time goes in v5:
time: 772 us; the launch traced here: 765 us
  Pallas kernels  672 us (87%)
  matrix products  46.6 us (6%)
  local copies, waits for them, and re-layouts  26.4 us (3%)
  other arithmetic  15.5 us (2%)
    pallas_call x1, Pallas kernels, experts_products(): pl.pallas_call(functools.partial(experts_kernel, experts_all), out_shape=...  169 us
    pallas_call x1, Pallas kernels, gather_blocks(): pl.pallas_call(functools.partial(gather_kernel, count, with_pair), out_sh...  163 us
    pallas_call x1, Pallas kernels, return_sums(): pl.pallas_call(return_kernel, out_shape=[jax.ShapeDtypeStruct((2 * rows,...  161 us
    pallas_call x1, Pallas kernels, scatter_sums(): pl.pallas_call(functools.partial(scatter_kernel, len(pieces)), out_shape=...  159 us
    dot_general x6, matrix products, contract(): lax.dot_general(first_op, second_op, (((first_dim,), (second_dim,)), ((),...  33 us
  transfers between devices with their start and end apart: 2, of which 1 were waited for; matrix products, arithmetic and copies ran while one was open for 2% of the time, Pallas kernels for 0%

profile of v5, /device:TPU:0, one launch (start us, length us, event | category | flops | bytes accessed | tf_op | source)
XLA Modules:
  0.0 765.3 jit_solution(18440580111490542992)
XLA Ops:
  6.7 162.6 %shard_map.263 = bf16[16,128,4736]{2,1,0:T(8,128)(2,1)} custom-call(bf16[128,4736]{1,0:T(8,128)(2,1)} %copy-done.19), custom_call_target="tpu_custom_call" | custom-call | tf_op jit(solution)/shard_map/pallas_call | solution.py:311
  169.5 5.7 fusion.2.raw_ref
  175.2 8.6 %shard_map.264 = (bf16[256,2048]{1,0:T(8,128)(2,1)S(1)}, bf16[256,2048]{1,0:T(8,128)(2,1)S(1)}, bf16[256,256]{1,0:T(8,128)(2,1)S(1)}, bf16[256,256]{1,0:T(8,128)(2,1)S(1)}, f32[16,256]{1,0:T(8,128)S(1)}) custom-call(f32[256,2560]{1,0:T(8,128)S(1)} %fusion.2.raw_ref, f32[256,128]{1,0:T(8,128)S(1)} %get-tuple-element.128.cosine_ref, ...), custom_call_target="tpu_custom_call" | custom-call | tf_op jit(solution)/shard_map/pallas_call | solution.py:1297
  183.9 7.8 %fusion.6 = f32[256,2048]{1,0:T(8,128)} fusion(bf16[256,2048]{1,0:T(8,128)(2,1)S(1)} %get-tuple-element.31, bf16[2048,4736]{1,0:T(8,128)(2,1)} %bitcast.42), kind=kOutput, calls=%fused_computation.8 | convolution fusion | flops 2147483648 | bytes 11534336 | tf_op jit(solution)/shard_map/dot_general | solution.py:40
  191.9 1.9 constant_dynamic-slice_fusion.refs_1_
  193.7 2.6 collective-permute-done
  196.3 2.6 multiply_reduce_fusion.2
  202.8 168.7 %shard_map.265 = (bf16[2,16,128,384]{3,2,1,0:T(8,128)(2,1)}, bf16[2,16,128,768]{3,2,1,0:T(8,128)(2,1)}, bf16[2,16,128,128]{3,2,1,0:T(8,128)(2,1)}, f32[2048,384]...) custom-call(bf16[128,2176]{1,0:T(8,128)(2,1)} %pad_maximum_fusion.re, ...), custom_call_target="tpu_custom_call" | custom-call | tf_op jit(solution)/shard_map/pallas_call | solution.py:532
  371.5 161.1 %shard_map.266 = (f32[256,2176]{1,0:T(8,128)}, f32[256,2048]{1,0:T(8,128)}) custom-call(bf16[2,16,128,768]{3,2,1,0:T(8,128)(2,1)} %get-tuple-element.32.grad_in, bf16[2,16,128,384]{3,2,1,0:T(8,128)(2,1)} %get-tuple-element.33.weighted, bf16[2,16,128,128]{3,2,1,0:T(8,128)(2,1)} %get-tuple-element.34.terms, bf16[2048,384]{1,0:T(8,128)(2,1)} %bitcast.48, ...), custom_call_target="tpu_custom_call" | custom-call | tf_op jit(solution)/shard_map/pallas_call | solution.py:1027
  533.7 3.4 multiply_reduce_fusion
  537.7 1.8 multiply_add_fusion
  539.5 6.5 fusion.12.grad_ref
  546.0 12.5 %shard_map.267 = (bf16[256,2560]{1,0:T(8,128)(2,1)S(1)}, f32[8,128]{1,0:T(8,128)S(1)}) custom-call(f32[256,2560]{1,0:T(8,128)} %copy-done, f32[256,128]{1,0:T(8,128)S(1)} %get-tuple-element.128.cosine_ref, f32[256,128]{1,0:T(8,128)S(1)} %get-tuple-element.129.sine_ref, s32[256,1]{1,0:T(8,128)S(1)} %copy.52.docs_column, s32[1,256]{1,0:T(1,128)S(1)} %copy-done.5, ...), custom_call_target="tpu_custom_call" | custom-call | tf_op jit(solution)/shard_map/pallas_call | solution.py:1312
  558.5 8.3 %fusion = f32[256,2048]{1,0:T(8,128)} fusion(bf16[256,2560]{1,0:T(8,128)(2,1)S(1)} %get-tuple-element.41, bf16[2048,4736]{1,0:T(8,128)(2,1)} %bitcast.46), kind=kOutput, calls=%fused_computation.1 | convolution fusion | flops 2684354560 | bytes 13893632 | tf_op jit(solution)/shard_map/dot_general | solution.py:40
  568.7 7.4 convolution_convert_fusion.1
  576.1 5.9 convolution_convert_fusion
  582.0 3.0 fusion.21
  585.6 158.8 %shard_map.268 = (f32[128,4736]{1,0:T(8,128)}, f32[40,128]{1,0:T(8,128)}) custom-call(bf16[16,128,2560]{2,1,0:T(8,128)(2,1)} %bitcast.39, bf16[16,128,128]{2,1,0:T(8,128)(2,1)} %bitcast.56, bf16[16,128,2048]{2,1,0:T(8,128)(2,1)} %bitcast.40, f32[40,128]{1,0:T(8,128)} %select_maximum_fusion.refs_3_), custom_call_target="tpu_custom_call" | custom-call | tf_op jit(solution)/shard_map/pallas_call | solution.py:854
  747.8 1.7 fusion.40
  749.5 3.2 fusion.39
  753.4 4.0 fusion.20
  757.4 1.7 copy.66
  760.4 1.7 copy.67
  763.4 1.7 copy.68
  (99 shorter events, 20.8 us)
Async XLA Ops:
  0.6 4.8 copy-start.25
  0.7 4.9 copy-start.26
  0.7 4.9 copy-start.22
  6.6 162.8 %copy-start.10 = (bf16[256,2048]{1,0:T(8,128)(2,1)S(1)}, bf16[256,2048]{1,0:T(8,128)(2,1)}, u32[]{:S(2)}) copy-start(bf16[256,2048]{1,0:T(8,128)(2,1)} %param.16) | copy-start | bytes 3145732
  6.6 162.8 %copy-start.23 = (f32[2048]{0:T(1024)S(1)}, f32[2048]{0:T(1024)}, u32[]{:S(2)}) copy-start(f32[2048]{0:T(1024)} %param.24) | copy-start | bytes 24580
  169.5 5.7 copy-start.5
  169.5 5.7 copy-start.6
  169.5 5.7 copy-start.7
  175.2 16.5 %copy-start = (f32[256,2560]{1,0:T(8,128)}, f32[256,2560]{1,0:T(8,128)S(1)}, u32[]{:S(2)}) copy-start(f32[256,2560]{1,0:T(8,128)S(1)} %fusion.2.raw_ref) | copy-start | bytes 7864324
  183.9 7.9 %copy-start.1 = (bf16[256,2048]{1,0:T(8,128)(2,1)}, bf16[256,2048]{1,0:T(8,128)(2,1)S(1)}, u32[]{:S(2)}) copy-start(bf16[256,2048]{1,0:T(8,128)(2,1)S(1)} %get-tuple-element.37.query_ref) | copy-start | bytes 3145732
  183.9 7.9 %copy-start.3 = (bf16[256,2048]{1,0:T(8,128)(2,1)}, bf16[256,2048]{1,0:T(8,128)(2,1)S(1)}, u32[]{:S(2)}) copy-start(bf16[256,2048]{1,0:T(8,128)(2,1)S(1)} %get-tuple-element.31) | copy-start | bytes 3145732
  183.9 7.9 %copy-start.27 = (s32[256,8]{0,1:T(8,128)S(1)}, s32[256,8]{0,1:T(8,128)}, u32[]{:S(2)}) copy-start(s32[256,8]{0,1:T(8,128)} %param.18) | copy-start | bytes 24580
  191.7 4.6 collective-permute-start
  193.7 5.2 copy-start.24
  533.7 3.4 copy-start.9
  533.7 3.4 copy-start.20
  533.7 4.0 copy-start.21
  539.5 6.5 copy-start.12
  539.5 6.5 copy-start.2
  558.5 8.7 %copy-start.15 = (bf16[256,2048]{1,0:T(8,128)(2,1)S(1)}, bf16[256,2048]{1,0:T(8,128)(2,1)}, u32[]{:S(2)}) copy-start(bf16[256,2048]{1,0:T(8,128)(2,1)} %copy-done.14) | copy-start | bytes 3145732
  566.8 15.1 %collective-permute-start.1 = (f32[256,2048]{1,0:T(8,128)}, f32[256,2048]{1,0:T(8,128)}, u32[]{:S(2)}, u32[]{:S(2)}) collective-permute-start(f32[256,2048]{1,0:T(8,128)} %fusion), channel_id=1, source_target_pairs={{0,1},{1,0},{2,3},{3,2},{4,5},{5,4},{6,7},{7,6},{8,9},{9,8},{10,11... | collective-permute-start | bytes 6291464 | tf_op jit(solution)/shard_map/ppermute | solution.py:1161
  568.7 7.4 copy-start.11
  749.5 3.9 copy-start.13
  753.4 4.0 copy-start.18
  (6 other events, 12.8 us)

commit v6 on v5

--- a/solution.py
+++ b/solution.py
@@ -781,9 +781,9 @@
 PLACES = 12
 
 
-def scatter_kernel(count, *refs):
-    pieces, gain_ref, out, gain_out = refs[:count], *refs[count : count + 3]
-    held, (load_sem, gain_slots, gain_send, gain_recv) = refs[count + 3 : -4], refs[-4:]
+def scatter_kernel(*refs):
+    normed, grad_qkv, router_term, grad_attn, attended, gain_ref, out, gain_out = refs[:8]
+    held, (load_sem, gain_slots, gain_send, gain_recv) = refs[8:-4], refs[-4:]
     moves = scatter_moves(held, out)
     me, core, level = moves.me, moves.core, moves.level
     far = me + 2 * PLANE - 4 * PLANE * (level // 2)
@@ -811,22 +811,35 @@
         else:
             gain_out[...] = gain_slots[2 * turn]
 
+    router_lane = grad_qkv.shape[1]
+
     def load(turn):
-        copies, lane = [], 0
         span = pl.ds(PLANE * moves.order[turn], PLANE)
-        for i, piece in enumerate(pieces):
-            place = moves.mine.at[span, :, pl.ds(lane, piece.shape[2])]
-            copies.append(pltpu.make_async_copy(piece.at[span], place, load_sem.at[i, turn]))
-            lane += piece.shape[2]
-        return copies
+        place = moves.mine.at[span, :, pl.ds(router_lane, LANES)]
+        return pltpu.make_async_copy(router_term.at[span], place, load_sem.at[turn])
+
+    def products(turn):
+        level_rows, wide = PLANE * moves.rows, 256
+        span = pl.ds(PLANE * moves.order[turn], PLANE)
+        features = pl.ds(pl.multiple_of(moves.order[turn] * level_rows, level_rows), level_rows)
+        for left, right, lane in ((normed, grad_qkv, 0), (grad_attn, attended, router_lane + LANES)):
+            left_rows = left[:, features].astype(jnp.float32).T.astype(jnp.bfloat16)
+
+            def body(step, carry, left_rows=left_rows, right=right, lane=lane):
+                at = pl.multiple_of(step * wide, wide)
+                value = dot_nn(left_rows, right[:, pl.ds(at, wide)]).astype(jnp.bfloat16)
+                lanes = pl.ds(pl.multiple_of(lane + at, LANES), wide)
+                moves.mine[span, :, lanes] = value.reshape(PLANE, moves.rows, wide)
+                return carry
+
+            lax.fori_loop(0, right.shape[1] // wide, body, 0)
 
     for turn in range(LEVELS):
-        for copy in load(turn):
-            copy.start()
+        load(turn).start()
     gain_step(0)
     for turn in range(LEVELS):
-        for copy in load(turn):
-            copy.wait()
+        products(turn)
+        load(turn).wait()
         moves.first(turn)
         moves.chain_small(turn)
     for turn in range(LEVELS - 1):
@@ -846,22 +859,22 @@
     moves.end_waits()
 
 
-def scatter_sums(pieces, gains, collective_id):
-    blocks, rows = pieces[0].shape[:2]
-    width = sum(piece.shape[2] for piece in pieces)
+def scatter_sums(normed, grad_qkv, router_term, grad_attn, attended, gains, collective_id):
+    blocks, rows, _ = router_term.shape
+    width = grad_qkv.shape[1] + LANES + attended.shape[1]
     dma = pltpu.SemaphoreType.DMA
     vmem, everywhere = pl.BlockSpec(memory_space=pltpu.VMEM), pl.BlockSpec(memory_space=pl.ANY)
     return pl.pallas_call(
-        functools.partial(scatter_kernel, len(pieces)),
+        scatter_kernel,
         out_shape=[
             jax.ShapeDtypeStruct((rows, width), jnp.float32),
             jax.ShapeDtypeStruct(gains.shape, gains.dtype),
         ],
-        in_specs=[everywhere] * len(pieces) + [vmem],
+        in_specs=[vmem, vmem, everywhere, vmem, vmem, vmem],
         out_specs=[vmem] * 2,
         scratch_shapes=[
             *scatter_places(blocks, rows, width),
-            dma((len(pieces), LEVELS)),
+            dma((LEVELS,)),
             pltpu.VMEM((11, *gains.shape), gains.dtype),
             dma((5,)),
             dma((5,)),
@@ -869,7 +882,7 @@
         compiler_params=pltpu.CompilerParams(
             collective_id=collective_id, has_side_effects=True, vmem_limit_bytes=60 * 1024 * 1024
         ),
-    )(*pieces, gains)
+    )(normed, grad_qkv, router_term, grad_attn, attended, gains)
 
 
 def return_kernel(grad_in, weighted, terms, w_gate, w_up, w_down, back_out, mixed_out, *refs):
@@ -1387,13 +1400,11 @@
     ffn_gain_term = jnp.sum(grad_ffn_in * unit_two, axis=0)
     grad_residual = grad_out_f + norm_back(grad_ffn_in * ffn_gain, unit_two, scale_two)
     grad_attn = grad_residual.astype(jnp.bfloat16)
-    out_term = contract(grad_attn, attended, 0, 0)
     grad_attended = jnp.dot(grad_attn, o_full, preferred_element_type=jnp.float32).astype(
         jnp.bfloat16
     )
     grad_qkv, head_gains = attend_back(shared, kept, grad_attended, heads_local, kv_local)
     q_gain_term, k_gain_term = head_gains[0], head_gains[1]
-    qkv_term = contract(normalized_input, grad_qkv, 0, 0)
     grad_normed_part = contract(grad_qkv, qkv_full, 1, 1)
     grad_normed = grad_normed_part + swap_cores(grad_normed_part)
     attn_gain_term = jnp.sum(grad_normed * unit_one, axis=0)
@@ -1404,17 +1415,20 @@
     gains = (attn_gain_term * own_mask, ffn_gain_term * own_mask, q_gain_term, k_gain_term)
     router_lanes = jnp.pad(router_term, ((0, 0), (0, LANES - experts_all)))
     if dense:
-        pieces = [
-            term.astype(jnp.bfloat16).reshape(devices_gx, -1, term.shape[1])
-            for term in (qkv_term, router_lanes, out_term)
-        ]
-        sums, gain_rows = scatter_sums(pieces, packed_gains(gains), 4)
+        router_blocks = router_lanes.astype(jnp.bfloat16).reshape(devices_gx, -1, LANES)
+        sums, gain_rows = scatter_sums(
+            normalized_input, grad_qkv, router_blocks, grad_attn, attended, packed_gains(gains), 4
+        )
         gains = unpacked_gains(gain_rows, gains)
     else:
         sums = jnp.concatenate(
             [
                 lax.psum_scatter(term, "gx", scatter_dimension=0, tiled=True)
-                for term in (qkv_term, router_lanes, out_term)
+                for term in (
+                    contract(normalized_input, grad_qkv, 0, 0),
+                    router_lanes,
+                    contract(grad_attn, attended, 0, 0),
+                )
             ],
             axis=1,
         )

time: 772 us -> 765 us (level)
  matrix products: 46.6 us -> 31.1 us
    dot_general x6 -> x4, matrix products: 33 us -> 17.6 us  [contract(): lax.dot_general(first_op, second_op, (((first_dim,), (second_dim,)), ((),...]
  transfers between devices with their start and end apart: 2 -> 2, of which waited for: 1 -> 2; matrix products, arithmetic and copies ran while one was open for 2% -> 1% of each run, Pallas kernels for 0% -> 0%
where the time goes in v6:
time: 765 us; the launch traced here: 759 us
  Pallas kernels  677 us (88%)
  matrix products  31.1 us (4%)
  local copies, waits for them, and re-layouts  28.9 us (4%)
  other arithmetic  16.6 us (2%)
    pallas_call x1, Pallas kernels, experts_products(): pl.pallas_call(functools.partial(experts_kernel, experts_all), out_shape=...  168 us
    pallas_call x1, Pallas kernels, scatter_sums(): pl.pallas_call(scatter_kernel, out_shape=[jax.ShapeDtypeStruct((rows, wid...  163 us
    pallas_call x1, Pallas kernels, gather_blocks(): pl.pallas_call(functools.partial(gather_kernel, count, with_pair), out_sh...  163 us
    pallas_call x1, Pallas kernels, return_sums(): pl.pallas_call(return_kernel, out_shape=[jax.ShapeDtypeStruct((2 * rows,...  161 us
    dot_general x4, matrix products, contract(): lax.dot_general(first_op, second_op, (((first_dim,), (second_dim,)), ((),...  17.6 us
  transfers between devices with their start and end apart: 2, of which 2 were waited for; matrix products, arithmetic and copies ran while one was open for 1% of the time, Pallas kernels for 0%

profile of v6, /device:TPU:0, one launch (start us, length us, event | category | flops | bytes accessed | tf_op | source)
XLA Modules:
  0.0 758.8 jit_solution(12013217567638249538)
XLA Ops:
  0.7 1.6 fusion.22
  6.7 162.6 %shard_map.263 = bf16[16,128,4736]{2,1,0:T(8,128)(2,1)} custom-call(bf16[128,4736]{1,0:T(8,128)(2,1)} %copy-done.23), custom_call_target="tpu_custom_call" | custom-call | tf_op jit(solution)/shard_map/pallas_call | solution.py:311
  169.7 6.0 fusion.2.raw_ref
  175.9 8.6 %shard_map.264 = (bf16[256,2048]{1,0:T(8,128)(2,1)S(1)}, bf16[256,2048]{1,0:T(8,128)(2,1)S(1)}, bf16[256,256]{1,0:T(8,128)(2,1)S(1)}, bf16[256,256]{1,0:T(8,128)(2,1)S(1)}, f32[16,256]{1,0:T(8,128)S(1)}) custom-call(f32[256,2560]{1,0:T(8,128)S(1)} %fusion.2.raw_ref, f32[256,128]{1,0:T(8,128)S(1)} %get-tuple-element.128.cosine_ref, ...), custom_call_target="tpu_custom_call" | custom-call | tf_op jit(solution)/shard_map/pallas_call | solution.py:1310
  184.6 7.8 %fusion.6 = f32[256,2048]{1,0:T(8,128)} fusion(bf16[256,2048]{1,0:T(8,128)(2,1)S(1)} %get-tuple-element.31.refs_4_, bf16[2048,4736]{1,0:T(8,128)(2,1)} %bitcast.38), kind=kOutput, calls=%fused_computation.6 | convolution fusion | flops 2147483648 | bytes 11534336 | tf_op jit(solution)/shard_map/dot_general | solution.py:40
  192.5 1.9 constant_dynamic-slice_fusion.refs_1_
  194.4 2.6 collective-permute-done
  197.0 2.6 multiply_reduce_fusion.2
  200.9 1.5 fusion.38
  203.4 168.4 %shard_map.265 = (bf16[2,16,128,384]{3,2,1,0:T(8,128)(2,1)}, bf16[2,16,128,768]{3,2,1,0:T(8,128)(2,1)}, bf16[2,16,128,128]{3,2,1,0:T(8,128)(2,1)}, f32[2048,384]...) custom-call(bf16[128,2176]{1,0:T(8,128)(2,1)} %pad_maximum_fusion.re, ...), custom_call_target="tpu_custom_call" | custom-call | tf_op jit(solution)/shard_map/pallas_call | solution.py:532
  371.8 161.2 %shard_map.266 = (f32[256,2176]{1,0:T(8,128)}, f32[256,2048]{1,0:T(8,128)}) custom-call(bf16[2,16,128,768]{3,2,1,0:T(8,128)(2,1)} %get-tuple-element.32.grad_in, bf16[2,16,128,384]{3,2,1,0:T(8,128)(2,1)} %get-tuple-element.33.weighted, bf16[2,16,128,128]{3,2,1,0:T(8,128)(2,1)} %get-tuple-element.34.terms, bf16[2048,384]{1,0:T(8,128)(2,1)} %bitcast.44, ...), custom_call_target="tpu_custom_call" | custom-call | tf_op jit(solution)/shard_map/pallas_call | solution.py:1040
  534.1 3.4 multiply_reduce_fusion
  539.5 6.1 fusion.12.grad_ref
  545.7 12.5 %shard_map.267 = (bf16[256,2560]{1,0:T(8,128)(2,1)S(1)}, f32[8,128]{1,0:T(8,128)S(1)}) custom-call(f32[256,2560]{1,0:T(8,128)} %copy-done, f32[256,128]{1,0:T(8,128)S(1)} %get-tuple-element.128.cosine_ref, f32[256,128]{1,0:T(8,128)S(1)} %get-tuple-element.129.sine_ref, s32[256,1]{1,0:T(8,128)S(1)} %copy.52.docs_column, s32[1,256]{1,0:T(1,128)S(1)} %copy-done.5, ...), custom_call_target="tpu_custom_call" | custom-call | tf_op jit(solution)/shard_map/pallas_call | solution.py:1325
  558.2 6.1 fusion
  566.1 1.9 pad.19.clone
  568.7 2.5 fusion.21
  571.9 163.3 %shard_map.268 = (f32[128,4736]{1,0:T(8,128)}, f32[40,128]{1,0:T(8,128)}) custom-call(bf16[256,2048]{1,0:T(8,128)(2,1)} %copy-done.18, bf16[256,2560]{1,0:T(8,128)(2,1)} %copy-done.1, bf16[16,128,128]{2,1,0:T(8,128)(2,1)} %bitcast.52, bf16[256,2048]{1,0:T(8,128)(2,1)} %copy-done.19, bf16[256,2048]{1,0:T(8,128)(2,1)} %copy-done.4, ...), custom_call_target="tpu_custom_call" | custom-call | tf_op jit(solution)/shard_map/pallas_call | solution.py:867
  738.6 1.7 fusion.37
  740.3 3.2 fusion.36
  744.2 6.4 fusion.20
  750.6 1.7 copy.66
  753.7 1.7 copy.67
  756.7 1.7 copy.68
  (102 shorter events, 20.1 us)
Async XLA Ops:
  0.6 4.8 copy-start.27
  0.7 4.9 copy-start.28
  0.7 4.9 copy-start.24
  6.6 162.7 %copy-start.11 = (bf16[256,2048]{1,0:T(8,128)(2,1)S(1)}, bf16[256,2048]{1,0:T(8,128)(2,1)}, u32[]{:S(2)}) copy-start(bf16[256,2048]{1,0:T(8,128)(2,1)} %param.16) | copy-start | bytes 3145732
  6.7 162.7 %copy-start.26 = (f32[2048]{0:T(1024)S(1)}, f32[2048]{0:T(1024)}, u32[]{:S(2)}) copy-start(f32[2048]{0:T(1024)} %param.24) | copy-start | bytes 24580
  169.6 6.0 copy-start.18
  169.6 6.2 copy-start.5
  169.7 6.2 copy-start.6
  169.7 6.2 copy-start.7
  175.7 16.7 %copy-start = (f32[256,2560]{1,0:T(8,128)}, f32[256,2560]{1,0:T(8,128)S(1)}, u32[]{:S(2)}) copy-start(f32[256,2560]{1,0:T(8,128)S(1)} %fusion.2.raw_ref) | copy-start | bytes 7864324
  184.5 7.9 %copy-start.2 = (bf16[256,2048]{1,0:T(8,128)(2,1)}, bf16[256,2048]{1,0:T(8,128)(2,1)S(1)}, u32[]{:S(2)}) copy-start(bf16[256,2048]{1,0:T(8,128)(2,1)S(1)} %get-tuple-element.37.query_ref) | copy-start | bytes 3145732
  184.5 7.9 %copy-start.4 = (bf16[256,2048]{1,0:T(8,128)(2,1)}, bf16[256,2048]{1,0:T(8,128)(2,1)S(1)}, u32[]{:S(2)}) copy-start(bf16[256,2048]{1,0:T(8,128)(2,1)S(1)} %get-tuple-element.31.refs_4_) | copy-start | bytes 3145732
  184.5 7.9 %copy-start.29 = (s32[256,8]{0,1:T(8,128)S(1)}, s32[256,8]{0,1:T(8,128)}, u32[]{:S(2)}) copy-start(s32[256,8]{0,1:T(8,128)} %param.18) | copy-start | bytes 24580
  192.4 4.6 collective-permute-start
  194.4 5.2 copy-start.25
  534.1 4.7 copy-start.9
  534.1 4.7 copy-start.17
  539.5 6.1 copy-start.19
  539.5 6.1 copy-start.3
  558.2 6.1 copy-start.1
  558.2 6.6 copy-start.15
  564.3 6.9 copy-start.16
  564.3 4.4 collective-permute-start.1
  744.2 6.4 copy-start.22
  (8 other events, 20.5 us)

commit v7 on v6

--- a/solution.py
+++ b/solution.py
@@ -120,6 +120,8 @@
         self.up, self.down = (self.me + PLANE, self.core), (self.me - PLANE, self.core)
         self.to_x, self.to_y = (self.x_side, self.core), (self.y_side, self.core)
         self.sent, self.mirrored, self.everyone = [], [], range(len(ins))
+        for k in self.everyone:
+            self.own_copy(k).start()
         greet(self.level, (self.x_side, self.y_side), any(p is not None for p in pairs), self.me, self.core)
         self.order = [
             self.start,
@@ -207,7 +209,6 @@
         whole_a, half_a, whole_b, half_b = self.spans
         last, me = self.last, self.me
         for k in self.everyone:
-            self.own_copy(k).start()
             self.send(None, k, last, "own", me, 1, whole_b, self.to_x)
             self.send(None, k, last + 1, "own", me, 1, whole_b, self.to_y)
             self.send(self.has_up, k, 0, "own", me, 1, whole_a, self.up)
@@ -331,11 +332,17 @@
     weighted_out, grad_in_out, terms_out, gate_out, up_out, down_out, grads_own, grads_pair = refs[5:13]
     held, grads, w_in, left_in, left_down, weighted_ref, grad_in_ref, terms_ref = refs[13:21]
     sums_in, sums_down, turned, grad_sem, w_sem, out_sem, sum_sem = refs[21:28]
+    hidden, width = w_down.shape
+    joins = [
+        pltpu.make_async_copy(part, w_in.at[:, pl.ds(i * hidden, hidden)], w_sem.at[i])
+        for i, part in enumerate((w_gate, w_up))
+    ]
+    for join in joins:
+        join.start()
     steps = gather_steps(
         [rows_ref, grad_rows_ref], [held.at[0], grads_own], [held.at[1], grads_pair], refs[28:]
     )
     level, core = steps.level, steps.core
-    hidden, width = w_down.shape
     tiles = hidden // LANES
     rows = rows_ref.shape[0]
     visits = [
@@ -356,10 +363,6 @@
         fetch(turn, 0).start()
         fetch(turn, 1).start()
 
-    joins = [
-        pltpu.make_async_copy(part, w_in.at[:, pl.ds(i * hidden, hidden)], w_sem.at[i])
-        for i, part in enumerate((w_gate, w_up))
-    ]
     lane = lax.broadcasted_iota(jnp.int32, (1, LANES), 1)
     expert = steps.me
     gate_pick = (((lane == expert) | (lane == experts_all + expert))).astype(jnp.float32)
@@ -466,8 +469,6 @@
         fetch_start(turn)
 
     steps.start()
-    for join in joins:
-        join.start()
     steps.side_small()
     steps.column(1)
     steps.cross(0)
@@ -782,12 +783,13 @@
 
 
 def scatter_kernel(*refs):
-    normed, grad_qkv, router_term, grad_attn, attended, gain_ref, out, gain_out = refs[:8]
-    held, (load_sem, gain_slots, gain_send, gain_recv) = refs[8:-4], refs[-4:]
+    normed, grad_qkv, router_term, grad_attn, attended, gain_ref = refs[:6]
+    tokens, grad_residual, grad_normed, attn_gain = refs[6:10]
+    pieces_out, (gain_out, grad_input) = refs[10:15], refs[15:17]
+    held, (out, load_sem, leave_sem, gain_slots, gain_send, gain_recv) = refs[17:-6], refs[-6:]
     moves = scatter_moves(held, out)
     me, core, level = moves.me, moves.core, moves.level
     far = me + 2 * PLANE - 4 * PLANE * (level // 2)
-    greet(level, (moves.to_x[0], moves.to_y[0], far), True, me, core)
     partners = ((me, 1 - core), moves.to_x, moves.to_y, (me + PLANE - 2 * PLANE * (level % 2), core), (far, core))
 
     def gain_copy(turn):
@@ -834,14 +836,39 @@
 
             lax.fori_loop(0, right.shape[1] // wide, body, 0)
 
+    def input_rows():
+        step = 16
+
+        def body(i, carry):
+            span = pl.ds(pl.multiple_of(i * step, step), step)
+            unit, scale = unit_rows(tokens[span].astype(jnp.float32))
+            grad = grad_normed[span] * attn_gain[...]
+            grad = scale * (grad - unit * jnp.mean(grad * unit, axis=1, keepdims=True))
+            grad_input[span] = (grad_residual[span] + grad).astype(jnp.bfloat16)
+            return carry
+
+        lax.fori_loop(0, tokens.shape[0] // step, body, 0)
+
+    def leave():
+        copies, lane = [], 0
+        for i, piece in enumerate(pieces_out):
+            width = piece.shape[1]
+            copies.append(pltpu.make_async_copy(out.at[:, pl.ds(lane, width)], piece, leave_sem.at[i]))
+            lane += width
+        return copies
+
     for turn in range(LEVELS):
         load(turn).start()
+    products(0)
+    greet(level, (moves.to_x[0], moves.to_y[0], far), True, me, core)
     gain_step(0)
     for turn in range(LEVELS):
-        products(turn)
+        if turn:
+            products(turn)
         load(turn).wait()
         moves.first(turn)
         moves.chain_small(turn)
+    input_rows()
     for turn in range(LEVELS - 1):
         moves.second(turn)
         gain_step(turn + 1)
@@ -854,35 +881,43 @@
     moves.end_sides()
     gain_step(5)
     moves.end_sums(0)
+    for copy in leave():
+        copy.start()
     for turn in range(len(partners)):
         gain_copy(turn).wait_send()
     moves.end_waits()
-
-
-def scatter_sums(normed, grad_qkv, router_term, grad_attn, attended, gains, collective_id):
+    for copy in leave():
+        copy.wait()
+
+
+def scatter_sums(factors, gains, lasts, kv_width, collective_id):
+    _, grad_qkv, router_term, _, attended = factors
     blocks, rows, _ = router_term.shape
-    width = grad_qkv.shape[1] + LANES + attended.shape[1]
-    dma = pltpu.SemaphoreType.DMA
+    widths = (grad_qkv.shape[1] - 2 * kv_width, kv_width, kv_width, LANES, attended.shape[1])
+    dma, tokens = pltpu.SemaphoreType.DMA, lasts[0]
     vmem, everywhere = pl.BlockSpec(memory_space=pltpu.VMEM), pl.BlockSpec(memory_space=pl.ANY)
     return pl.pallas_call(
         scatter_kernel,
         out_shape=[
-            jax.ShapeDtypeStruct((rows, width), jnp.float32),
+            *[jax.ShapeDtypeStruct((rows, width), jnp.float32) for width in widths],
             jax.ShapeDtypeStruct(gains.shape, gains.dtype),
+            jax.ShapeDtypeStruct(tokens.shape, tokens.dtype),
         ],
-        in_specs=[vmem, vmem, everywhere, vmem, vmem, vmem],
-        out_specs=[vmem] * 2,
+        in_specs=[vmem, vmem, everywhere, vmem, vmem, vmem, vmem, vmem, vmem, vmem],
+        out_specs=[everywhere] * 5 + [vmem] * 2,
         scratch_shapes=[
-            *scatter_places(blocks, rows, width),
+            *scatter_places(blocks, rows, sum(widths)),
+            pltpu.VMEM((rows, sum(widths)), jnp.float32),
             dma((LEVELS,)),
+            dma((5,)),
             pltpu.VMEM((11, *gains.shape), gains.dtype),
             dma((5,)),
             dma((5,)),
         ],
         compiler_params=pltpu.CompilerParams(
-            collective_id=collective_id, has_side_effects=True, vmem_limit_bytes=60 * 1024 * 1024
+            collective_id=collective_id, has_side_effects=True, vmem_limit_bytes=63 * 1024 * 1024
         ),
-    )(normed, grad_qkv, router_term, grad_attn, attended, gains)
+    )(*factors, gains, *lasts)
 
 
 def return_kernel(grad_in, weighted, terms, w_gate, w_up, w_down, back_out, mixed_out, *refs):
@@ -893,7 +928,6 @@
     sibling, away, left, right_in, right_down = refs[2 * PLACES : 2 * PLACES + 5]
     pair_send, pair_recv, left_sem, right_sem, term_sem, ready_sem, credit = refs[2 * PLACES + 5 :]
     me, core, order, rows = streams[0].me, streams[0].core, streams[0].order, streams[0].rows
-    greet(streams[0].level, (streams[0].to_x[0], streams[0].to_y[0]), True, me, core)
     hidden, features = w_down.shape
     depths, lefts = (2 * hidden, hidden), (grad_in, weighted)
     turns, wide = 2 * LEVELS, 256
@@ -960,6 +994,8 @@
         if turn < LEVELS:
             term_copy(turn, 1).wait()
             term_copy(turn, 0).wait()
+        if turn == 0:
+            greet(streams[0].level, (streams[0].to_x[0], streams[0].to_y[0]), True, me, core)
         if turn >= 2:
             pl.semaphore_wait(credit, 1)
         hand(turn).start()
@@ -1217,10 +1253,51 @@
     return pl.ds(pl.multiple_of(head * HEAD_DIM, HEAD_DIM), HEAD_DIM)
 
 
+def weight_copies(w_ref, w_in, w_out, w_sem, wide, last_first):
+    groups = list(range(w_in.shape[1] // wide))
+    if last_first:
+        groups = groups[-1:] + groups[:-1]
+    into = [
+        (n, pltpu.make_async_copy(w_ref.at[:, pl.ds(n * wide, wide)], w_in.at[:, pl.ds(n * wide, wide)], w_sem.at[n]))
+        for n in groups
+    ]
+    start = w_in.shape[1] + LANES
+    out = [
+        pltpu.make_async_copy(
+            w_ref.at[:, pl.ds(start + n * wide, wide)],
+            w_out.at[:, pl.ds(n * wide, wide)],
+            w_sem.at[len(groups) + n],
+        )
+        for n in range(w_out.shape[1] // wide)
+    ]
+    return into, out
+
+
+def dot_groups(target, left, right, begin, count, transposed, wide=256):
+    def body(i, carry):
+        span = pl.ds(pl.multiple_of(begin + i * wide, wide), wide)
+        value = dot_nt(left[...], right[span]) if transposed else dot_nn(left[...], right[:, span])
+        target[:, span] = value.astype(target.dtype)
+        return carry
+
+    lax.fori_loop(0, count // wide, body, 0)
+
+
+GROUP = 512
+
+
 def attend_kernel(
-    q_heads, kv_heads, raw_ref, cosine_ref, sine_ref, docs_column, docs_row, q_gain, k_gain,
-    attended_ref, query_ref, key_ref, value_ref, totals_ref,
+    q_heads, kv_heads, normed_ref, w_ref, cosine_ref, sine_ref, docs_column, docs_row, q_gain, k_gain,
+    raw_ref, attended_ref, query_ref, key_ref, value_ref, totals_ref, part_ref, w_in, w_out, w_sem,
 ):
+    into, out = weight_copies(w_ref, w_in, w_out, w_sem, GROUP, True)
+    for _, copy in into:
+        copy.start()
+    for copy in out:
+        copy.start()
+    for n, copy in into:
+        copy.wait()
+        dot_groups(raw_ref, normed_ref, w_in, n * GROUP, GROUP, False)
     cosine, sine_table = cosine_ref[...], sine_ref[...]
     allowed = allowed_pairs(docs_column[...], docs_row[...])
     group, inv_root = q_heads // kv_heads, 1.0 / math.sqrt(HEAD_DIM)
@@ -1247,12 +1324,24 @@
             return carry
 
         lax.fori_loop(0, group, body, 0, unroll=2)
+    for copy in out:
+        copy.wait()
+    dot_groups(part_ref, attended_ref, w_out, 0, w_out.shape[0], True)
 
 
 def attend_back_kernel(
-    q_heads, kv_heads, raw_ref, cosine_ref, sine_ref, docs_column, docs_row, q_gain, k_gain,
-    query_ref, key_ref, value_ref, totals_ref, grad_ref, grad_raw_ref, gains_ref, sums_ref,
+    q_heads, kv_heads, grad_attn_ref, w_ref, cosine_ref, sine_ref, docs_column, docs_row, q_gain, k_gain,
+    raw_ref, query_ref, key_ref, value_ref, totals_ref,
+    grad_raw_ref, gains_ref, part_ref, grad_ref, sums_ref, w_in, w_out, w_sem,
 ):
+    into, out = weight_copies(w_ref, w_in, w_out, w_sem, GROUP, False)
+    for copy in out:
+        copy.start()
+    for _, copy in into:
+        copy.start()
+    for n, copy in enumerate(out):
+        copy.wait()
+        dot_groups(grad_ref, grad_attn_ref, w_out, n * GROUP, GROUP, False)
     cosine, sine_table = cosine_ref[...], sine_ref[...]
     allowed = allowed_pairs(docs_column[...], docs_row[...])
     group, inv_root = q_heads // kv_heads, 1.0 / math.sqrt(HEAD_DIM)
@@ -1288,14 +1377,17 @@
         lax.fori_loop(0, group, body, 0, unroll=2)
         back_to_raw(sums_ref[1] * inv_root, q_heads + kv, k_gain[...], 1)
         grad_raw_ref[:, head_span(q_heads + kv_heads + kv)] = sums_ref[0].astype(jnp.bfloat16)
-
-
-def attention_shared(qkv_rows, doc_ids, query_norm_gain, k_gain):
-    length = qkv_rows.shape[0]
+    for _, copy in into:
+        copy.wait()
+    dot_groups(part_ref, grad_raw_ref, w_in, 0, w_in.shape[0], True)
+
+
+def attention_shared(weights_all, doc_ids, query_norm_gain, k_gain):
+    length = doc_ids.shape[1]
     cosine, sine_table = rotary_tables(length, HEAD_DIM)
     cosine, sine_table = cosine[:, 0], sine_table[:, 0]
     return (
-        qkv_rows,
+        weights_all,
         jnp.concatenate([cosine, cosine], axis=1),
         jnp.concatenate([-sine_table, sine_table], axis=1),
         doc_ids.reshape(length, 1),
@@ -1305,29 +1397,55 @@
     )
 
 
-def attend(shared, q_heads, kv_heads):
-    length, low, shape = shared[0].shape[0], jnp.bfloat16, jax.ShapeDtypeStruct
+def attention_specs(q_heads, kv_heads, features, inputs):
+    vmem, everywhere = pl.BlockSpec(memory_space=pltpu.VMEM), pl.BlockSpec(memory_space=pl.ANY)
+    wide, out_wide = (q_heads + 2 * kv_heads) * HEAD_DIM, q_heads * HEAD_DIM
+    scratch = [
+        pltpu.VMEM((features, wide), jnp.bfloat16),
+        pltpu.VMEM((features, out_wide), jnp.bfloat16),
+        pltpu.SemaphoreType.DMA(((wide + out_wide) // GROUP,)),
+    ]
+    return [vmem, everywhere] + [vmem] * (inputs - 2), scratch
+
+
+def attend(normed, shared, q_heads, kv_heads):
+    (length, features), low, shape = normed.shape, jnp.bfloat16, jax.ShapeDtypeStruct
+    in_specs, scratch = attention_specs(q_heads, kv_heads, features, 1 + len(shared))
     return pl.pallas_call(
         functools.partial(attend_kernel, q_heads, kv_heads),
         out_shape=[
+            shape((length, (q_heads + 2 * kv_heads) * HEAD_DIM), jnp.float32),
             shape((length, q_heads * HEAD_DIM), low),
             shape((length, q_heads * HEAD_DIM), low),
             shape((length, kv_heads * HEAD_DIM), low),
             shape((length, kv_heads * HEAD_DIM), low),
             shape((q_heads, length), jnp.float32),
+            shape((length, features), jnp.float32),
+        ],
+        in_specs=in_specs,
+        scratch_shapes=scratch,
+        compiler_params=pltpu.CompilerParams(vmem_limit_bytes=48 * 1024 * 1024),
+    )(normed, *shared)
+
+
+def attend_back(grad_attn, shared, kept, q_heads, kv_heads):
+    (length, features), shape = grad_attn.shape, jax.ShapeDtypeStruct
+    in_specs, scratch = attention_specs(q_heads, kv_heads, features, 1 + len(shared) + len(kept))
+    return pl.pallas_call(
+        functools.partial(attend_back_kernel, q_heads, kv_heads),
+        out_shape=[
+            shape((length, (q_heads + 2 * kv_heads) * HEAD_DIM), jnp.bfloat16),
+            shape((8, HEAD_DIM), jnp.float32),
+            shape((length, features), jnp.float32),
+        ],
+        in_specs=in_specs,
+        scratch_shapes=[
+            pltpu.VMEM((length, q_heads * HEAD_DIM), jnp.bfloat16),
+            pltpu.VMEM((2, length, HEAD_DIM), jnp.float32),
+            *scratch,
         ],
         compiler_params=pltpu.CompilerParams(vmem_limit_bytes=48 * 1024 * 1024),
-    )(*shared)
-
-
-def attend_back(shared, kept, grad_attended, q_heads, kv_heads):
-    length, shape = shared[0].shape[0], jax.ShapeDtypeStruct
-    return pl.pallas_call(
-        functools.partial(attend_back_kernel, q_heads, kv_heads),
-        out_shape=[shape(shared[0].shape, jnp.bfloat16), shape((8, HEAD_DIM), jnp.float32)],
-        scratch_shapes=[pltpu.VMEM((2, length, HEAD_DIM), jnp.float32)],
-        compiler_params=pltpu.CompilerParams(vmem_limit_bytes=48 * 1024 * 1024),
-    )(*shared, *kept, grad_attended)
+    )(grad_attn, *shared, *kept)
 
 
 def on_device(
@@ -1364,19 +1482,15 @@
         weights_all = lax.all_gather(rows_local, "gx", axis=0, tiled=True)
     q_width, kv_width = q_weight.shape[1], key_matrix.shape[1]
     qkv_width = q_width + 2 * kv_width
-    qkv_full = weights_all[:, :qkv_width]
     router_full = weights_all[:, qkv_width : qkv_width + experts_all]
-    o_full = weights_all[:, qkv_width + LANES :]
     heads_local = q_width // HEAD_DIM
     kv_local = kv_width // HEAD_DIM
     inputs_f = tokens_in.astype(jnp.float32)
     scale_one = root_mean_scale(inputs_f)
     unit_one = inputs_f * scale_one
     normalized_input = (unit_one * attn_gain).astype(jnp.bfloat16)
-    qkv_rows = jnp.dot(normalized_input, qkv_full, preferred_element_type=jnp.float32)
-    shared = attention_shared(qkv_rows, doc_ids, query_norm_gain, k_gain)
-    attended, *kept = attend(shared, heads_local, kv_local)
-    attn_part = contract(attended, o_full, 1, 1)
+    shared = attention_shared(weights_all, doc_ids, query_norm_gain, k_gain)
+    raw_rows, attended, *kept, attn_part = attend(normalized_input, shared, heads_local, kv_local)
     attn_total = attn_part + swap_cores(attn_part)
     residual = inputs_f + attn_total
     scale_two = root_mean_scale(residual)
@@ -1400,24 +1514,21 @@
     ffn_gain_term = jnp.sum(grad_ffn_in * unit_two, axis=0)
     grad_residual = grad_out_f + norm_back(grad_ffn_in * ffn_gain, unit_two, scale_two)
     grad_attn = grad_residual.astype(jnp.bfloat16)
-    grad_attended = jnp.dot(grad_attn, o_full, preferred_element_type=jnp.float32).astype(
-        jnp.bfloat16
+    grad_qkv, head_gains, grad_normed_part = attend_back(
+        grad_attn, shared, (raw_rows, *kept), heads_local, kv_local
     )
-    grad_qkv, head_gains = attend_back(shared, kept, grad_attended, heads_local, kv_local)
     q_gain_term, k_gain_term = head_gains[0], head_gains[1]
-    grad_normed_part = contract(grad_qkv, qkv_full, 1, 1)
     grad_normed = grad_normed_part + swap_cores(grad_normed_part)
     attn_gain_term = jnp.sum(grad_normed * unit_one, axis=0)
-    grad_input = (grad_residual + norm_back(grad_normed * attn_gain, unit_one, scale_one)).astype(
-        jnp.bfloat16
-    )
     own_mask = (jnp.arange(model_width) // part_width == lax.axis_index("gy")).astype(jnp.float32)
     gains = (attn_gain_term * own_mask, ffn_gain_term * own_mask, q_gain_term, k_gain_term)
     router_lanes = jnp.pad(router_term, ((0, 0), (0, LANES - experts_all)))
     if dense:
         router_blocks = router_lanes.astype(jnp.bfloat16).reshape(devices_gx, -1, LANES)
-        sums, gain_rows = scatter_sums(
-            normalized_input, grad_qkv, router_blocks, grad_attn, attended, packed_gains(gains), 4
+        factors = (normalized_input, grad_qkv, router_blocks, grad_attn, attended)
+        lasts = (tokens_in, grad_residual, grad_normed, attn_gain.reshape(1, model_width))
+        grad_q, grad_k, grad_v, grad_router, grad_out, gain_rows, grad_input = scatter_sums(
+            factors, packed_gains(gains), lasts, kv_width, 4
         )
         gains = unpacked_gains(gain_rows, gains)
     else:
@@ -1433,12 +1544,15 @@
             axis=1,
         )
         gains = lax.psum(gains, ("gx", "gy"))
+        grad_q = sums[:, :q_width]
+        grad_k = sums[:, q_width : q_width + kv_width]
+        grad_v = sums[:, q_width + kv_width : qkv_width]
+        grad_router = sums[:, qkv_width : qkv_width + LANES]
+        grad_out = sums[:, qkv_width + LANES :]
+        grad_input = grad_residual + norm_back(grad_normed * attn_gain, unit_one, scale_one)
+        grad_input = grad_input.astype(jnp.bfloat16)
     gain_attn, gain_ffn, gain_query, gain_key = gains
-    grad_q = sums[:, :q_width]
-    grad_k = sums[:, q_width : q_width + kv_width]
-    grad_v = sums[:, q_width + kv_width : qkv_width]
-    grad_router = sums[:, qkv_width : qkv_width + experts_all]
-    grad_out = sums[:, qkv_width + LANES :]
+    grad_router = grad_router[:, :experts_all]
     return (
         output,
         grad_input,

time: 765 us -> 760 us (level)
  matrix products: 31.1 us -> 5.11 us
  Pallas kernels: 677 us -> 699 us
    dot_general x4 -> x2, matrix products: 17.6 us -> 3.64 us  [contract(): lax.dot_general(first_op, second_op, (((first_dim,), (second_dim,)), ((),...]
    dot_general x2 -> x0, matrix products: 12.1 us -> none  [the longest x1 6.11 us: on_device(): jnp.dot(grad_attn, o_full, preferred_element_type=jnp.float32)]
    pallas_call x1, Pallas kernels: 8.64 us -> 19.7 us  [attend(): pl.pallas_call(functools.partial(attend_kernel, q_heads, kv_heads), out_s...]
    pallas_call x1, Pallas kernels: 12.5 us -> 22.6 us  [attend_back(): pl.pallas_call(functools.partial(attend_back_kernel, q_heads, kv_heads),...]
    unnamed x70 -> x77, local copies, waits for them, and re-layouts: 14.7 us -> 23.6 us
where the time goes in v7:
time: 760 us; the launch traced here: 754 us
  Pallas kernels  699 us (92%)
  local copies, waits for them, and re-layouts  32 us (4%)
  other arithmetic  12.5 us (2%)
    pallas_call x1, Pallas kernels, experts_products(): pl.pallas_call(functools.partial(experts_kernel, experts_all), out_shape=...  168 us
    pallas_call x1, Pallas kernels, scatter_sums(): pl.pallas_call(scatter_kernel, out_shape=[*[jax.ShapeDtypeStruct((rows, w...  166 us
    pallas_call x1, Pallas kernels, gather_blocks(): pl.pallas_call(functools.partial(gather_kernel, count, with_pair), out_sh...  162 us
    pallas_call x1, Pallas kernels, return_sums(): pl.pallas_call(return_kernel, out_shape=[jax.ShapeDtypeStruct((2 * rows,...  161 us
    unnamed x77, local copies, waits for them, and re-layouts  23.6 us
    pallas_call x1, Pallas kernels, attend_back(): pl.pallas_call(functools.partial(attend_back_kernel, q_heads, kv_heads),...  22.6 us
    pallas_call x1, Pallas kernels, attend(): pl.pallas_call(functools.partial(attend_kernel, q_heads, kv_heads), out_s...  19.7 us
  transfers between devices with their start and end apart: 2, of which 2 were waited for; matrix products, arithmetic and copies ran while one was open for 1% of the time, Pallas kernels for 0%

profile of v7, /device:TPU:0, one launch (start us, length us, event | category | flops | bytes accessed | tf_op | source)
XLA Modules:
  0.0 754.0 jit_solution(12779475303587813286)
XLA Ops:
  0.7 1.6 fusion.4
  6.7 161.7 %shard_map.263 = bf16[16,128,4736]{2,1,0:T(8,128)(2,1)} custom-call(bf16[128,4736]{1,0:T(8,128)(2,1)} %copy-done.18), custom_call_target="tpu_custom_call" | custom-call | tf_op jit(solution)/shard_map/pallas_call | solution.py:312
  169.0 19.7 %shard_map.264 = (f32[256,2560]{1,0:T(8,128)}, bf16[256,2048]{1,0:T(8,128)(2,1)S(1)}, bf16[256,2048]{1,0:T(8,128)(2,1)S(1)}, bf16[256,256]{1,0:T(8,128)(2,1)S(1)...) custom-call(bf16[256,2048]{1,0:T(8,128)(2,1)S(1)} %fusion.2.normed_ref.refs_0_, ...), custom_call_target="tpu_custom_call" | custom-call | tf_op jit(solution)/shard_map/pallas_call | solution.py:1414
  190.7 1.9 constant_dynamic-slice_fusion.refs_1_
  192.6 2.4 collective-permute-done
  195.0 2.3 multiply_reduce_fusion.2
  198.6 1.5 fusion.18
  201.1 168.3 %shard_map.265 = (bf16[2,16,128,384]{3,2,1,0:T(8,128)(2,1)}, bf16[2,16,128,768]{3,2,1,0:T(8,128)(2,1)}, bf16[2,16,128,128]{3,2,1,0:T(8,128)(2,1)}, f32[2048,384]...) custom-call(bf16[128,2176]{1,0:T(8,128)(2,1)} %pad_maximum_fusion.re, ...), custom_call_target="tpu_custom_call" | custom-call | tf_op jit(solution)/shard_map/pallas_call | solution.py:533
  369.4 161.2 %shard_map.266 = (f32[256,2176]{1,0:T(8,128)}, f32[256,2048]{1,0:T(8,128)}) custom-call(bf16[2,16,128,768]{3,2,1,0:T(8,128)(2,1)} %get-tuple-element.40.grad_in, bf16[2,16,128,384]{3,2,1,0:T(8,128)(2,1)} %get-tuple-element.41.weighted, bf16[2,16,128,128]{3,2,1,0:T(8,128)(2,1)} %get-tuple-element.42.terms, bf16[2048,384]{1,0:T(8,128)(2,1)} %bitcast.40, ...), custom_call_target="tpu_custom_call" | custom-call | tf_op jit(solution)/shard_map/pallas_call | solution.py:1076
  531.7 3.4 multiply_reduce_fusion
  535.7 2.4 fusion.17
  538.1 22.6 %shard_map.267 = (bf16[256,2560]{1,0:T(8,128)(2,1)S(1)}, f32[8,128]{1,0:T(8,128)S(1)}, f32[256,2048]{1,0:T(8,128)S(1)}) custom-call(bf16[256,2048]{1,0:T(8,128)(2,1)S(1)} %get-tuple-element.124.grad_attn_ref.refs_3_, bf16[2048,4736]{1,0:T(8,128)(2,1)} %bitcast.38, f32[256,128]{1,0:T(8,128)S(1)} %get-tuple-element.141.cosine_ref, ...), custom_call_target="tpu_custom_call" | custom-call | tf_op jit(solution)/shard_map/pallas_call | solution.py:1434
  563.4 1.9 pad.19.clone
  566.1 3.5 fusion.3
  570.2 165.8 %shard_map.268 = (f32[128,2048]{1,0:T(8,128)}, f32[128,256]{1,0:T(8,128)}, f32[128,256]{1,0:T(8,128)}, f32[128,128]{1,0:T(8,128)}, f32[128,2048]{1,0:T(8,128)}, ...) custom-call(bf16[256,2048]{1,0:T(8,128)(2,1)} %copy-done.1, bf16[256,2560]{1,0:T(8,128)(2,1)} %copy-done.2, ...), custom_call_target="tpu_custom_call" | custom-call | tf_op jit(solution)/shard_map/pallas_call | solution.py:899
  736.0 1.3 slice_bitcast_fusion.2
  737.3 1.3 slice_bitcast_fusion
  738.6 1.5 copy.57
  740.1 2.4 copy.71
  745.8 1.7 copy.76
  747.5 1.4 copy-done.16
  748.8 1.7 copy.77
  750.5 1.4 copy-done.15
  751.9 1.7 copy.78
  (100 shorter events, 18.1 us)
Async XLA Ops:
  0.6 4.8 copy-start.27
  0.7 4.9 copy-start.28
  0.7 4.9 copy-start.23
  6.6 161.7 %copy-start.11 = (bf16[256,2048]{1,0:T(8,128)(2,1)S(1)}, bf16[256,2048]{1,0:T(8,128)(2,1)}, u32[]{:S(2)}) copy-start(bf16[256,2048]{1,0:T(8,128)(2,1)} %refs_6_.1) | copy-start | bytes 3145732
  6.7 161.7 %copy-start.29 = (f32[2048]{0:T(1024)S(1)}, f32[2048]{0:T(1024)}, u32[]{:S(2)}) copy-start(f32[2048]{0:T(1024)} %param.24) | copy-start | bytes 24580
  168.7 20.0 %copy-start.1 = (bf16[256,2048]{1,0:T(8,128)(2,1)}, bf16[256,2048]{1,0:T(8,128)(2,1)S(1)}, u32[]{:S(2)}) copy-start(bf16[256,2048]{1,0:T(8,128)(2,1)S(1)} %fusion.2.normed_ref.refs_0_) | copy-start | bytes 3145732
  169.0 21.7 %copy-start.30 = (s32[256,8]{0,1:T(8,128)S(1)}, s32[256,8]{0,1:T(8,128)}, u32[]{:S(2)}) copy-start(s32[256,8]{0,1:T(8,128)} %param.18) | copy-start | bytes 24580
  190.7 4.3 collective-permute-start
  192.6 4.7 copy-start.26
  197.5 2.5 copy-start.13
  531.7 3.4 copy-start.10
  531.7 3.4 copy-start.19
  531.7 4.0 copy-start.20
  538.1 22.6 %copy-start = (bf16[256,2048]{1,0:T(8,128)(2,1)}, bf16[256,2048]{1,0:T(8,128)(2,1)S(1)}, u32[]{:S(2)}) copy-start(bf16[256,2048]{1,0:T(8,128)(2,1)S(1)} %get-tuple-element.124.grad_attn_ref.refs_3_) | copy-start | bytes 3145732
  538.1 24.1 %copy-start.14 = (bf16[256,2048]{1,0:T(8,128)(2,1)S(1)}, bf16[256,2048]{1,0:T(8,128)(2,1)}, u32[]{:S(2)}) copy-start(bf16[256,2048]{1,0:T(8,128)(2,1)} %copy-done.13) | copy-start | bytes 3145732
  561.8 4.3 copy-start.12
  561.8 4.3 collective-permute-start.1
  736.0 6.5 copy-start.22
  740.1 3.4 copy-start.25
  740.1 4.0 copy-start.24
  740.1 4.7 copy-start.21
  742.5 3.3 copy-start.17
  745.8 3.0 copy-start.16
  748.8 3.0 copy-start.15
  (9 other events, 9.8 us)

commit v8 on v7

--- a/solution.py
+++ b/solution.py
@@ -220,15 +220,15 @@
         whole_a, half_a, whole_b, half_b = self.spans
         last = self.last
         for k in self.everyone:
-            self.arrive(None, k, last, self.x_side, 1, whole_b, 0)
+            self.arrive(None, k, last, self.x_side, 1, whole_b, (0, 1))
             self.send(None, k, last + 3, "out", self.x_side, 1, half_b[1], self.to_y)
-            self.arrive(None, k, last + 1, self.y_side, 1, whole_b, 0)
+            self.arrive(None, k, last + 1, self.y_side, 1, whole_b, (0, 1))
             self.send(None, k, last + 2, "out", self.y_side, 1, half_b[0], self.to_x)
         for k in self.everyone:
             self.own_copy(k).wait()
-            self.mirror(None, k, self.me, 1, (0, self.ins[k].shape[0]), 0)
-            self.arrive(None, k, last + 2, self.diagonal, 1, half_b[0], 0)
-            self.arrive(None, k, last + 3, self.diagonal, 1, half_b[1], 0)
+            self.mirror(None, k, self.me, 1, (0, self.ins[k].shape[0]), (0, 0))
+            self.arrive(None, k, last + 2, self.diagonal, 1, half_b[0], (0, 1))
+            self.arrive(None, k, last + 3, self.diagonal, 1, half_b[1], (0, 1))
 
     def start_planes(self):
         whole_b = self.spans[2]
@@ -241,10 +241,10 @@
         for k in self.everyone:
             for condition, index, distance in self.members(step):
                 first = self.x_side + PLANE * distance
-                self.arrive(condition, k, self.slot_of(0, index), first, 1, whole_a, distance)
+                self.arrive(condition, k, self.slot_of(0, index), first, 1, whole_a, (distance, 0))
                 self.send(condition, k, self.slot_of(3, index), "out", first, 1, half_a[1], self.to_y)
                 first = self.y_side + PLANE * distance
-                self.arrive(condition, k, self.slot_of(1, index), first, 1, whole_a, distance)
+                self.arrive(condition, k, self.slot_of(1, index), first, 1, whole_a, (distance, 0))
                 self.send(condition, k, self.slot_of(2, index), "out", first, 1, half_a[0], self.to_x)
 
     def halves(self, step):
@@ -252,8 +252,8 @@
         for k in self.everyone:
             for condition, index, distance in self.members(step):
                 first = self.diagonal + PLANE * distance
-                self.arrive(condition, k, self.slot_of(2, index), first, 1, half_a[0], distance)
-                self.arrive(condition, k, self.slot_of(3, index), first, 1, half_a[1], distance)
+                self.arrive(condition, k, self.slot_of(2, index), first, 1, half_a[0], (distance, 0))
+                self.arrive(condition, k, self.slot_of(3, index), first, 1, half_a[1], (distance, 0))
 
     def column(self, step):
         whole_a = self.spans[0]
@@ -261,7 +261,7 @@
             for condition, index, distance in self.members(step):
                 first = self.me + PLANE * distance
                 rising = distance < 0
-                self.arrive(condition, k, step - 1 if rising else 2 + step, first, 1, whole_a, distance)
+                self.arrive(condition, k, step - 1 if rising else 2 + step, first, 1, whole_a, (distance, 0))
                 if step < LEVELS - 1:
                     onward = condition & (self.has_up if rising else self.has_down)
                     slot = step if rising else 3 + step
@@ -275,15 +275,16 @@
             for condition, index, distance in self.members(step):
                 first = PLANE * (self.level + distance)
                 rising = distance < 0
-                self.arrive(condition, k, self.last + (3 if rising else 6) + step, first, PLANE, whole_b, distance)
+                slot = self.last + (3 if rising else 6) + step
+                self.arrive(condition, k, slot, first, PLANE, whole_b, (distance, 1))
                 if step < LEVELS - 1:
                     onward = condition & (self.has_up if rising else self.has_down)
                     slot = self.last + (4 if rising else 7) + step
                     self.send(onward, k, slot, "out", first, PLANE, whole_b, self.up if rising else self.down)
 
-    def paired_level(self, distance):
+    def paired_level(self, distance, parts):
         for condition, copy, group in self.mirrored:
-            if group == distance:
+            if group[0] == distance and group[1] in parts:
                 when(condition, lambda copy=copy: copy().wait_recv())
 
     def end(self, levels_waited=False):
@@ -331,7 +332,7 @@
     rows_ref, grad_rows_ref, w_gate, w_up, w_down = refs[:5]
     weighted_out, grad_in_out, terms_out, gate_out, up_out, down_out, grads_own, grads_pair = refs[5:13]
     held, grads, w_in, left_in, left_down, weighted_ref, grad_in_ref, terms_ref = refs[13:21]
-    sums_in, sums_down, turned, grad_sem, w_sem, out_sem, sum_sem = refs[21:28]
+    sums_in, sums_down, turned, down_low, grad_sem, part_sem, w_sem, out_sem, sum_sem = refs[21:30]
     hidden, width = w_down.shape
     joins = [
         pltpu.make_async_copy(part, w_in.at[:, pl.ds(i * hidden, hidden)], w_sem.at[i])
@@ -339,12 +340,11 @@
     ]
     for join in joins:
         join.start()
-    steps = gather_steps(
-        [rows_ref, grad_rows_ref], [held.at[0], grads_own], [held.at[1], grads_pair], refs[28:]
-    )
+    rows = rows_ref.shape[0]
+    grad_half = grad_rows_ref.at[pl.ds(pl.multiple_of(lax.axis_index("gy") * rows, rows), rows)]
+    steps = gather_steps([rows_ref, grad_half], [held.at[0], grads_own], [held.at[1], grads_pair], refs[30:])
     level, core = steps.level, steps.core
     tiles = hidden // LANES
-    rows = rows_ref.shape[0]
     visits = [
         level,
         jnp.where(level == 0, 1, level - 1),
@@ -359,16 +359,24 @@
             grad_sem.at[turn % 2, half],
         )
 
-    def fetch_start(turn):
-        fetch(turn, 0).start()
-        fetch(turn, 1).start()
+    part_rows = {None: (0, rows), 0: steps.spans[0], 1: steps.spans[2]}
+
+    def fetch_part(part, half):
+        span = pl.ds(*part_rows[part])
+        return pltpu.make_async_copy(
+            (grads_own, grads_pair)[half].at[pl.ds(PLANE * visits[-1], PLANE), span],
+            grads.at[(LEVELS - 1) % 2, half, :, span],
+            part_sem.at[part, half],
+        )
+
+    def fetches(turn, part):
+        return [fetch(turn, half) if part is None else fetch_part(part, half) for half in range(2)]
 
     lane = lax.broadcasted_iota(jnp.int32, (1, LANES), 1)
     expert = steps.me
     gate_pick = (((lane == expert) | (lane == experts_all + expert))).astype(jnp.float32)
     high_lane = (lane == 2 * experts_all * core + expert).astype(jnp.float32)
     low_lane = (lane == 2 * experts_all * core + experts_all + expert).astype(jnp.float32)
-    group = 2 * rows
 
     def leave(turn):
         span = pl.ds(PLANE * visits[turn], PLANE)
@@ -378,23 +386,26 @@
             for i, (here, there) in enumerate(pairs)
         ]
 
-    def forward(turn, begin, end):
-        first = PLANE * visits[turn]
+    def forward(turn, begin=0, end=4, part=None):
+        first, (row, number) = PLANE * visits[turn], part_rows[part]
+        together = 2 if part is None else PLANE
+        group, per_half, span_rows = together * number, PLANE // together, pl.ds(row, number)
         if begin == 0:
-            fetch(turn, 0).wait()
-            fetch(turn, 1).wait()
+            for copy in fetches(turn, part):
+                copy.wait()
 
         def body(step, carry):
-            half, pair = step // 2, step % 2
-            at = first + 2 * pair
-            lanes = held[half, pl.ds(at, 2), :, pl.ds(width, LANES)].reshape(group, LANES)
+            half, pair = step // per_half, step % per_half
+            at = first + together * pair
+            blocks = pl.ds(at, together)
+            lanes = held[half, blocks, span_rows, pl.ds(width, LANES)].reshape(group, LANES)
             gate_rows = jnp.sum(lanes.astype(jnp.float32) * gate_pick, axis=1, keepdims=True)
-            grad_rows = grads[turn % 2, half, pl.ds(2 * pair, 2)].reshape(group, width)
-            token_rows = held[half, pl.ds(at, 2), :, pl.ds(0, width)].reshape(group, width)
+            grad_rows = grads[turn % 2, half, pl.ds(together * pair, together), span_rows].reshape(group, width)
+            token_rows = held[half, blocks, span_rows, pl.ds(0, width)].reshape(group, width)
             grad_hidden = dot_nt(grad_rows, w_down[...])
             both = dot_nn(token_rows, w_in[...])
             terms = jnp.zeros((group, 1), jnp.float32)
-            column = pl.multiple_of(step * group, group)
+            column = pl.multiple_of(2 * PLANE * row + step * group, LANES)
             for j in range(tiles):
                 gate_in = both[:, j * LANES : (j + 1) * LANES]
                 up_in = both[:, hidden + j * LANES : hidden + (j + 1) * LANES]
@@ -413,38 +424,42 @@
                     (grad_up, grad_in_ref, tiles + j, left_in),
                 ):
                     span = pl.ds(tile * LANES, LANES)
-                    array[half, pl.ds(at, 2), :, span] = value.astype(jnp.bfloat16).reshape(2, rows, LANES)
+                    low = value.astype(jnp.bfloat16).reshape(together, number, LANES)
+                    array[half, blocks, span_rows, span] = low
                     left[span, pl.ds(column, group)] = value.T.astype(jnp.bfloat16)
             high = terms.astype(jnp.bfloat16).astype(jnp.float32)
             spread = high * high_lane + (terms - high) * low_lane
-            terms_ref[half, pl.ds(at, 2)] = spread.astype(jnp.bfloat16).reshape(2, rows, LANES)
+            terms_ref[half, blocks, span_rows] = spread.astype(jnp.bfloat16).reshape(together, number, LANES)
             return carry
 
-        lax.fori_loop(begin, end, body, 0)
-        if end == 4:
+        lax.fori_loop(begin, min(end, 2 * per_half), body, 0)
+        if end == 4 and part != 0:
             for copy in leave(turn):
                 copy.start()
 
     wide = 256
 
-    def weights(turn, begin, end):
-        first = PLANE * visits[turn]
+    def weights(turn, begin=0, end=8, part=None):
+        first, (row, number) = PLANE * visits[turn], part_rows[part]
+        span_rows, depth = pl.ds(row, number), 2 * PLANE * number
+        columns = pl.ds(2 * PLANE * row, depth)
 
         def body(step, carry):
             span = pl.ds(pl.multiple_of(step * wide, wide), wide)
-            token_rows = held[:, pl.ds(first, PLANE), :, span].reshape(2 * PLANE * rows, wide)
-            grad_rows = grads[turn % 2, :, :, :, span].reshape(2 * PLANE * rows, wide)
-            part_in = dot_nn(left_in[...], token_rows)
-            part_down = dot_nn(left_down[...], grad_rows)
+            token_rows = held[:, pl.ds(first, PLANE), span_rows, span].reshape(depth, wide)
+            grad_rows = grads[turn % 2, :, :, span_rows, span].reshape(depth, wide)
+            part_in = dot_nn(left_in[:, columns], token_rows)
+            part_down = dot_nn(left_down[:, columns], grad_rows)
             if turn:
                 part_in = sums_in[:, span] + part_in
                 part_down = sums_down[:, span] + part_down
-            sums_down[:, span] = part_down
-            if turn < LEVELS - 1:
+            if part != 1:
                 sums_in[:, span] = part_in
+                sums_down[:, span] = part_down
             else:
                 for i in range(2):
-                    turned[i, span] = part_in[i * hidden : (i + 1) * hidden].T
+                    turned[i, span] = part_in[i * hidden : (i + 1) * hidden].T.astype(jnp.bfloat16)
+                down_low[:, span] = part_down.astype(jnp.bfloat16)
                 for copy in leave_sums(step):
                     copy.start()
             return carry
@@ -456,17 +471,19 @@
         return [
             pltpu.make_async_copy(turned.at[0, span], gate_out.at[span], sum_sem.at[step, 0]),
             pltpu.make_async_copy(turned.at[1, span], up_out.at[span], sum_sem.at[step, 1]),
-            pltpu.make_async_copy(sums_down.at[:, span], down_out.at[:, span], sum_sem.at[step, 2]),
+            pltpu.make_async_copy(down_low.at[:, span], down_out.at[:, span], sum_sem.at[step, 2]),
         ]
 
-    def level_ready(turn):
+    def level_ready(turn, part=None):
+        parts = (0, 1) if part is None else (part,)
         if turn == 0:
-            steps.paired_level(0)
+            steps.paired_level(0, parts)
         for distance in range(-3, 4):
             if turn and distance:
                 wanted = visits[turn] == level + distance
-                pl.when(wanted)(lambda distance=distance: steps.paired_level(distance))
-        fetch_start(turn)
+                pl.when(wanted)(lambda distance=distance: steps.paired_level(distance, parts))
+        for copy in fetches(turn, part):
+            copy.start()
 
     steps.start()
     steps.side_small()
@@ -495,12 +512,15 @@
     level_ready(2)
     weights(1, 4, 8)
     forward(2, 0, 4)
+    steps.halves(3)
+    level_ready(3, 0)
     weights(2, 0, 8)
+    forward(3, part=0)
+    weights(3, part=0)
     steps.planes(3)
-    steps.halves(3)
-    level_ready(3)
-    forward(3, 0, 4)
-    weights(3, 0, 8)
+    level_ready(3, 1)
+    forward(3, part=1)
+    weights(3, part=1)
     for turn in range(LEVELS):
         for copy in leave(turn):
             copy.wait()
@@ -523,9 +543,9 @@
         jax.ShapeDtypeStruct((*block_shape, hidden), low),
         jax.ShapeDtypeStruct((*block_shape, 2 * hidden), low),
         jax.ShapeDtypeStruct((*block_shape, LANES), low),
-        jax.ShapeDtypeStruct((width, hidden), jnp.float32),
-        jax.ShapeDtypeStruct((width, hidden), jnp.float32),
-        jax.ShapeDtypeStruct((hidden, width), jnp.float32),
+        jax.ShapeDtypeStruct((width, hidden), low),
+        jax.ShapeDtypeStruct((width, hidden), low),
+        jax.ShapeDtypeStruct((hidden, width), low),
         *[jax.ShapeDtypeStruct((blocks, count, width), low)] * 2,
     ]
     level_rows = 2 * PLANE * count
@@ -544,7 +564,9 @@
             *[pltpu.VMEM(shape.shape, low) for shape in shapes[:3]],
             pltpu.VMEM((2 * hidden, width), jnp.float32),
             pltpu.VMEM((hidden, width), jnp.float32),
-            pltpu.VMEM((2, width, hidden), jnp.float32),
+            pltpu.VMEM((2, width, hidden), low),
+            pltpu.VMEM((hidden, width), low),
+            dma((2, 2)),
             dma((2, 2)),
             dma((2,)),
             dma((LEVELS, 3)),
@@ -1223,7 +1245,7 @@
     gate_lanes = jnp.pad(jnp.concatenate(two_parts(gate_all), axis=1), ((0, 0), (0, LANES - 2 * experts_all)))
     row_lanes = jnp.concatenate([own_half(normed_ffn), own_half(gate_lanes)], axis=1)
     weighted, grad_in, terms, gate_term, up_term, down_term = experts_products(
-        row_lanes, own_half(cotangent), w_gate, w_up, w_down, experts_all, 2
+        row_lanes, cotangent, w_gate, w_up, w_down, experts_all, 2
     )
     back, mixed_rows = return_sums(grad_in, weighted, terms, w_gate, w_up, w_down, 3)
     term_lanes = back[:, model_width : model_width + 4 * experts_all]
@@ -1231,7 +1253,9 @@
     grad_logits = (
         gate_all * (grad_gates - jnp.sum(gate_all * grad_gates, axis=1, keepdims=True))
     ).astype(jnp.bfloat16)
-    return mixed_rows, back[:, :model_width], grad_logits, (gate_term[None], up_term[None], down_term[None])
+    return mixed_rows, back[:, :model_width], grad_logits, tuple(
+        term[None].astype(jnp.float32) for term in (gate_term, up_term, down_term)
+    )
 
 
 def turn_lanes(values, cosine, sine_table):
@@ -1287,14 +1311,22 @@
 
 
 def attend_kernel(
-    q_heads, kv_heads, normed_ref, w_ref, cosine_ref, sine_ref, docs_column, docs_row, q_gain, k_gain,
-    raw_ref, attended_ref, query_ref, key_ref, value_ref, totals_ref, part_ref, w_in, w_out, w_sem,
+    q_heads, kv_heads, tokens_ref, w_ref, cosine_ref, sine_ref, docs_column, docs_row, q_gain, k_gain, attn_gain,
+    normed_ref, raw_ref, attended_ref, query_ref, key_ref, value_ref, totals_ref, part_ref, w_in, w_out, w_sem,
 ):
     into, out = weight_copies(w_ref, w_in, w_out, w_sem, GROUP, True)
     for _, copy in into:
         copy.start()
     for copy in out:
         copy.start()
+
+    def norm_rows(i, carry):
+        span = pl.ds(pl.multiple_of(i * 16, 16), 16)
+        unit, _ = unit_rows(tokens_ref[span].astype(jnp.float32))
+        normed_ref[span] = (unit * attn_gain[...]).astype(jnp.bfloat16)
+        return carry
+
+    lax.fori_loop(0, tokens_ref.shape[0] // 16, norm_rows, 0)
     for n, copy in into:
         copy.wait()
         dot_groups(raw_ref, normed_ref, w_in, n * GROUP, GROUP, False)
@@ -1408,12 +1440,13 @@
     return [vmem, everywhere] + [vmem] * (inputs - 2), scratch
 
 
-def attend(normed, shared, q_heads, kv_heads):
-    (length, features), low, shape = normed.shape, jnp.bfloat16, jax.ShapeDtypeStruct
-    in_specs, scratch = attention_specs(q_heads, kv_heads, features, 1 + len(shared))
+def attend(tokens, attn_gain, shared, q_heads, kv_heads):
+    (length, features), low, shape = tokens.shape, jnp.bfloat16, jax.ShapeDtypeStruct
+    in_specs, scratch = attention_specs(q_heads, kv_heads, features, 2 + len(shared))
     return pl.pallas_call(
         functools.partial(attend_kernel, q_heads, kv_heads),
         out_shape=[
+            shape((length, features), low),
             shape((length, (q_heads + 2 * kv_heads) * HEAD_DIM), jnp.float32),
             shape((length, q_heads * HEAD_DIM), low),
             shape((length, q_heads * HEAD_DIM), low),
@@ -1425,7 +1458,7 @@
         in_specs=in_specs,
         scratch_shapes=scratch,
         compiler_params=pltpu.CompilerParams(vmem_limit_bytes=48 * 1024 * 1024),
-    )(normed, *shared)
+    )(tokens, *shared, attn_gain.reshape(1, features))
 
 
 def attend_back(grad_attn, shared, kept, q_heads, kv_heads):
@@ -1488,9 +1521,10 @@
     inputs_f = tokens_in.astype(jnp.float32)
     scale_one = root_mean_scale(inputs_f)
     unit_one = inputs_f * scale_one
-    normalized_input = (unit_one * attn_gain).astype(jnp.bfloat16)
     shared = attention_shared(weights_all, doc_ids, query_norm_gain, k_gain)
-    raw_rows, attended, *kept, attn_part = attend(normalized_input, shared, heads_local, kv_local)
+    normalized_input, raw_rows, attended, *kept, attn_part = attend(
+        tokens_in, attn_gain, shared, heads_local, kv_local
+    )
     attn_total = attn_part + swap_cores(attn_part)
     residual = inputs_f + attn_total
     scale_two = root_mean_scale(residual)
@@ -1509,7 +1543,8 @@
         )
     output = (residual + mixed_rows).astype(jnp.bfloat16)
     grad_out_f = cotangent.astype(jnp.float32)
-    router_term = contract(normed_ffn, grad_logits, 0, 0)
+    logit_lanes = jnp.pad(grad_logits, ((0, 0), (0, LANES - experts_all)))
+    router_lanes = contract(normed_ffn, logit_lanes, 0, 0)
     grad_ffn_in = contract(grad_logits, router_full, 1, 1) + grad_rows_sum
     ffn_gain_term = jnp.sum(grad_ffn_in * unit_two, axis=0)
     grad_residual = grad_out_f + norm_back(grad_ffn_in * ffn_gain, unit_two, scale_two)
@@ -1522,7 +1557,6 @@
     attn_gain_term = jnp.sum(grad_normed * unit_one, axis=0)
     own_mask = (jnp.arange(model_width) // part_width == lax.axis_index("gy")).astype(jnp.float32)
     gains = (attn_gain_term * own_mask, ffn_gain_term * own_mask, q_gain_term, k_gain_term)
-    router_lanes = jnp.pad(router_term, ((0, 0), (0, LANES - experts_all)))
     if dense:
         router_blocks = router_lanes.astype(jnp.bfloat16).reshape(devices_gx, -1, LANES)
         factors = (normalized_input, grad_qkv, router_blocks, grad_attn, attended)

time: 760 us -> 751 us (0.988)
  local copies, waits for them, and re-layouts: 32 us -> 20.4 us
    unnamed x77 -> x69, local copies, waits for them, and re-layouts: 23.6 us -> 15.8 us
  transfers between devices with their start and end apart: 2 -> 2, of which waited for: 2 -> 1; matrix products, arithmetic and copies ran while one was open for 1% -> 1% of each run, Pallas kernels for 0% -> 0%
where the time goes in v8:
time: 751 us; the launch traced here: 746 us
  Pallas kernels  697 us (93%)
  local copies, waits for them, and re-layouts  20.4 us (3%)
  other arithmetic  15.4 us (2%)
    pallas_call x1, Pallas kernels, scatter_sums(): pl.pallas_call(scatter_kernel, out_shape=[*[jax.ShapeDtypeStruct((rows, w...  167 us
    pallas_call x1, Pallas kernels, experts_products(): pl.pallas_call(functools.partial(experts_kernel, experts_all), out_shape=...  167 us
    pallas_call x1, Pallas kernels, gather_blocks(): pl.pallas_call(functools.partial(gather_kernel, count, with_pair), out_sh...  162 us
    pallas_call x1, Pallas kernels, return_sums(): pl.pallas_call(return_kernel, out_shape=[jax.ShapeDtypeStruct((2 * rows,...  159 us
    pallas_call x1, Pallas kernels, attend_back(): pl.pallas_call(functools.partial(attend_back_kernel, q_heads, kv_heads),...  22.6 us
    pallas_call x1, Pallas kernels, attend(): pl.pallas_call(functools.partial(attend_kernel, q_heads, kv_heads), out_s...  20.6 us
    unnamed x69, local copies, waits for them, and re-layouts  15.8 us
  transfers between devices with their start and end apart: 2, of which 1 were waited for; matrix products, arithmetic and copies ran while one was open for 1% of the time, Pallas kernels for 0%

profile of v8, /device:TPU:0, one launch (start us, length us, event | category | flops | bytes accessed | tf_op | source)
XLA Modules:
  0.0 746.1 jit_solution(5032732223859845565)
XLA Ops:
  2.9 1.1 constant_dynamic-update-slice_fusion.3
  5.7 1.0 copy-done.17
  6.8 161.7 %shard_map.263 = bf16[16,128,4736]{2,1,0:T(8,128)(2,1)} custom-call(bf16[128,4736]{1,0:T(8,128)(2,1)} %copy-done.17), custom_call_target="tpu_custom_call" | custom-call | tf_op jit(solution)/shard_map/pallas_call | solution.py:313
  168.7 20.6 %shard_map.264 = (bf16[256,2048]{1,0:T(8,128)(2,1)S(1)}, f32[256,2560]{1,0:T(8,128)}, bf16[256,2048]{1,0:T(8,128)(2,1)S(1)}, bf16[256,2048]{1,0:T(8,128)(2,1)S(1...) custom-call(bf16[256,2048]{1,0:T(8,128)(2,1)S(1)} %copy-done, ...), custom_call_target="tpu_custom_call" | custom-call | tf_op jit(solution)/shard_map/pallas_call | solution.py:1446
  191.2 1.0 copy-done.7
  192.2 4.5 collective-permute-done
  196.7 2.8 multiply_reduce_fusion.2
  199.8 1.9 fusion.18
  202.7 166.6 %shard_map.265 = (bf16[2,16,128,384]{3,2,1,0:T(8,128)(2,1)}, bf16[2,16,128,768]{3,2,1,0:T(8,128)(2,1)}, bf16[2,16,128,128]{3,2,1,0:T(8,128)(2,1)}, bf16[2048,384...) custom-call(bf16[128,2176]{1,0:T(8,128)(2,1)} %pad_maximum_fusion.re, ...), custom_call_target="tpu_custom_call" | custom-call | tf_op jit(solution)/shard_map/pallas_call | solution.py:553
  369.4 159.0 %shard_map.266 = (f32[256,2176]{1,0:T(8,128)}, f32[256,2048]{1,0:T(8,128)}) custom-call(bf16[2,16,128,768]{3,2,1,0:T(8,128)(2,1)} %get-tuple-element.41.grad_in, bf16[2,16,128,384]{3,2,1,0:T(8,128)(2,1)} %get-tuple-element.42.weighted, bf16[2,16,128,128]{3,2,1,0:T(8,128)(2,1)} %get-tuple-element.43.terms, bf16[2048,384]{1,0:T(8,128)(2,1)} %bitcast.47, ...), custom_call_target="tpu_custom_call" | custom-call | tf_op jit(solution)/shard_map/pallas_call | solution.py:1098
  529.5 3.4 multiply_reduce_fusion
  533.4 2.4 fusion.17
  535.9 22.6 %shard_map.267 = (bf16[256,2560]{1,0:T(8,128)(2,1)S(1)}, f32[8,128]{1,0:T(8,128)S(1)}, f32[256,2048]{1,0:T(8,128)S(1)}) custom-call(bf16[256,2048]{1,0:T(8,128)(2,1)S(1)} %get-tuple-element.126.grad_attn_ref.refs_3_, bf16[2048,4736]{1,0:T(8,128)(2,1)} %bitcast.45, f32[256,128]{1,0:T(8,128)S(1)} %get-tuple-element.144.cosine_ref, ...), custom_call_target="tpu_custom_call" | custom-call | tf_op jit(solution)/shard_map/pallas_call | solution.py:1467
  559.0 1.3 convolution_convert_fusion
  560.4 1.9 bitcast_convert_fusion.2
  562.5 1.9 bitcast_convert_fusion.1
  564.5 2.0 bitcast_convert_fusion
  566.5 1.9 fusion.2
  569.1 166.7 %shard_map.268 = (f32[128,2048]{1,0:T(8,128)}, f32[128,256]{1,0:T(8,128)}, f32[128,256]{1,0:T(8,128)}, f32[128,128]{1,0:T(8,128)}, f32[128,2048]{1,0:T(8,128)}, ...) custom-call(bf16[256,2048]{1,0:T(8,128)(2,1)} %copy-done.6, bf16[256,2560]{1,0:T(8,128)(2,1)} %copy-done.3, ...), custom_call_target="tpu_custom_call" | custom-call | tf_op jit(solution)/shard_map/pallas_call | solution.py:921
  735.9 1.3 slice_bitcast_fusion.2
  737.1 1.3 slice_bitcast_fusion
  738.5 1.5 copy.53
  740.0 2.4 copy.63
  742.4 1.0 copy.64
  (91 shorter events, 12.8 us)
Async XLA Ops:
  0.6 5.0 copy-start.24
  6.7 161.9 %copy-start = (bf16[256,2048]{1,0:T(8,128)(2,1)S(1)}, bf16[256,2048]{1,0:T(8,128)(2,1)}, u32[]{:S(2)}) copy-start(bf16[256,2048]{1,0:T(8,128)(2,1)} %refs_6_.1) | copy-start | bytes 3145732
  6.7 161.9 %copy-start.8 = (f32[2048]{0:T(1024)S(1)}, f32[2048]{0:T(1024)}, u32[]{:S(2)}) copy-start(f32[2048]{0:T(1024)} %param.24) | copy-start | bytes 24580
  6.7 161.9 %copy-start.9 = (s32[1,256]{1,0:T(1,128)S(1)}, s32[1,256]{1,0:T(1,128)}, u32[]{:S(2)}) copy-start(s32[1,256]{1,0:T(1,128)} %docs_row.3) | copy-start | bytes 3076
  6.7 161.9 %copy-start.10 = (f32[128]{0:T(128)S(1)}, f32[128]{0:T(128)}, u32[]{:S(2)}) copy-start(f32[128]{0:T(128)} %param.26) | copy-start | bytes 1540
  6.7 161.9 %copy-start.11 = (f32[128]{0:T(128)S(1)}, f32[128]{0:T(128)}, u32[]{:S(2)}) copy-start(f32[128]{0:T(128)} %param.27) | copy-start | bytes 1540
  168.6 23.5 %copy-start.28 = (s32[256,8]{0,1:T(8,128)S(1)}, s32[256,8]{0,1:T(8,128)}, u32[]{:S(2)}) copy-start(s32[256,8]{0,1:T(8,128)} %param.18) | copy-start | bytes 24580
  192.2 4.5 collective-permute-start
  192.2 7.3 copy-start.27
  199.5 2.2 copy-start.12
  199.7 2.1 copy-start.14
  529.5 3.5 copy-start.13
  529.5 3.5 copy-start.16
  529.5 4.0 copy-start.18
  533.4 2.5 copy-start.5
  535.9 22.7 %copy-start.2 = (bf16[256,2048]{1,0:T(8,128)(2,1)}, bf16[256,2048]{1,0:T(8,128)(2,1)S(1)}, u32[]{:S(2)}) copy-start(bf16[256,2048]{1,0:T(8,128)(2,1)S(1)} %get-tuple-element.126.grad_attn_ref.refs_3_) | copy-start | bytes 3145732
  535.9 23.1 %copy-start.15 = (bf16[256,2048]{1,0:T(8,128)(2,1)S(1)}, bf16[256,2048]{1,0:T(8,128)(2,1)}, u32[]{:S(2)}) copy-start(bf16[256,2048]{1,0:T(8,128)(2,1)} %copy-done.14) | copy-start | bytes 3145732
  558.5 3.8 copy-start.3
  558.6 8.0 %collective-permute-start.1 = (f32[256,2048]{1,0:T(8,128)S(1)}, f32[256,2048]{1,0:T(8,128)S(1)}, u32[]{:S(2)}, u32[]{:S(2)}) collective-permute-start(f32[256,2048]{1,0:T(8,128)S(1)} %get-tuple-element.54), channel_id=1, source_target_pairs={{0,1},{1,0},{2,3},{3,2},{4,5},{5,4},{6,7},{7,6},{8,9},{9,8},{10,11... | collective-permute-start | bytes 6291464 | tf_op jit(solution)/shard_map/ppermute | solution.py:1232
  564.5 2.0 copy-start.1
  735.8 6.5 copy-start.23
  740.0 3.4 copy-start.26
  740.0 4.0 copy-start.25
  740.0 4.7 copy-start.22
  (7 other events, 9.9 us)

commit v9 on v8

--- a/solution.py
+++ b/solution.py
@@ -98,12 +98,18 @@
         pl.when(condition)(action)
 
 
-def gather_kernel(count, with_pair, *refs):
-    paired = sum(with_pair)
-    ins, outs, pairs = refs[:count], refs[count : 2 * count], list(refs[2 * count : 2 * count + paired])
-    pairs = [pairs.pop(0) if wanted else None for wanted in with_pair]
-    sems = refs[2 * count + paired :]
-    steps = gather_steps(ins, outs, pairs, sems)
+def gather_kernel(count, *refs):
+    pieces, out, own, piece_sem = refs[:count], refs[count], refs[count + 1], refs[count + 2]
+    copies, lane = [], 0
+    for i, piece in enumerate(pieces):
+        place = own.at[:, pl.ds(lane, piece.shape[1])]
+        copies.append(pltpu.make_async_copy(piece, place, piece_sem.at[i]))
+        lane += piece.shape[1]
+    for copy in copies:
+        copy.start()
+    for copy in copies:
+        copy.wait()
+    steps = gather_steps([own], [out], [None], refs[count + 3 :])
     for step in steps.order:
         step()
     steps.end()
@@ -306,18 +312,21 @@
     return [dma(slots), dma(slots), dma((count,)), dma(pair_slots), dma(pair_slots)]
 
 
-def gather_blocks(arrays, with_pair, collective_id):
-    count, blocks, paired = len(arrays), lax.axis_size("gx"), sum(with_pair)
-    shapes = [jax.ShapeDtypeStruct((blocks, *a.shape), a.dtype) for a in arrays]
-    shapes += [shape for shape, wanted in zip(shapes, with_pair) if wanted]
+def gather_blocks(pieces, collective_id):
+    rows, width = pieces[0].shape[0], sum(piece.shape[1] for piece in pieces)
+    low = pieces[0].dtype
     return pl.pallas_call(
-        functools.partial(gather_kernel, count, with_pair),
-        out_shape=shapes,
-        in_specs=[pl.BlockSpec(memory_space=pl.ANY)] * count,
-        out_specs=[pl.BlockSpec(memory_space=pl.ANY)] * len(shapes),
-        scratch_shapes=gather_semaphores(count, paired),
+        functools.partial(gather_kernel, len(pieces)),
+        out_shape=jax.ShapeDtypeStruct((lax.axis_size("gx"), rows, width), low),
+        in_specs=[pl.BlockSpec(memory_space=pl.ANY)] * len(pieces),
+        out_specs=pl.BlockSpec(memory_space=pl.ANY),
+        scratch_shapes=[
+            pltpu.VMEM((rows, width), low),
+            pltpu.SemaphoreType.DMA((len(pieces),)),
+            *gather_semaphores(1, 0),
+        ],
         compiler_params=pltpu.CompilerParams(collective_id=collective_id, has_side_effects=True),
-    )(*arrays)
+    )(*pieces)
 
 
 def dot_nn(left, right):
@@ -1506,13 +1515,13 @@
     part_width = model_width // devices_gy
     experts_all = router_weight.shape[1]
     router_lanes = jnp.pad(router_weight, ((0, 0), (0, LANES - experts_all)))
-    rows_local = jnp.concatenate([q_weight, key_matrix, value_matrix, router_lanes, out_weight], axis=1)
+    pieces = [q_weight, key_matrix, value_matrix, router_lanes, out_weight]
     dense = kernels_fit() and experts_all <= 2 * TOP
     if dense:
-        (weights_all,) = gather_blocks([rows_local], (0,), 1)
-        weights_all = weights_all.reshape(-1, rows_local.shape[1])
+        weights_all = gather_blocks(pieces, 1)
+        weights_all = weights_all.reshape(-1, weights_all.shape[2])
     else:
-        weights_all = lax.all_gather(rows_local, "gx", axis=0, tiled=True)
+        weights_all = lax.all_gather(jnp.concatenate(pieces, axis=1), "gx", axis=0, tiled=True)
     q_width, kv_width = q_weight.shape[1], key_matrix.shape[1]
     qkv_width = q_width + 2 * kv_width
     router_full = weights_all[:, qkv_width : qkv_width + experts_all]

time: 751 us -> 743 us (0.989)
    unnamed x69 -> x61, local copies, waits for them, and re-layouts: 15.8 us -> 11.9 us
where the time goes in v9:
time: 743 us; the launch traced here: 737 us
  Pallas kernels  692 us (93%)
  local copies, waits for them, and re-layouts  17.2 us (2%)
  other arithmetic  15.4 us (2%)
    pallas_call x1, Pallas kernels, scatter_sums(): pl.pallas_call(scatter_kernel, out_shape=[*[jax.ShapeDtypeStruct((rows, w...  167 us
    pallas_call x1, Pallas kernels, experts_products(): pl.pallas_call(functools.partial(experts_kernel, experts_all), out_shape=...  166 us
    pallas_call x1, Pallas kernels, return_sums(): pl.pallas_call(return_kernel, out_shape=[jax.ShapeDtypeStruct((2 * rows,...  159 us
    pallas_call x1, Pallas kernels, gather_blocks(): pl.pallas_call(functools.partial(gather_kernel, len(pieces)), out_shape=j...  156 us
    pallas_call x1, Pallas kernels, attend_back(): pl.pallas_call(functools.partial(attend_back_kernel, q_heads, kv_heads),...  22.6 us
    pallas_call x1, Pallas kernels, attend(): pl.pallas_call(functools.partial(attend_kernel, q_heads, kv_heads), out_s...  20.6 us
  transfers between devices with their start and end apart: 2, of which 1 were waited for; matrix products, arithmetic and copies ran while one was open for 1% of the time, Pallas kernels for 0%

profile of v9, /device:TPU:0, one launch (start us, length us, event | category | flops | bytes accessed | tf_op | source)
XLA Modules:
  0.0 737.5 jit_solution(7070994572624418030)
XLA Ops:
  3.6 156.2 %shard_map.263 = bf16[16,128,4736]{2,1,0:T(8,128)(2,1)} custom-call(bf16[128,2048]{1,0:T(8,128)(2,1)} %refs_0_.1, bf16[128,256]{1,0:T(8,128)(2,1)} %refs_1_.2, bf16[128,256]{1,0:T(8,128)(2,1)} %refs_2_.1, bf16[128,128]{1,0:T(8,128)(2,1)} %pad.16.refs_3_, bf16[128,2048]{1,0:T(8,128)(2,1)} %refs_4_.1), custom_call_target="tpu_custom_call" | custom-call | tf_op jit(solution)/shard_map/pallas_call | solution.py:318
  159.9 20.6 %shard_map.264 = (bf16[256,2048]{1,0:T(8,128)(2,1)S(1)}, f32[256,2560]{1,0:T(8,128)}, bf16[256,2048]{1,0:T(8,128)(2,1)S(1)}, bf16[256,2048]{1,0:T(8,128)(2,1)S(1...) custom-call(bf16[256,2048]{1,0:T(8,128)(2,1)S(1)} %copy-done, ...), custom_call_target="tpu_custom_call" | custom-call | tf_op jit(solution)/shard_map/pallas_call | solution.py:1455
  181.5 1.0 copy-done.6
  182.4 1.0 copy-done.7
  183.4 4.5 collective-permute-done
  187.9 2.8 multiply_reduce_fusion.2
  191.0 1.9 fusion.18
  194.0 166.4 %shard_map.265 = (bf16[2,16,128,384]{3,2,1,0:T(8,128)(2,1)}, bf16[2,16,128,768]{3,2,1,0:T(8,128)(2,1)}, bf16[2,16,128,128]{3,2,1,0:T(8,128)(2,1)}, bf16[2048,384...) custom-call(bf16[128,2176]{1,0:T(8,128)(2,1)} %pad_maximum_fusion.re, ...), custom_call_target="tpu_custom_call" | custom-call | tf_op jit(solution)/shard_map/pallas_call | solution.py:562
  360.4 159.4 %shard_map.266 = (f32[256,2176]{1,0:T(8,128)}, f32[256,2048]{1,0:T(8,128)}) custom-call(bf16[2,16,128,768]{3,2,1,0:T(8,128)(2,1)} %get-tuple-element.41.grad_in, bf16[2,16,128,384]{3,2,1,0:T(8,128)(2,1)} %get-tuple-element.42.weighted, bf16[2,16,128,128]{3,2,1,0:T(8,128)(2,1)} %get-tuple-element.43.terms, bf16[2048,384]{1,0:T(8,128)(2,1)} %bitcast.47, ...), custom_call_target="tpu_custom_call" | custom-call | tf_op jit(solution)/shard_map/pallas_call | solution.py:1107
  520.9 3.4 multiply_reduce_fusion
  524.8 2.4 fusion.17
  527.3 22.6 %shard_map.267 = (bf16[256,2560]{1,0:T(8,128)(2,1)S(1)}, f32[8,128]{1,0:T(8,128)S(1)}, f32[256,2048]{1,0:T(8,128)S(1)}) custom-call(bf16[256,2048]{1,0:T(8,128)(2,1)S(1)} %get-tuple-element.126.grad_attn_ref.refs_3_, bf16[2048,4736]{1,0:T(8,128)(2,1)} %bitcast.45, f32[256,128]{1,0:T(8,128)S(1)} %get-tuple-element.144.cosine_ref, ...), custom_call_target="tpu_custom_call" | custom-call | tf_op jit(solution)/shard_map/pallas_call | solution.py:1476
  550.4 1.3 convolution_convert_fusion
  551.8 1.9 bitcast_convert_fusion.2
  553.8 1.9 bitcast_convert_fusion.1
  555.9 2.0 bitcast_convert_fusion
  557.9 1.9 fusion.2
  560.5 166.8 %shard_map.268 = (f32[128,2048]{1,0:T(8,128)}, f32[128,256]{1,0:T(8,128)}, f32[128,256]{1,0:T(8,128)}, f32[128,128]{1,0:T(8,128)}, f32[128,2048]{1,0:T(8,128)}, ...) custom-call(bf16[256,2048]{1,0:T(8,128)(2,1)} %copy-done.6, bf16[256,2560]{1,0:T(8,128)(2,1)} %copy-done.3, ...), custom_call_target="tpu_custom_call" | custom-call | tf_op jit(solution)/shard_map/pallas_call | solution.py:930
  727.2 1.3 slice_bitcast_fusion.2
  728.5 1.3 slice_bitcast_fusion
  729.9 1.5 copy.53
  731.4 2.4 copy.59
  733.8 1.0 copy.60
  736.1 1.0 copy.63
  (83 shorter events, 9.7 us)
Async XLA Ops:
  3.6 156.3 %copy-start = (bf16[256,2048]{1,0:T(8,128)(2,1)S(1)}, bf16[256,2048]{1,0:T(8,128)(2,1)}, u32[]{:S(2)}) copy-start(bf16[256,2048]{1,0:T(8,128)(2,1)} %refs_6_.1) | copy-start | bytes 3145732
  3.6 156.3 %copy-start.8 = (f32[2048]{0:T(1024)S(1)}, f32[2048]{0:T(1024)}, u32[]{:S(2)}) copy-start(f32[2048]{0:T(1024)} %param.24) | copy-start | bytes 24580
  3.6 156.3 %copy-start.9 = (s32[1,256]{1,0:T(1,128)S(1)}, s32[1,256]{1,0:T(1,128)}, u32[]{:S(2)}) copy-start(s32[1,256]{1,0:T(1,128)} %docs_row.3) | copy-start | bytes 3076
  3.6 156.3 %copy-start.10 = (f32[128]{0:T(128)S(1)}, f32[128]{0:T(128)}, u32[]{:S(2)}) copy-start(f32[128]{0:T(128)} %param.26) | copy-start | bytes 1540
  3.6 156.3 %copy-start.11 = (f32[128]{0:T(128)S(1)}, f32[128]{0:T(128)}, u32[]{:S(2)}) copy-start(f32[128]{0:T(128)} %param.27) | copy-start | bytes 1540
  159.9 23.5 %copy-start.26 = (s32[256,8]{0,1:T(8,128)S(1)}, s32[256,8]{0,1:T(8,128)}, u32[]{:S(2)}) copy-start(s32[256,8]{0,1:T(8,128)} %param.18) | copy-start | bytes 24580
  183.4 4.5 collective-permute-start
  183.4 7.3 copy-start.25
  190.7 2.2 copy-start.12
  191.0 2.1 copy-start.14
  520.8 3.5 copy-start.13
  520.8 3.5 copy-start.16
  520.9 4.0 copy-start.17
  524.8 2.4 copy-start.5
  527.3 22.6 %copy-start.2 = (bf16[256,2048]{1,0:T(8,128)(2,1)}, bf16[256,2048]{1,0:T(8,128)(2,1)S(1)}, u32[]{:S(2)}) copy-start(bf16[256,2048]{1,0:T(8,128)(2,1)S(1)} %get-tuple-element.126.grad_attn_ref.refs_3_) | copy-start | bytes 3145732
  527.3 23.1 %copy-start.15 = (bf16[256,2048]{1,0:T(8,128)(2,1)S(1)}, bf16[256,2048]{1,0:T(8,128)(2,1)}, u32[]{:S(2)}) copy-start(bf16[256,2048]{1,0:T(8,128)(2,1)} %copy-done.14) | copy-start | bytes 3145732
  549.9 3.8 copy-start.3
  549.9 8.0 %collective-permute-start.1 = (f32[256,2048]{1,0:T(8,128)S(1)}, f32[256,2048]{1,0:T(8,128)S(1)}, u32[]{:S(2)}, u32[]{:S(2)}) collective-permute-start(f32[256,2048]{1,0:T(8,128)S(1)} %get-tuple-element.54), channel_id=1, source_target_pairs={{0,1},{1,0},{2,3},{3,2},{4,5},{5,4},{6,7},{7,6},{8,9},{9,8},{10,11... | collective-permute-start | bytes 6291464 | tf_op jit(solution)/shard_map/ppermute | solution.py:1241
  551.8 2.0 copy-start.19
  555.8 2.0 copy-start.1
  727.2 6.5 copy-start.22
  731.4 3.4 copy-start.24
  731.4 4.0 copy-start.23
  731.4 4.7 copy-start.21
  (5 other events, 6.8 us)

commit v10 on v9

--- a/solution.py
+++ b/solution.py
@@ -1364,7 +1364,7 @@
             attended_ref[:, head_span(head)] = dot_nn(value_columns, probs).T.astype(jnp.bfloat16)
             return carry
 
-        lax.fori_loop(0, group, body, 0, unroll=2)
+        lax.fori_loop(0, group, body, 0, unroll=4)
     for copy in out:
         copy.wait()
     dot_groups(part_ref, attended_ref, w_out, 0, w_out.shape[0], True)
@@ -1415,7 +1415,7 @@
             back_to_raw(grad_queries, head, q_gain[...], 0)
             return carry
 
-        lax.fori_loop(0, group, body, 0, unroll=2)
+        lax.fori_loop(0, group, body, 0, unroll=4)
         back_to_raw(sums_ref[1] * inv_root, q_heads + kv, k_gain[...], 1)
         grad_raw_ref[:, head_span(q_heads + kv_heads + kv)] = sums_ref[0].astype(jnp.bfloat16)
     for _, copy in into:

time: 743 us -> 740 us (level)
  no operation moved by 1% of the time
where the time goes in v10:
time: 740 us; the launch traced here: 734 us
  Pallas kernels  688 us (93%)
  local copies, waits for them, and re-layouts  17.2 us (2%)
  other arithmetic  15.4 us (2%)
    pallas_call x1, Pallas kernels, scatter_sums(): pl.pallas_call(scatter_kernel, out_shape=[*[jax.ShapeDtypeStruct((rows, w...  167 us
    pallas_call x1, Pallas kernels, experts_products(): pl.pallas_call(functools.partial(experts_kernel, experts_all), out_shape=...  166 us
    pallas_call x1, Pallas kernels, return_sums(): pl.pallas_call(return_kernel, out_shape=[jax.ShapeDtypeStruct((2 * rows,...  159 us
    pallas_call x1, Pallas kernels, gather_blocks(): pl.pallas_call(functools.partial(gather_kernel, len(pieces)), out_shape=j...  156 us
    pallas_call x1, Pallas kernels, attend_back(): pl.pallas_call(functools.partial(attend_back_kernel, q_heads, kv_heads),...  20.6 us
    pallas_call x1, Pallas kernels, attend(): pl.pallas_call(functools.partial(attend_kernel, q_heads, kv_heads), out_s...  19.1 us
  transfers between devices with their start and end apart: 2, of which 1 were waited for; matrix products, arithmetic and copies ran while one was open for 1% of the time, Pallas kernels for 0%

profile of v10, /device:TPU:0, one launch (start us, length us, event | category | flops | bytes accessed | tf_op | source)
XLA Modules:
  0.0 734.0 jit_solution(16963143394813333243)
XLA Ops:
  3.6 156.2 %shard_map.263 = bf16[16,128,4736]{2,1,0:T(8,128)(2,1)} custom-call(bf16[128,2048]{1,0:T(8,128)(2,1)} %refs_0_.1, bf16[128,256]{1,0:T(8,128)(2,1)} %refs_1_.2, bf16[128,256]{1,0:T(8,128)(2,1)} %refs_2_.1, bf16[128,128]{1,0:T(8,128)(2,1)} %pad.16.refs_3_, bf16[128,2048]{1,0:T(8,128)(2,1)} %refs_4_.1), custom_call_target="tpu_custom_call" | custom-call | tf_op jit(solution)/shard_map/pallas_call | solution.py:318
  159.9 19.1 %shard_map.264 = (bf16[256,2048]{1,0:T(8,128)(2,1)S(1)}, f32[256,2560]{1,0:T(8,128)}, bf16[256,2048]{1,0:T(8,128)(2,1)S(1)}, bf16[256,2048]{1,0:T(8,128)(2,1)S(1...) custom-call(bf16[256,2048]{1,0:T(8,128)(2,1)S(1)} %copy-done, ...), custom_call_target="tpu_custom_call" | custom-call | tf_op jit(solution)/shard_map/pallas_call | solution.py:1455
  180.0 1.0 copy-done.6
  181.0 1.0 copy-done.7
  182.0 4.5 collective-permute-done
  186.4 2.8 multiply_reduce_fusion.2
  189.5 1.9 fusion.18
  192.5 166.4 %shard_map.265 = (bf16[2,16,128,384]{3,2,1,0:T(8,128)(2,1)}, bf16[2,16,128,768]{3,2,1,0:T(8,128)(2,1)}, bf16[2,16,128,128]{3,2,1,0:T(8,128)(2,1)}, bf16[2048,384...) custom-call(bf16[128,2176]{1,0:T(8,128)(2,1)} %pad_maximum_fusion.re, ...), custom_call_target="tpu_custom_call" | custom-call | tf_op jit(solution)/shard_map/pallas_call | solution.py:562
  358.9 159.4 %shard_map.266 = (f32[256,2176]{1,0:T(8,128)}, f32[256,2048]{1,0:T(8,128)}) custom-call(bf16[2,16,128,768]{3,2,1,0:T(8,128)(2,1)} %get-tuple-element.41.grad_in, bf16[2,16,128,384]{3,2,1,0:T(8,128)(2,1)} %get-tuple-element.42.weighted, bf16[2,16,128,128]{3,2,1,0:T(8,128)(2,1)} %get-tuple-element.43.terms, bf16[2048,384]{1,0:T(8,128)(2,1)} %bitcast.47, ...), custom_call_target="tpu_custom_call" | custom-call | tf_op jit(solution)/shard_map/pallas_call | solution.py:1107
  519.4 3.4 multiply_reduce_fusion
  523.3 2.4 fusion.17
  525.8 20.6 %shard_map.267 = (bf16[256,2560]{1,0:T(8,128)(2,1)S(1)}, f32[8,128]{1,0:T(8,128)S(1)}, f32[256,2048]{1,0:T(8,128)S(1)}) custom-call(bf16[256,2048]{1,0:T(8,128)(2,1)S(1)} %get-tuple-element.126.grad_attn_ref.refs_3_, bf16[2048,4736]{1,0:T(8,128)(2,1)} %bitcast.45, f32[256,128]{1,0:T(8,128)S(1)} %get-tuple-element.144.cosine_ref, ...), custom_call_target="tpu_custom_call" | custom-call | tf_op jit(solution)/shard_map/pallas_call | solution.py:1476
  546.9 1.3 convolution_convert_fusion
  548.3 1.9 bitcast_convert_fusion.2
  550.3 1.9 bitcast_convert_fusion.1
  552.3 2.0 bitcast_convert_fusion
  554.4 1.9 fusion.2
  556.9 166.8 %shard_map.268 = (f32[128,2048]{1,0:T(8,128)}, f32[128,256]{1,0:T(8,128)}, f32[128,256]{1,0:T(8,128)}, f32[128,128]{1,0:T(8,128)}, f32[128,2048]{1,0:T(8,128)}, ...) custom-call(bf16[256,2048]{1,0:T(8,128)(2,1)} %copy-done.6, bf16[256,2560]{1,0:T(8,128)(2,1)} %copy-done.3, ...), custom_call_target="tpu_custom_call" | custom-call | tf_op jit(solution)/shard_map/pallas_call | solution.py:930
  723.7 1.3 slice_bitcast_fusion.2
  725.0 1.3 slice_bitcast_fusion
  726.3 1.5 copy.53
  727.8 2.4 copy.59
  730.3 1.0 copy.60
  732.5 1.0 copy.63
  (83 shorter events, 9.7 us)
Async XLA Ops:
  3.6 156.3 %copy-start = (bf16[256,2048]{1,0:T(8,128)(2,1)S(1)}, bf16[256,2048]{1,0:T(8,128)(2,1)}, u32[]{:S(2)}) copy-start(bf16[256,2048]{1,0:T(8,128)(2,1)} %refs_6_.1) | copy-start | bytes 3145732
  3.6 156.3 %copy-start.8 = (f32[2048]{0:T(1024)S(1)}, f32[2048]{0:T(1024)}, u32[]{:S(2)}) copy-start(f32[2048]{0:T(1024)} %param.24) | copy-start | bytes 24580
  3.6 156.3 %copy-start.9 = (s32[1,256]{1,0:T(1,128)S(1)}, s32[1,256]{1,0:T(1,128)}, u32[]{:S(2)}) copy-start(s32[1,256]{1,0:T(1,128)} %docs_row.3) | copy-start | bytes 3076
  3.6 156.3 %copy-start.10 = (f32[128]{0:T(128)S(1)}, f32[128]{0:T(128)}, u32[]{:S(2)}) copy-start(f32[128]{0:T(128)} %param.26) | copy-start | bytes 1540
  3.6 156.3 %copy-start.11 = (f32[128]{0:T(128)S(1)}, f32[128]{0:T(128)}, u32[]{:S(2)}) copy-start(f32[128]{0:T(128)} %param.27) | copy-start | bytes 1540
  159.9 22.1 %copy-start.26 = (s32[256,8]{0,1:T(8,128)S(1)}, s32[256,8]{0,1:T(8,128)}, u32[]{:S(2)}) copy-start(s32[256,8]{0,1:T(8,128)} %param.18) | copy-start | bytes 24580
  181.9 4.5 collective-permute-start
  182.0 7.3 copy-start.25
  189.2 2.2 copy-start.12
  189.5 2.1 copy-start.14
  519.4 3.5 copy-start.13
  519.4 3.5 copy-start.16
  519.4 4.0 copy-start.17
  523.3 2.4 copy-start.5
  525.8 20.6 %copy-start.2 = (bf16[256,2048]{1,0:T(8,128)(2,1)}, bf16[256,2048]{1,0:T(8,128)(2,1)S(1)}, u32[]{:S(2)}) copy-start(bf16[256,2048]{1,0:T(8,128)(2,1)S(1)} %get-tuple-element.126.grad_attn_ref.refs_3_) | copy-start | bytes 3145732
  525.8 21.1 %copy-start.15 = (bf16[256,2048]{1,0:T(8,128)(2,1)S(1)}, bf16[256,2048]{1,0:T(8,128)(2,1)}, u32[]{:S(2)}) copy-start(bf16[256,2048]{1,0:T(8,128)(2,1)} %copy-done.14) | copy-start | bytes 3145732
  546.4 3.8 copy-start.3
  546.4 8.0 %collective-permute-start.1 = (f32[256,2048]{1,0:T(8,128)S(1)}, f32[256,2048]{1,0:T(8,128)S(1)}, u32[]{:S(2)}, u32[]{:S(2)}) collective-permute-start(f32[256,2048]{1,0:T(8,128)S(1)} %get-tuple-element.54), channel_id=1, source_target_pairs={{0,1},{1,0},{2,3},{3,2},{4,5},{5,4},{6,7},{7,6},{8,9},{9,8},{10,11... | collective-permute-start | bytes 6291464 | tf_op jit(solution)/shard_map/ppermute | solution.py:1241
  548.3 2.0 copy-start.19
  552.3 2.0 copy-start.1
  723.7 6.5 copy-start.22
  727.8 3.4 copy-start.24
  727.8 4.0 copy-start.23
  727.8 4.7 copy-start.21
  (5 other events, 6.8 us)
